TPU v7x, 32 devices: a whole 2x2x4 slice. The times are simulated.
32 devices in a mesh: dp: 8 (over z, x), mp: 4 (over y, core).
Axes of the slice: x: 2, y: 2, z: 4, core: 2. Of those that a mesh axis runs over, the one named last changes fastest.
Arguments:
- x_in: bfloat16 [1024, 1024], P('dp', 'mp'), may hold values from -90 to 90
- gain: float32 [1024], replicated, may hold values from 0.25 to 1.75
- w_in: bfloat16 [1024, 4096], P('mp'), may hold values from -0.5 to 0.5
- w_out: bfloat16 [1024, 4096], P('mp'), may hold values from -0.1875 to 0.1875
- grad_out: bfloat16 [1024, 1024], P('dp', 'mp'), may hold values from -6 to 6
- block_cols: int32 [4, 256], P('mp'), may hold values from 0 to 127, as said below
- slots: int32 [4, 256], P('mp'), may hold values from 0 to 511, as said below
Outputs:
- branch: bfloat16 [1024, 1024], P('dp', 'mp')
- grad_normed: bfloat16 [1024, 1024], P('dp', 'mp')
- owned_grad: float32 [4, 512, 4096], P('mp', 'dp')
Inputs may be any that keep to these rules, and one draw needn't show every extreme that they name: Within one row of block_cols, the 16 entries k with the same k // 16 are distinct. The entries of one row of slots are distinct; slot s lies on index s // 64 of dp. In each row every index of dp holds at most 64 slots that are named, and some index holds exactly 64.
All inputs are finite; a program needn't handle non-finite values.
Results may differ from a plain program's by a relative error of at most 0.0062.
Values may be sent and summed in bfloat16 or wider, within the bound.
No kernel may reach another device: no remote copies, remote signals or barrier semaphores. Data moves between devices by JAX's collectives and lax.ppermute only.
A program may use at most 128 MiB of HBM per device.

v0:
```python
import functools
import math

import jax
import jax.numpy as jnp
from jax import lax
from jax.experimental import pallas as pl
from jax.experimental.pallas import tpu as pltpu
from jax.sharding import PartitionSpec as P

FF = 32768
BLK = 64
HALF = BLK // 2
GROUP = 4


norm_eps = 1e-06
tanh_coef = 0.7978845608028654

F32 = jnp.float32
BF16 = jnp.bfloat16
MIB = 1024 * 1024


def gelu_value(pre_act):
    cubic = pre_act * pre_act * pre_act
    slope_arg = jnp.tanh(tanh_coef * (pre_act + 0.044715 * cubic))
    return 0.5 * pre_act * (1.0 + slope_arg)


def gelu_slope(pre_act):
    cubic = pre_act * pre_act * pre_act
    slope_arg = jnp.tanh(tanh_coef * (pre_act + 0.044715 * cubic))
    inner = tanh_coef * (1.0 + 0.134145 * pre_act * pre_act)
    return 0.5 * (1.0 + slope_arg) + 0.5 * pre_act * (1.0 - slope_arg * slope_arg) * inner


def gelu_both(v):
    square = v * v
    th = jnp.tanh(v * (tanh_coef + (tanh_coef * 0.044715) * square))
    gate = 0.5 + 0.5 * th
    inner = 2.0 * tanh_coef + (2.0 * tanh_coef * 0.134145) * square
    return v * gate, gate + v * (gate - gate * gate) * inner


def dot(a, b, dims=((1,), (0,))):
    return lax.dot_general(a, b, (dims, ((), ())), preferred_element_type=F32)


def iota(shape, axis):
    return lax.broadcasted_iota(jnp.int32, shape, axis)


def even_first(width):
    row, col = iota((width, width), 0), iota((width, width), 1)
    inside = row & (BLK - 1)
    target = (row - inside) + (inside & 1) * HALF + (inside >> 1)
    return jnp.where(col == target, 1.0, 0.0).astype(BF16)


def plan_kernel(cap, col_blocks, cols_ref, slots_ref, out_ref):
    kept = cols_ref.shape[1]
    me = lax.axis_index("dp")
    cols, slots = cols_ref[...], slots_ref[...]
    owner = lax.div(slots, jnp.int32(cap))
    eq = cols == iota((col_blocks, kept), 0)
    own = jnp.where(owner == me, 1.0, 0.0)
    peer = jnp.where(owner == (me ^ 1), 1.0, 0.0)
    needed = jnp.max(jnp.where(eq, own + peer, 0.0), axis=1, keepdims=True)

    def listed(flags_r, flags_c):
        size = flags_r.shape[1]
        before = iota((size, size), 1) < iota((size, size), 0)
        place = jnp.sum(jnp.where(before, flags_r, 0.0), axis=1, keepdims=True)
        hit = (place == iota((size, kept), 1).astype(F32)) & (flags_c > 0)
        index = iota((size, 1), 0).astype(F32)
        row = jnp.sum(jnp.where(hit, index, 0.0), axis=0, keepdims=True)
        return row, jnp.sum(flags_r, axis=1, keepdims=True)

    def to_column(row):
        size = row.shape[1]
        eye = iota((size, size), 0) == iota((size, size), 1)
        return jnp.sum(jnp.where(eye, row, 0.0), axis=1, keepdims=True)

    def to_row(column):
        size = column.shape[0]
        eye = iota((size, size), 0) == iota((size, size), 1)
        return jnp.sum(jnp.where(eye, column, 0.0), axis=0, keepdims=True)

    peer_list, peer_count = listed(peer, to_column(peer))
    own_list, own_count = listed(own, to_column(own))
    need_list, need_count = listed(to_row(needed), needed)
    rows = [
        cols.astype(F32),
        (slots - owner * cap).astype(F32),
        peer_list,
        own_list,
        need_list,
        peer_count,
        own_count,
        need_count,
    ]
    for index, row in enumerate(rows):
        out_ref[index : index + 1, :] = jnp.broadcast_to(row, (1, kept)).astype(jnp.int32)


def prepare_kernel(win_ref, wout_ref, a_in, b_in, p_out, a_out, order):
    per_row, length = win_ref.shape
    lanes = 2 * BLK
    rows = per_row * HALF

    @pl.when(pl.program_id(0) == 0)
    def _():
        row, col = iota((rows, rows), 0), iota((rows, rows), 1)
        source = (row & (HALF - 1)) * per_row + lax.div(row, jnp.int32(HALF))
        order[...] = jnp.where(col == source, 1.0, 0.0).astype(BF16)

    row, col = iota((lanes, lanes), 0), iota((lanes, lanes), 1)
    swap = jnp.where(((col + BLK) & (lanes - 1)) == row, 1.0, 0.0).astype(BF16)
    perm = even_first(lanes)
    both = jnp.concatenate([perm, dot(perm, swap).astype(BF16)], axis=1)

    def by_block(ref):
        stacked = jnp.concatenate(
            [ref[:, j * lanes : (j + 1) * lanes] for j in range(length // lanes)], axis=0
        )
        return dot(order[...], stacked).astype(BF16)

    kept_in = dot(by_block(win_ref), both).astype(BF16)
    kept_out = by_block(wout_ref)
    p_out[0] = kept_out
    left = iota((HALF, lanes), 1) < BLK
    for pair in range(per_row // 2):
        first = kept_in[2 * pair * HALF : (2 * pair + 1) * HALF].astype(F32)
        second = kept_in[(2 * pair + 1) * HALF : (2 * pair + 2) * HALF].astype(F32)
        at = slice(pair * lanes, (pair + 1) * lanes)
        b_in[0, :HALF, at] = jnp.where(left, first[:, :lanes], second[:, lanes:]).astype(BF16)
        b_in[0, HALF:, at] = jnp.where(left, first[:, lanes:], second[:, :lanes]).astype(BF16)
    for quad in range(per_row // GROUP):
        rows_of = slice(quad * lanes, (quad + 1) * lanes)
        turned = kept_in[rows_of, :lanes].T
        a_in[0, quad * BLK : (quad + 1) * BLK, :lanes] = turned[:BLK]
        a_in[0, quad * BLK : (quad + 1) * BLK, lanes:] = turned[BLK:]
        turned = kept_out[rows_of].T
        a_out[0, :, rows_of] = turned[:BLK]
        a_out[0, :, rows + quad * lanes : rows + (quad + 1) * lanes] = turned[BLK:]


def load_tokens(pieces, tok, gain_ref, perm, n_s, nt_s, gt_s, base):
    mine = lax.axis_index("mp")
    width = pieces[0][0].shape[1]
    values, total = [], 0.0
    for ref, first in pieces:
        value = ref[first : first + tok, :].astype(F32)
        values.append(value)
        total = total + jnp.sum(value * value, axis=-1, keepdims=True)
    inv_rms = lax.rsqrt(total / (width * len(pieces)) + norm_eps)
    for q, (ref, first) in enumerate(pieces):
        at = pl.ds(pl.multiple_of((mine ^ q) * width, width), width)
        normed = (values[q] * inv_rms * gain_ref[:, at]).astype(BF16)
        n_s[base : base + tok, at] = normed
        nt_s[at, :] = dot(normed, perm).astype(BF16).T
        gt_s[at, :] = ref[first + tok : first + 2 * tok, :].T


def expand(plan, a_in, p_out, nt_s, gt_s, acc_v, acc_a):
    row_blocks = a_in.shape[0]
    tok = nt_s.shape[1]
    per_row = p_out.shape[1] // HALF
    acc_v[...] = jnp.zeros_like(acc_v)
    acc_a[...] = jnp.zeros_like(acc_a)
    gap = jnp.zeros((HALF, tok), BF16)
    gap2 = jnp.zeros((BLK, tok), BF16)

    def step(r, carry):
        at = pl.ds(pl.multiple_of(r * BLK, BLK), BLK)
        normed, cot = nt_s[at, :], gt_s[at, :]
        spread = []
        for a in (0, 1):
            part = normed[a * HALF : (a + 1) * HALF]
            for u in range(GROUP):
                spread.append(
                    jnp.concatenate([part if v == u else gap for v in range(GROUP)], axis=1)
                )
        terms_v = dot(a_in[r], jnp.concatenate(spread, axis=0))
        cots = jnp.concatenate(
            [jnp.concatenate([cot, gap2], axis=1), jnp.concatenate([gap2, cot], axis=1)], axis=0
        )
        terms_a = dot(p_out[r], cots)
        for quad in range(per_row // GROUP):
            new = []
            for u in range(GROUP):
                k = quad * GROUP + u
                c = plan[0, r * per_row + k]
                v = acc_v[c] + terms_v[quad * BLK : (quad + 1) * BLK, u * tok : (u + 1) * tok]
                rows = terms_a[k * HALF : (k + 1) * HALF]
                a = acc_a[c] + jnp.concatenate([rows[:, :tok], rows[:, tok:]], axis=0)
                new.append((c, v, a))
            for c, v, a in new:
                acc_v[c] = v
                acc_a[c] = a
        return carry

    lax.fori_loop(0, row_blocks, step, 0)


def local_kernel(
    plan, gain_ref, s0, s1, s2, s3, a_in, b_in, p_out, a_out, o0, o1, o2, o3, gp_ref, n_ref,
    nt_s, gt_s, acc_v, acc_a, act_s, br_s, gn_s
):
    width = s0.shape[1]
    tok = s0.shape[0] // 2
    row_blocks, per_row = a_in.shape[0], p_out.shape[1] // HALF
    col_blocks = acc_v.shape[0]
    perm = even_first(width)
    load_tokens([(ref, 0) for ref in (s0, s1, s2, s3)], tok, gain_ref, perm, n_ref, nt_s, gt_s, 0)
    expand(plan, a_in, p_out, nt_s, gt_s, acc_v, acc_a)

    def bend(c, carry):
        value, slope = gelu_both(acc_v[c])
        act_s[c] = value.astype(BF16)
        gp_ref[c] = (acc_a[c] * slope).astype(BF16)
        return carry

    lax.fori_loop(0, col_blocks, bend, 0, unroll=2)

    def contract(r, carry):
        at = pl.ds(pl.multiple_of(r * BLK, BLK), BLK)
        ids = [plan[0, r * per_row + k] for k in range(per_row)]
        acts = [act_s[c, a * HALF : (a + 1) * HALF, :] for a in (0, 1) for c in ids]
        br_s[at, :] = dot(a_out[r], jnp.concatenate(acts, axis=0)).astype(BF16)
        grads = [gp_ref[c] for c in ids]
        gn_s[at, :] = dot(b_in[r], jnp.concatenate(grads, axis=0)).astype(BF16)
        return carry

    lax.fori_loop(0, row_blocks, contract, 0)
    mine = lax.axis_index("mp")
    for q, out in enumerate((o0, o1, o2, o3)):
        at = pl.ds(pl.multiple_of((mine ^ q) * width, width), width)
        out[:tok, :] = br_s[at, :].T
        out[tok:, :] = dot(gn_s[at, :].T, perm, ((1,), (1,))).astype(BF16)


def block_kernel(
    scale, plan, gain_ref, z0, z1, z2, z3, a_in, p_out, gp_own, n_own, peer_ref, own_ref,
    n_s, nt_s, gt_s, acc_v, acc_a, gp_s
):
    tok = n_own.shape[0]
    per_row = p_out.shape[1] // HALF
    lanes = 2 * BLK
    perm = even_first(z0.shape[1])
    n_s[:tok, :] = n_own[...]

    def keep(i, carry):
        c = plan[4, i]
        gp_s[c, :, :tok] = gp_own[c]
        return carry

    lax.fori_loop(0, plan[7, 0], keep, 0)
    for j in range(z0.shape[0] // (2 * tok)):
        pieces = [(ref, 2 * tok * j) for ref in (z0, z1, z2, z3)]
        load_tokens(pieces, tok, gain_ref, perm, n_s, nt_s, gt_s, (j + 1) * tok)
        expand(plan, a_in, p_out, nt_s, gt_s, acc_v, acc_a)

        def bend(i, carry):
            c = plan[4, i]
            _, slope = gelu_both(acc_v[c])
            gp_s[c, :, (j + 1) * tok : (j + 2) * tok] = (acc_a[c] * slope).astype(BF16)
            return carry

        lax.fori_loop(0, plan[7, 0], bend, 0)

    left = iota((HALF, lanes), 1) < BLK
    for out_ref, list_row, count_row in ((peer_ref, 2, 5), (own_ref, 3, 6)):
        out_ref[...] = jnp.zeros_like(out_ref)
        count = plan[count_row, 0]

        def outer(i, carry):
            done = []
            for u in range(GROUP):
                k = plan[list_row, jnp.minimum(i * GROUP + u, count - 1)]
                r = lax.div(k, jnp.int32(per_row))
                at_lane = pl.ds(pl.multiple_of((r >> 1) * lanes, lanes), lanes)
                block = dot(gp_s[plan[0, k]], n_s[:, at_lane]) * scale
                odd = (r & 1) == 1
                top, low = block[:HALF], block[HALF:]
                top = jnp.where(odd, pltpu.roll(top, BLK, 1), top)
                low = jnp.where(odd, low, pltpu.roll(low, BLK, 1))
                done.append((plan[1, k], jnp.where(left, top, low).astype(out_ref.dtype)))
            for slot, value in done:
                out_ref[slot] = value
            return carry

        lax.fori_loop(0, (count + GROUP - 1) // GROUP, outer, 0)


def fast_body(x_in, gain, w_in, w_out, grad_out, block_cols, slots):
    dp_count, mp_count = lax.axis_size("dp"), lax.axis_size("mp")
    tok, width = x_in.shape
    feat = width * mp_count
    kept = w_in.shape[0]
    row_blocks = feat // BLK
    per_row = kept // row_blocks
    hidden = FF // mp_count
    col_blocks = hidden // BLK
    lanes = 2 * BLK
    cap = 2 * kept // dp_count
    scale = 1.0 / math.sqrt(tok * dp_count)
    across_x = [(i, i ^ 1) for i in range(dp_count)]
    near = [[(i, i ^ q) for i in range(mp_count)] for q in range(mp_count)]
    z_count = dp_count // 2
    along_z = [
        [(((z + j) % z_count) * 2 + x, z * 2 + x) for z in range(z_count) for x in range(2)]
        for j in range(z_count)
    ]

    own = jnp.concatenate([x_in, grad_out], axis=0)
    gathered = [own] + [lax.ppermute(own, "mp", near[q]) for q in range(1, mp_count)]
    column = jnp.concatenate(
        [lax.ppermute(own, "dp", along_z[j]) for j in range(1, z_count)], axis=0
    )
    column_y = lax.ppermute(column, "mp", near[2])
    columns = [
        column,
        lax.ppermute(column, "mp", near[1]),
        column_y,
        lax.ppermute(column_y, "mp", near[1]),
    ]
    gain_row = gain.reshape(1, feat)
    whole = pl.BlockSpec(memory_space=pltpu.VMEM)
    mm = 2 * tok * kept * BLK * BLK

    plan = pl.pallas_call(
        functools.partial(plan_kernel, cap, col_blocks),
        out_shape=jax.ShapeDtypeStruct((8, kept), jnp.int32),
        cost_estimate=pl.CostEstimate(flops=4_000_000, bytes_accessed=16384, transcendentals=0),
        name="plan",
    )(block_cols, slots)

    shapes = [
        (per_row // GROUP * BLK, 2 * lanes),
        (BLK, per_row * BLK),
        (per_row * HALF, lanes),
        (BLK, per_row * BLK),
    ]
    a_in, b_in, p_out, a_out = pl.pallas_call(
        prepare_kernel,
        out_shape=[jax.ShapeDtypeStruct((row_blocks, *shape), BF16) for shape in shapes],
        grid=(row_blocks,),
        in_specs=[pl.BlockSpec((per_row, BLK * BLK), lambda r: (r, 0))] * 2,
        out_specs=[pl.BlockSpec((1, *shape), lambda r: (r, 0, 0)) for shape in shapes],
        scratch_shapes=[pltpu.VMEM((per_row * HALF, per_row * HALF), BF16)],
        compiler_params=pltpu.CompilerParams(vmem_limit_bytes=24 * MIB),
        cost_estimate=pl.CostEstimate(
            flops=8 * mm, bytes_accessed=12 * kept * BLK * BLK, transcendentals=0
        ),
        name="prepare",
    )(w_in, w_out)

    hidden_f32 = pltpu.VMEM((col_blocks, BLK, tok), F32)
    turned = pltpu.VMEM((feat, tok), BF16)
    *parts, gp_own, n_own = pl.pallas_call(
        local_kernel,
        out_shape=[jax.ShapeDtypeStruct((2 * tok, width), BF16)] * mp_count
        + [
            jax.ShapeDtypeStruct((col_blocks, BLK, tok), BF16),
            jax.ShapeDtypeStruct((tok, feat), BF16),
        ],
        grid_spec=pltpu.PrefetchScalarGridSpec(
            num_scalar_prefetch=1,
            grid=(),
            in_specs=[whole] * 9,
            out_specs=[whole] * (mp_count + 2),
            scratch_shapes=[
                turned,
                turned,
                hidden_f32,
                hidden_f32,
                pltpu.VMEM((col_blocks, BLK, tok), BF16),
                turned,
                turned,
            ],
        ),
        compiler_params=pltpu.CompilerParams(vmem_limit_bytes=32 * MIB),
        cost_estimate=pl.CostEstimate(
            flops=16 * mm,
            bytes_accessed=10 * kept * BLK * BLK,
            transcendentals=tok * hidden,
        ),
        name="local",
    )(plan, gain_row, *gathered, a_in, b_in, p_out, a_out)

    rows = tok * z_count
    for_peer, for_own = pl.pallas_call(
        functools.partial(block_kernel, scale),
        out_shape=[
            jax.ShapeDtypeStruct((cap, HALF, lanes), BF16),
            jax.ShapeDtypeStruct((cap, HALF, lanes), F32),
        ],
        grid_spec=pltpu.PrefetchScalarGridSpec(
            num_scalar_prefetch=1,
            grid=(),
            in_specs=[whole] * 9,
            out_specs=[whole] * 2,
            scratch_shapes=[
                pltpu.VMEM((rows, feat), BF16),
                turned,
                turned,
                hidden_f32,
                hidden_f32,
                pltpu.VMEM((col_blocks, BLK, rows), BF16),
            ],
        ),
        compiler_params=pltpu.CompilerParams(vmem_limit_bytes=40 * MIB),
        cost_estimate=pl.CostEstimate(
            flops=24 * mm,
            bytes_accessed=6 * kept * BLK * BLK,
            transcendentals=tok * hidden,
        ),
        name="blocks",
    )(plan, gain_row, *columns, a_in, p_out, gp_own, n_own)

    arrived = lax.ppermute(for_peer, "dp", across_x)
    summed = [parts[0]] + [lax.ppermute(parts[q], "mp", near[q]) for q in range(1, mp_count)]
    total = sum(part.astype(F32) for part in summed)
    branch, grad_normed = total[:tok].astype(BF16), total[tok:].astype(BF16)
    owned_grad = (for_own + arrived.astype(F32)).reshape(cap, BLK * BLK)
    return (branch, grad_normed, owned_grad[None])


def sum_sources(received):
    return jnp.sum(received, axis=0)


def body(x_in, gain, w_in, w_out, grad_out, block_cols, slots):
    whole_x, whole_grad = (
        lax.all_gather(x_in, "mp", axis=1, tiled=True),
        lax.all_gather(grad_out, "mp", axis=1, tiled=True),
    )
    tok_rows = whole_x.shape[0]
    feat_width = whole_x.shape[1]
    row_blocks = feat_width // BLK
    kept_count = w_in.shape[0]
    per_row = kept_count // row_blocks
    col_blocks = FF // lax.axis_size("mp") // BLK
    col_ids = block_cols[0]
    slot_ids = slots[0]
    x_float = whole_x.astype(jnp.float32)
    inv_rms = lax.rsqrt(jnp.mean(x_float * x_float, axis=-1, keepdims=True) + norm_eps)
    normed = (x_float * inv_rms * gain).astype(jnp.bfloat16)
    normed_cols = normed.reshape(tok_rows, row_blocks, BLK).transpose(1, 2, 0)
    grad_cols = whole_grad.reshape(tok_rows, row_blocks, BLK).transpose(1, 2, 0)
    in_blocks = w_in.reshape(row_blocks, per_row, BLK, BLK)
    out_blocks = w_out.reshape(row_blocks, per_row, BLK, BLK)
    col_onehot = (col_ids[None, :] == jnp.arange(col_blocks, dtype=jnp.int32)[:, None]).astype(
        jnp.float32
    )
    pre_parts = jnp.einsum(
        "rkbc,rbt->rkct", in_blocks, normed_cols, preferred_element_type=jnp.float32
    )
    pre_act = jnp.dot(
        col_onehot,
        pre_parts.reshape(kept_count, BLK * tok_rows),
        precision=lax.Precision.HIGHEST,
        preferred_element_type=jnp.float32,
    )
    pre_act = pre_act.reshape(col_blocks, BLK, tok_rows)
    activation = gelu_value(pre_act).astype(jnp.bfloat16)
    act_blocks = jnp.take(activation, col_ids, axis=0).reshape(row_blocks, per_row, BLK, tok_rows)
    branch_cols = jnp.einsum(
        "rkcb,rkct->rbt", out_blocks, act_blocks, preferred_element_type=jnp.float32
    )
    branch_part = branch_cols.transpose(2, 0, 1).reshape(tok_rows, feat_width)
    branch = lax.psum_scatter(branch_part, "mp", scatter_dimension=1, tiled=True).astype(
        jnp.bfloat16
    )
    act_parts = jnp.einsum(
        "rkcb,rbt->rkct", out_blocks, grad_cols, preferred_element_type=jnp.float32
    )
    grad_act = jnp.dot(
        col_onehot,
        act_parts.reshape(kept_count, BLK * tok_rows),
        precision=lax.Precision.HIGHEST,
        preferred_element_type=jnp.float32,
    )
    grad_act = grad_act.reshape(col_blocks, BLK, tok_rows)
    grad_pre = (grad_act * gelu_slope(pre_act)).astype(jnp.bfloat16)
    pre_blocks = jnp.take(grad_pre, col_ids, axis=0).reshape(row_blocks, per_row, BLK, tok_rows)
    dp_count = lax.axis_size("dp")
    weight_scale = 1.0 / math.sqrt(tok_rows * dp_count)
    block_terms = jnp.einsum(
        "rkct,rbt->rkcb", pre_blocks, normed_cols, preferred_element_type=jnp.float32
    )
    block_partial = (block_terms * weight_scale).reshape(kept_count, BLK * BLK)
    capacity = 2 * kept_count // dp_count
    outgoing = (
        jnp.zeros((dp_count * capacity, BLK * BLK), jnp.float32).at[slot_ids].set(block_partial)
    )
    outgoing = outgoing.reshape(dp_count, capacity, BLK * BLK)
    owned_grad = sum_sources(
        lax.all_to_all(
            outgoing.astype(jnp.bfloat16), "dp", split_axis=0, concat_axis=0, tiled=True
        ).astype(outgoing.dtype)
    )
    normed_part = jnp.einsum(
        "rkbc,rkct->rbt", in_blocks, pre_blocks, preferred_element_type=jnp.float32
    )
    normed_part = normed_part.transpose(2, 0, 1).reshape(tok_rows, feat_width)
    grad_normed = lax.psum_scatter(normed_part, "mp", scatter_dimension=1, tiled=True).astype(
        jnp.bfloat16
    )
    return (branch, grad_normed, owned_grad[None])


def solution(mesh):
    placed = (
        P("dp", "mp"),
        P(),
        P("mp", None),
        P("mp", None),
        P("dp", "mp"),
        P("mp", None),
        P("mp", None),
    )
    fits = mesh.shape["dp"] == 8 and mesh.shape["mp"] == 4
    return jax.shard_map(
        fast_body if fits else body,
        mesh=mesh,
        in_specs=placed,
        out_specs=(P("dp", "mp"), P("dp", "mp"), P("mp", "dp", None)),
        check_vma=False,
    )
```

profile of v0, /device:TPU:0, one launch (start us, length us, event | category | flops | bytes accessed | tf_op | source)
XLA Modules:
  0.0 98.7 jit_solution(17105734996748810492)
XLA Ops:
  0.6 0.8 constant_dynamic-update-slice_fusion.1
  1.5 0.8 constant_dynamic-update-slice_fusion.s0
  2.3 5.0 %collective-permute-start.6 = (bf16[256,256]{1,0:T(8,128)(2,1)S(1)}, bf16[256,256]{1,0:T(8,128)(2,1)S(1)}, u32[]{:S(2)}, u32[]{:S(2)}) collective-permute-start(bf16[256,256]{1,0:T(8,128)(2,1)S(1)} %constant_dynamic-update-slice_fusion.s0), channel_id=1, source_target_pairs={{8,0},{12,4},{16,8},{20,12},{24,16},{28,20},{0,24},{4,28},{9,1},{1... | collective-permute-start | bytes 393224 | tf_op jit(solution)/shard_map/ppermute | solution.py:320
  7.4 0.0 collective-permute-start.7
  7.4 1.0 %collective-permute-start.8 = (bf16[256,256]{1,0:T(8,128)(2,1)S(1)}, bf16[256,256]{1,0:T(8,128)(2,1)S(1)}, u32[]{:S(2)}, u32[]{:S(2)}) collective-permute-start(bf16[256,256]{1,0:T(8,128)(2,1)S(1)} %constant_dynamic-update-slice_fusion.s0), channel_id=1, source_target_pairs={{24,0},{28,4},{0,8},{4,12},{8,16},{12,20},{16,24},{20,28},{25,1},{... | collective-permute-start | bytes 393224 | tf_op jit(solution)/shard_map/ppermute | solution.py:320
  8.4 2.9 %collective-permute-done.6 = bf16[256,256]{1,0:T(8,128)(2,1)S(1)} collective-permute-done((bf16[256,256]{1,0:T(8,128)(2,1)S(1)}, bf16[256,256]{1,0:T(8,128)(2,1)S(1)}, u32[]{:S(2)}, u32[]{:S(2)}) %collective-permute-start.6) | collective-permute-done | bytes 131104 | tf_op jit(solution)/shard_map/ppermute | solution.py:320
  11.3 7.3 %collective-permute-done.7 = bf16[256,256]{1,0:T(8,128)(2,1)S(1)} collective-permute-done((bf16[256,256]{1,0:T(8,128)(2,1)S(1)}, bf16[256,256]{1,0:T(8,128)(2,1)S(1)}, u32[]{:S(2)}, u32[]{:S(2)}) %collective-permute-start.7) | collective-permute-done | bytes 131104 | tf_op jit(solution)/shard_map/ppermute | solution.py:320
  18.6 0.0 collective-permute-done.8
  18.6 1.6 %collective-permute-start.10 = (bf16[768,256]{1,0:T(8,128)(2,1)S(1)}, bf16[768,256]{1,0:T(8,128)(2,1)S(1)}, u32[]{:S(2)}, u32[]{:S(2)}) collective-permute-start(bf16[768,256]{1,0:T(8,128)(2,1)S(1)} %constant_dynamic-update-slice_fusion.2.z0), channel_id=1, source_target_pairs={{0,2},{1,3},{2,0},{3,1},{4,6},{5,7},{6,4},{7,5},{8,10},{9,11},{10,... | collective-permute-start | bytes 1179656 | tf_op jit(solution)/shard_map/ppermute | solution.py:322
  20.2 0.0 collective-permute-start
  20.2 0.5 collective-permute-start.1
  20.7 1.4 %collective-permute-start.2 = (bf16[256,256]{1,0:T(8,128)(2,1)S(1)}, bf16[256,256]{1,0:T(8,128)(2,1)S(1)}, u32[]{:S(2)}, u32[]{:S(2)}) collective-permute-start(bf16[256,256]{1,0:T(8,128)(2,1)S(1)} %constant_dynamic-update-slice_fusion.s0), channel_id=1, source_target_pairs={{0,3},{1,2},{2,1},{3,0},{4,7},{5,6},{6,5},{7,4},{8,11},{9,10},{10,... | collective-permute-start | bytes 393224 | tf_op jit(solution)/shard_map/ppermute | solution.py:318
  22.1 1.6 %plan.1 = s32[8,256]{1,0:T(8,128)} custom-call(s32[1,256]{1,0:T(1,128)} %cols_ref.1, s32[1,256]{1,0:T(1,128)} %slots_ref.1), custom_call_target="tpu_custom_call" | custom-call | flops 4000000 | bytes 16384 | tf_op jit(solution)/shard_map/plan/pallas_call | solution.py:333
  23.6 1.6 %copy-done = bf16[256,4096]{1,0:T(8,128)(2,1)S(1)} copy-done((bf16[256,4096]{1,0:T(8,128)(2,1)S(1)}, bf16[256,4096]{1,0:T(8,128)(2,1)}, u32[]{:S(2)}) %copy-start) | copy-done | bytes 2097176
  25.2 1.6 %copy-done.1 = bf16[256,4096]{1,0:T(8,128)(2,1)S(1)} copy-done((bf16[256,4096]{1,0:T(8,128)(2,1)S(1)}, bf16[256,4096]{1,0:T(8,128)(2,1)}, u32[]{:S(2)}) %copy-start.1) | copy-done | bytes 2097176
  26.8 13.1 %prepare.1 = (bf16[16,256,256]{2,1,0:T(8,128)(2,1)S(1)}, bf16[16,64,1024]{2,1,0:T(8,128)(2,1)S(1)}, bf16[16,512,128]{2,1,0:T(8,128)(2,1)S(1)}, bf16[16,64,1024]{2,1,0:T(8,128)(2,1)S(1)}) custom-call(bf16[256,4096]{1,0:T(8,128)(2,1)S(1)} %copy-done, bf16[256,4096]{1,0:T(8,128)(2,1)S(1)} %copy-done.1), custom_call_target="tpu_custom_call" | custom-call | flops 2147483648 | bytes 12582912 | tf_op jit(solution)/shard_map/prepare/pallas_call | solution.py:346
  39.9 0.3 collective-permute-start.9
  40.3 0.0 collective-permute-done.10.z2
  40.3 0.2 collective-permute-start.11
  40.6 13.7 %local.1 = (bf16[256,256]{1,0:T(8,128)(2,1)S(1)}, bf16[256,256]{1,0:T(8,128)(2,1)S(1)}, bf16[256,256]{1,0:T(8,128)(2,1)S(1)}, bf16[256,256]{1,0:T(8,128)(2,1)S(1...) custom-call(s32[8,256]{1,0:T(8,128)S(1)} %copy-done.3, f32[1,1024]{1,0:T(1,128)S(1)} %bitcast.1, ...), custom_call_target="tpu_custom_call" | custom-call | flops 4294967296 | bytes 10485760 | tf_op jit(solution)/shard_map/local/pallas_call | solution.py:362
  54.3 0.3 collective-permute-start.3
  54.6 0.5 collective-permute-start.4
  55.1 1.1 %collective-permute-start.5 = (bf16[256,256]{1,0:T(8,128)(2,1)S(1)}, bf16[256,256]{1,0:T(8,128)(2,1)S(1)}, u32[]{:S(2)}, u32[]{:S(2)}) collective-permute-start(bf16[256,256]{1,0:T(8,128)(2,1)S(1)} %get-tuple-element.22), channel_id=1, source_target_pairs={{0,3},{1,2},{2,1},{3,0},{4,7},{5,6},{6,5},{7,4},{8,11},{9,10},{10,... | collective-permute-start | bytes 393224 | tf_op jit(solution)/shard_map/ppermute | solution.py:424
  56.2 26.5 %blocks.1 = (bf16[64,32,128]{2,1,0:T(8,128)(2,1)S(1)}, f32[64,32,128]{2,1,0:T(8,128)S(1)}) custom-call(s32[8,256]{1,0:T(8,128)S(1)} %copy-done.3, f32[1,1024]{1,0:T(1,128)S(1)} %bitcast.2, bf16[768,256]{1,0:T(8,128)(2,1)S(1)} %constant_dynamic-update-slice_fusion.2.z0, bf16[768,256]{1,0:T(8,128)(2,1)S(1)} %collective-permute-done.9.z1, ...), custom_call_target="tpu_custom_call" | custom-call | flops 6442450944 | bytes 6291456 | tf_op jit(solution)/shard_map/blocks/pallas_call | solution.py:394
  82.7 1.6 %collective-permute-start.12 = (bf16[64,32,128]{2,1,0:T(8,128)(2,1)S(1)}, bf16[64,32,128]{2,1,0:T(8,128)(2,1)S(1)}, u32[]{:S(2)}, u32[]{:S(2)}) collective-permute-start(bf16[64,32,128]{2,1,0:T(8,128)(2,1)S(1)} %get-tuple-element.26), channel_id=1, source_target_pairs={{0,4},{4,0},{8,12},{12,8},{16,20},{20,16},{24,28},{28,24},{1,5},{5... | collective-permute-start | bytes 1572872 | tf_op jit(solution)/shard_map/ppermute | solution.py:423
  84.2 0.0 collective-permute-done.4
  84.2 0.0 collective-permute-done.5
  84.2 0.1 add_convert_fusion
  84.3 0.7 fusion
  85.0 12.3 %collective-permute-done.12 = bf16[64,32,128]{2,1,0:T(8,128)(2,1)S(1)} collective-permute-done((bf16[64,32,128]{2,1,0:T(8,128)(2,1)S(1)}, bf16[64,32,128]{2,1,0:T(8,128)(2,1)S(1)}, u32[]{:S(2)}, u32[]{:S(2)}) %collective-permute-start.12) | collective-permute-done | bytes 524320 | tf_op jit(solution)/shard_map/ppermute | solution.py:423
  97.3 0.2 convert_add_fusion
  97.5 1.2 %broadcast_in_dim_reshape.3 = f32[1,64,4096]{2,1,0:T(8,128)} reshape(f32[64,32,128]{2,1,0:T(8,128)S(1)} %convert_add_fusion) | data formatting | bytes 2097152 | tf_op jit(solution)/shard_map/broadcast_in_dim;reshape | solution.py:428
  (15 shorter events, 0.1 us)
Async XLA Ops:
  2.3 9.0 %collective-permute-start.6 = (bf16[256,256]{1,0:T(8,128)(2,1)S(1)}, bf16[256,256]{1,0:T(8,128)(2,1)S(1)}, u32[]{:S(2)}, u32[]{:S(2)}) collective-permute-start(bf16[256,256]{1,0:T(8,128)(2,1)S(1)} %constant_dynamic-update-slice_fusion.s0), channel_id=1, source_target_pairs={{8,0},{12,4},{16,8},{20,12},{24,16},{28,20},{0,24},{4,28},{9,1},{1... | collective-permute-start | bytes 393224 | tf_op jit(solution)/shard_map/ppermute | solution.py:320
  7.4 11.2 %collective-permute-start.7 = (bf16[256,256]{1,0:T(8,128)(2,1)S(1)}, bf16[256,256]{1,0:T(8,128)(2,1)S(1)}, u32[]{:S(2)}, u32[]{:S(2)}) collective-permute-start(bf16[256,256]{1,0:T(8,128)(2,1)S(1)} %constant_dynamic-update-slice_fusion.s0), channel_id=1, source_target_pairs={{16,0},{20,4},{24,8},{28,12},{0,16},{4,20},{8,24},{12,28},{17,1},{... | collective-permute-start | bytes 393224 | tf_op jit(solution)/shard_map/ppermute | solution.py:320
  7.4 11.2 %collective-permute-start.8 = (bf16[256,256]{1,0:T(8,128)(2,1)S(1)}, bf16[256,256]{1,0:T(8,128)(2,1)S(1)}, u32[]{:S(2)}, u32[]{:S(2)}) collective-permute-start(bf16[256,256]{1,0:T(8,128)(2,1)S(1)} %constant_dynamic-update-slice_fusion.s0), channel_id=1, source_target_pairs={{24,0},{28,4},{0,8},{4,12},{8,16},{12,20},{16,24},{20,28},{25,1},{... | collective-permute-start | bytes 393224 | tf_op jit(solution)/shard_map/ppermute | solution.py:320
  18.6 21.7 %collective-permute-start.10 = (bf16[768,256]{1,0:T(8,128)(2,1)S(1)}, bf16[768,256]{1,0:T(8,128)(2,1)S(1)}, u32[]{:S(2)}, u32[]{:S(2)}) collective-permute-start(bf16[768,256]{1,0:T(8,128)(2,1)S(1)} %constant_dynamic-update-slice_fusion.2.z0), channel_id=1, source_target_pairs={{0,2},{1,3},{2,0},{3,1},{4,6},{5,7},{6,4},{7,5},{8,10},{9,11},{10,... | collective-permute-start | bytes 1179656 | tf_op jit(solution)/shard_map/ppermute | solution.py:322
  20.2 20.3 %collective-permute-start = (bf16[256,256]{1,0:T(8,128)(2,1)S(1)}, bf16[256,256]{1,0:T(8,128)(2,1)S(1)}, u32[]{:S(2)}, u32[]{:S(2)}) collective-permute-start(bf16[256,256]{1,0:T(8,128)(2,1)S(1)} %constant_dynamic-update-slice_fusion.s0), channel_id=1, source_target_pairs={{0,1},{1,0},{2,3},{3,2},{4,5},{5,4},{6,7},{7,6},{8,9},{9,8},{10,11... | collective-permute-start | bytes 393224 | tf_op jit(solution)/shard_map/ppermute | solution.py:318
  20.2 20.3 %collective-permute-start.1 = (bf16[256,256]{1,0:T(8,128)(2,1)S(1)}, bf16[256,256]{1,0:T(8,128)(2,1)S(1)}, u32[]{:S(2)}, u32[]{:S(2)}) collective-permute-start(bf16[256,256]{1,0:T(8,128)(2,1)S(1)} %constant_dynamic-update-slice_fusion.s0), channel_id=1, source_target_pairs={{0,2},{1,3},{2,0},{3,1},{4,6},{5,7},{6,4},{7,5},{8,10},{9,11},{10,... | collective-permute-start | bytes 393224 | tf_op jit(solution)/shard_map/ppermute | solution.py:318
  20.7 19.8 %collective-permute-start.2 = (bf16[256,256]{1,0:T(8,128)(2,1)S(1)}, bf16[256,256]{1,0:T(8,128)(2,1)S(1)}, u32[]{:S(2)}, u32[]{:S(2)}) collective-permute-start(bf16[256,256]{1,0:T(8,128)(2,1)S(1)} %constant_dynamic-update-slice_fusion.s0), channel_id=1, source_target_pairs={{0,3},{1,2},{2,1},{3,0},{4,7},{5,6},{6,5},{7,4},{8,11},{9,10},{10,... | collective-permute-start | bytes 393224 | tf_op jit(solution)/shard_map/ppermute | solution.py:318
  23.6 1.6 %copy-start = (bf16[256,4096]{1,0:T(8,128)(2,1)S(1)}, bf16[256,4096]{1,0:T(8,128)(2,1)}, u32[]{:S(2)}) copy-start(bf16[256,4096]{1,0:T(8,128)(2,1)} %win_ref.1) | copy-start | bytes 6291460
  25.2 1.6 %copy-start.1 = (bf16[256,4096]{1,0:T(8,128)(2,1)S(1)}, bf16[256,4096]{1,0:T(8,128)(2,1)}, u32[]{:S(2)}) copy-start(bf16[256,4096]{1,0:T(8,128)(2,1)} %wout_ref.1) | copy-start | bytes 6291460
  26.8 13.7 %copy-start.2 = (f32[1024]{0:T(1024)S(1)}, f32[1024]{0:T(1024)}, u32[]{:S(2)}) copy-start(f32[1024]{0:T(1024)} %param.8) | copy-start | bytes 12292
  26.8 13.7 %copy-start.3 = (s32[8,256]{1,0:T(8,128)S(1)}, s32[8,256]{1,0:T(8,128)}, u32[]{:S(2)}) copy-start(s32[8,256]{1,0:T(8,128)} %plan.1) | copy-start | bytes 24580
  39.9 16.3 %collective-permute-start.9 = (bf16[768,256]{1,0:T(8,128)(2,1)S(1)}, bf16[768,256]{1,0:T(8,128)(2,1)S(1)}, u32[]{:S(2)}, u32[]{:S(2)}) collective-permute-start(bf16[768,256]{1,0:T(8,128)(2,1)S(1)} %constant_dynamic-update-slice_fusion.2.z0), channel_id=1, source_target_pairs={{0,1},{1,0},{2,3},{3,2},{4,5},{5,4},{6,7},{7,6},{8,9},{9,8},{10,11... | collective-permute-start | bytes 1179656 | tf_op jit(solution)/shard_map/ppermute | solution.py:325
  40.3 15.9 %collective-permute-start.11 = (bf16[768,256]{1,0:T(8,128)(2,1)S(1)}, bf16[768,256]{1,0:T(8,128)(2,1)S(1)}, u32[]{:S(2)}, u32[]{:S(2)}) collective-permute-start(bf16[768,256]{1,0:T(8,128)(2,1)S(1)} %collective-permute-done.10.z2), channel_id=1, source_target_pairs={{0,1},{1,0},{2,3},{3,2},{4,5},{5,4},{6,7},{7,6},{8,9},{9,8},{10,11... | collective-permute-start | bytes 1179656 | tf_op jit(solution)/shard_map/ppermute | solution.py:327
  54.3 29.9 %collective-permute-start.3 = (bf16[256,256]{1,0:T(8,128)(2,1)S(1)}, bf16[256,256]{1,0:T(8,128)(2,1)S(1)}, u32[]{:S(2)}, u32[]{:S(2)}) collective-permute-start(bf16[256,256]{1,0:T(8,128)(2,1)S(1)} %get-tuple-element.20), channel_id=1, source_target_pairs={{0,1},{1,0},{2,3},{3,2},{4,5},{5,4},{6,7},{7,6},{8,9},{9,8},{10,11... | collective-permute-start | bytes 393224 | tf_op jit(solution)/shard_map/ppermute | solution.py:424
  54.6 29.6 %collective-permute-start.4 = (bf16[256,256]{1,0:T(8,128)(2,1)S(1)}, bf16[256,256]{1,0:T(8,128)(2,1)S(1)}, u32[]{:S(2)}, u32[]{:S(2)}) collective-permute-start(bf16[256,256]{1,0:T(8,128)(2,1)S(1)} %get-tuple-element.21), channel_id=1, source_target_pairs={{0,2},{1,3},{2,0},{3,1},{4,6},{5,7},{6,4},{7,5},{8,10},{9,11},{10,... | collective-permute-start | bytes 393224 | tf_op jit(solution)/shard_map/ppermute | solution.py:424
  55.1 29.1 %collective-permute-start.5 = (bf16[256,256]{1,0:T(8,128)(2,1)S(1)}, bf16[256,256]{1,0:T(8,128)(2,1)S(1)}, u32[]{:S(2)}, u32[]{:S(2)}) collective-permute-start(bf16[256,256]{1,0:T(8,128)(2,1)S(1)} %get-tuple-element.22), channel_id=1, source_target_pairs={{0,3},{1,2},{2,1},{3,0},{4,7},{5,6},{6,5},{7,4},{8,11},{9,10},{10,... | collective-permute-start | bytes 393224 | tf_op jit(solution)/shard_map/ppermute | solution.py:424
  82.7 14.7 %collective-permute-start.12 = (bf16[64,32,128]{2,1,0:T(8,128)(2,1)S(1)}, bf16[64,32,128]{2,1,0:T(8,128)(2,1)S(1)}, u32[]{:S(2)}, u32[]{:S(2)}) collective-permute-start(bf16[64,32,128]{2,1,0:T(8,128)(2,1)S(1)} %get-tuple-element.26), channel_id=1, source_target_pairs={{0,4},{4,0},{8,12},{12,8},{16,20},{20,16},{24,28},{28,24},{1,5},{5... | collective-permute-start | bytes 1572872 | tf_op jit(solution)/shard_map/ppermute | solution.py:423
where the time goes:
time: 101 us; the launch traced here: 98.7 us
  Pallas kernels  54.9 us (54%)
  waiting for transfers between devices  22.5 us (22%)
  starting transfers between devices  13.6 us (13%)
  local copies, waits for them, and re-layouts  6.73 us (7%)
    pallas_call x1, Pallas kernels, fast_body(): pl.pallas_call(functools.partial(block_kernel, scale), out_shape=[jax.Sha...  26.5 us
    pallas_call x1, Pallas kernels, fast_body(): pl.pallas_call(local_kernel, out_shape=[jax.ShapeDtypeStruct((2 * tok, wi...  13.7 us
    pallas_call x1, Pallas kernels, fast_body(): pl.pallas_call(prepare_kernel, out_shape=[jax.ShapeDtypeStruct((row_block...  13.1 us
    ppermute x1, waiting for transfers between devices, fast_body(): arrived = lax.ppermute(for_peer, 'dp', across_x)  12.3 us
    ppermute x3, waiting for transfers between devices, fast_body(): lax.ppermute(own, 'dp', along_z[j])  10.2 us
    ppermute x3, starting transfers between devices, fast_body(): lax.ppermute(own, 'dp', along_z[j])  6.06 us
    unnamed x11, local copies, waits for them, and re-layouts  4.05 us
  transfers between devices with their start and end apart: 13, of which 3 were waited for; matrix products, arithmetic and copies ran while one was open for 1% of the time, Pallas kernels for 56%

commit v1 on v0

--- a/solution.py
+++ b/solution.py
@@ -12,6 +12,8 @@
 BLK = 64
 HALF = BLK // 2
 GROUP = 4
+FIRST = 1024
+BATCH = 16
 
 
 norm_eps = 1e-06
@@ -58,15 +60,29 @@
     return jnp.where(col == target, 1.0, 0.0).astype(BF16)
 
 
-def plan_kernel(cap, col_blocks, cols_ref, slots_ref, out_ref):
+def plan_kernel(cap, col_blocks, row_blocks, cols_ref, slots_ref, x_ref, grad_ref, out_ref, both_ref):
     kept = cols_ref.shape[1]
+    per_row = kept // row_blocks
     me = lax.axis_index("dp")
+    tok = x_ref.shape[0]
+    both_ref[:tok, :] = x_ref[...]
+    both_ref[tok:, :] = grad_ref[...]
     cols, slots = cols_ref[...], slots_ref[...]
     owner = lax.div(slots, jnp.int32(cap))
-    eq = cols == iota((col_blocks, kept), 0)
     own = jnp.where(owner == me, 1.0, 0.0)
     peer = jnp.where(owner == (me ^ 1), 1.0, 0.0)
-    needed = jnp.max(jnp.where(eq, own + peer, 0.0), axis=1, keepdims=True)
+    flag = own + peer
+    needed = jnp.max(jnp.where(cols == iota((col_blocks, kept), 0), flag, 0.0), axis=1, keepdims=True)
+
+    def to_column(row):
+        size = row.shape[1]
+        eye = iota((size, size), 0) == iota((size, size), 1)
+        return jnp.sum(jnp.where(eye, row, 0.0), axis=1, keepdims=True)
+
+    def to_row(column):
+        size = column.shape[0]
+        eye = iota((size, size), 0) == iota((size, size), 1)
+        return jnp.sum(jnp.where(eye, column, 0.0), axis=0, keepdims=True)
 
     def listed(flags_r, flags_c):
         size = flags_r.shape[1]
@@ -74,38 +90,30 @@
         place = jnp.sum(jnp.where(before, flags_r, 0.0), axis=1, keepdims=True)
         hit = (place == iota((size, kept), 1).astype(F32)) & (flags_c > 0)
         index = iota((size, 1), 0).astype(F32)
-        row = jnp.sum(jnp.where(hit, index, 0.0), axis=0, keepdims=True)
-        return row, jnp.sum(flags_r, axis=1, keepdims=True)
-
-    def to_column(row):
-        size = row.shape[1]
-        eye = iota((size, size), 0) == iota((size, size), 1)
-        return jnp.sum(jnp.where(eye, row, 0.0), axis=1, keepdims=True)
-
-    def to_row(column):
-        size = column.shape[0]
-        eye = iota((size, size), 0) == iota((size, size), 1)
-        return jnp.sum(jnp.where(eye, column, 0.0), axis=0, keepdims=True)
-
-    peer_list, peer_count = listed(peer, to_column(peer))
-    own_list, own_count = listed(own, to_column(own))
-    need_list, need_count = listed(to_row(needed), needed)
+        return jnp.sum(jnp.where(hit, index, 0.0), axis=0, keepdims=True)
+
+    cols_r = cols.astype(F32)
+    cols_c = to_column(cols_r)
+    earlier = iota((kept, kept), 1) < iota((kept, kept), 0)
+    seen = jnp.max(jnp.where(earlier & (cols_r == cols_c), 1.0, 0.0), axis=1, keepdims=True)
+    flag_c = to_column(flag)
+    pair_end = iota((kept, kept), 0) < 2 * per_row * iota((kept, kept), 1)
     rows = [
-        cols.astype(F32),
-        (slots - owner * cap).astype(F32),
-        peer_list,
-        own_list,
-        need_list,
-        peer_count,
-        own_count,
-        need_count,
+        cols_r + FIRST * (1.0 - to_row(seen)),
+        (slots - owner * cap).astype(F32) + cap * own,
+        listed(flag, flag_c),
+        jnp.sum(jnp.where(pair_end, flag_c, 0.0), axis=0, keepdims=True),
+        listed(to_row(needed), needed),
+        jnp.sum(needed, axis=0, keepdims=True),
     ]
     for index, row in enumerate(rows):
         out_ref[index : index + 1, :] = jnp.broadcast_to(row, (1, kept)).astype(jnp.int32)
-
-
-def prepare_kernel(win_ref, wout_ref, a_in, b_in, p_out, a_out, order):
-    per_row, length = win_ref.shape
+    out_ref[len(rows) :, :] = jnp.zeros((out_ref.shape[0] - len(rows), kept), jnp.int32)
+
+
+def prepare_kernel(win_ref, wout_ref, a_in, b_in, p_out, a_out, order, both):
+    count = a_in.shape[0]
+    per_row, length = win_ref.shape[0] // count, win_ref.shape[1]
     lanes = 2 * BLK
     rows = per_row * HALF
 
@@ -114,36 +122,46 @@
         row, col = iota((rows, rows), 0), iota((rows, rows), 1)
         source = (row & (HALF - 1)) * per_row + lax.div(row, jnp.int32(HALF))
         order[...] = jnp.where(col == source, 1.0, 0.0).astype(BF16)
-
-    row, col = iota((lanes, lanes), 0), iota((lanes, lanes), 1)
-    swap = jnp.where(((col + BLK) & (lanes - 1)) == row, 1.0, 0.0).astype(BF16)
-    perm = even_first(lanes)
-    both = jnp.concatenate([perm, dot(perm, swap).astype(BF16)], axis=1)
+        row, col = iota((lanes, lanes), 0), iota((lanes, lanes), 1)
+        swap = jnp.where(((col + BLK) & (lanes - 1)) == row, 1.0, 0.0).astype(BF16)
+        perm = even_first(lanes)
+        both[:, :lanes] = perm
+        both[:, lanes:] = dot(perm, swap).astype(BF16)
 
     def by_block(ref):
-        stacked = jnp.concatenate(
-            [ref[:, j * lanes : (j + 1) * lanes] for j in range(length // lanes)], axis=0
-        )
-        return dot(order[...], stacked).astype(BF16)
-
-    kept_in = dot(by_block(win_ref), both).astype(BF16)
-    kept_out = by_block(wout_ref)
-    p_out[0] = kept_out
+        stacked = [
+            jnp.concatenate(
+                [
+                    ref[n * per_row : (n + 1) * per_row, j * lanes : (j + 1) * lanes]
+                    for j in range(length // lanes)
+                ],
+                axis=0,
+            )
+            for n in range(count)
+        ]
+        return dot(order[...], jnp.concatenate(stacked, axis=1)).astype(BF16)
+
+    ordered_in, ordered_out = by_block(win_ref), by_block(wout_ref)
     left = iota((HALF, lanes), 1) < BLK
-    for pair in range(per_row // 2):
-        first = kept_in[2 * pair * HALF : (2 * pair + 1) * HALF].astype(F32)
-        second = kept_in[(2 * pair + 1) * HALF : (2 * pair + 2) * HALF].astype(F32)
-        at = slice(pair * lanes, (pair + 1) * lanes)
-        b_in[0, :HALF, at] = jnp.where(left, first[:, :lanes], second[:, lanes:]).astype(BF16)
-        b_in[0, HALF:, at] = jnp.where(left, first[:, lanes:], second[:, :lanes]).astype(BF16)
-    for quad in range(per_row // GROUP):
-        rows_of = slice(quad * lanes, (quad + 1) * lanes)
-        turned = kept_in[rows_of, :lanes].T
-        a_in[0, quad * BLK : (quad + 1) * BLK, :lanes] = turned[:BLK]
-        a_in[0, quad * BLK : (quad + 1) * BLK, lanes:] = turned[BLK:]
-        turned = kept_out[rows_of].T
-        a_out[0, :, rows_of] = turned[:BLK]
-        a_out[0, :, rows + quad * lanes : rows + (quad + 1) * lanes] = turned[BLK:]
+    for n in range(count):
+        of_n = slice(n * lanes, (n + 1) * lanes)
+        kept_in = dot(ordered_in[:, of_n], both[...])
+        kept_out = ordered_out[:, of_n]
+        p_out[n] = kept_out
+        for pair in range(per_row // 2):
+            first = kept_in[2 * pair * HALF : (2 * pair + 1) * HALF]
+            second = kept_in[(2 * pair + 1) * HALF : (2 * pair + 2) * HALF]
+            at = slice(pair * lanes, (pair + 1) * lanes)
+            b_in[n, :HALF, at] = jnp.where(left, first[:, :lanes], second[:, lanes:]).astype(BF16)
+            b_in[n, HALF:, at] = jnp.where(left, first[:, lanes:], second[:, :lanes]).astype(BF16)
+        for quad in range(per_row // GROUP):
+            rows_of = slice(quad * lanes, (quad + 1) * lanes)
+            turned = kept_in[rows_of, :lanes].astype(BF16).T
+            a_in[n, quad * BLK : (quad + 1) * BLK, :lanes] = turned[:BLK]
+            a_in[n, quad * BLK : (quad + 1) * BLK, lanes:] = turned[BLK:]
+            turned = kept_out[rows_of].T
+            a_out[n, :, rows_of] = turned[:BLK]
+            a_out[n, :, rows + quad * lanes : rows + (quad + 1) * lanes] = turned[BLK:]
 
 
 def load_tokens(pieces, tok, gain_ref, perm, n_s, nt_s, gt_s, base):
@@ -167,8 +185,6 @@
     row_blocks = a_in.shape[0]
     tok = nt_s.shape[1]
     per_row = p_out.shape[1] // HALF
-    acc_v[...] = jnp.zeros_like(acc_v)
-    acc_a[...] = jnp.zeros_like(acc_a)
     gap = jnp.zeros((HALF, tok), BF16)
     gap2 = jnp.zeros((BLK, tok), BF16)
 
@@ -191,17 +207,20 @@
             new = []
             for u in range(GROUP):
                 k = quad * GROUP + u
-                c = plan[0, r * per_row + k]
-                v = acc_v[c] + terms_v[quad * BLK : (quad + 1) * BLK, u * tok : (u + 1) * tok]
+                code = plan[0, r * per_row + k]
+                c, first = code & (FIRST - 1), code >= FIRST
+                v = terms_v[quad * BLK : (quad + 1) * BLK, u * tok : (u + 1) * tok]
                 rows = terms_a[k * HALF : (k + 1) * HALF]
-                a = acc_a[c] + jnp.concatenate([rows[:, :tok], rows[:, tok:]], axis=0)
+                a = jnp.concatenate([rows[:, :tok], rows[:, tok:]], axis=0)
+                v = jnp.where(first, v, acc_v[c] + v)
+                a = jnp.where(first, a, acc_a[c] + a)
                 new.append((c, v, a))
             for c, v, a in new:
                 acc_v[c] = v
                 acc_a[c] = a
         return carry
 
-    lax.fori_loop(0, row_blocks, step, 0)
+    lax.fori_loop(0, row_blocks, step, 0, unroll=4)
 
 
 def local_kernel(
@@ -222,18 +241,18 @@
         gp_ref[c] = (acc_a[c] * slope).astype(BF16)
         return carry
 
-    lax.fori_loop(0, col_blocks, bend, 0, unroll=2)
+    lax.fori_loop(0, col_blocks, bend, 0, unroll=4)
 
     def contract(r, carry):
         at = pl.ds(pl.multiple_of(r * BLK, BLK), BLK)
-        ids = [plan[0, r * per_row + k] for k in range(per_row)]
+        ids = [plan[0, r * per_row + k] & (FIRST - 1) for k in range(per_row)]
         acts = [act_s[c, a * HALF : (a + 1) * HALF, :] for a in (0, 1) for c in ids]
         br_s[at, :] = dot(a_out[r], jnp.concatenate(acts, axis=0)).astype(BF16)
         grads = [gp_ref[c] for c in ids]
         gn_s[at, :] = dot(b_in[r], jnp.concatenate(grads, axis=0)).astype(BF16)
         return carry
 
-    lax.fori_loop(0, row_blocks, contract, 0)
+    lax.fori_loop(0, row_blocks, contract, 0, unroll=4)
     mine = lax.axis_index("mp")
     for q, out in enumerate((o0, o1, o2, o3)):
         at = pl.ds(pl.multiple_of((mine ^ q) * width, width), width)
@@ -243,7 +262,7 @@
 
 def block_kernel(
     scale, plan, gain_ref, z0, z1, z2, z3, a_in, p_out, gp_own, n_own, peer_ref, own_ref,
-    n_s, nt_s, gt_s, acc_v, acc_a, gp_s
+    n_s, nt_s, gt_s, acc_v, acc_a, gp_s, found
 ):
     tok = n_own.shape[0]
     per_row = p_out.shape[1] // HALF
@@ -256,7 +275,7 @@
         gp_s[c, :, :tok] = gp_own[c]
         return carry
 
-    lax.fori_loop(0, plan[7, 0], keep, 0)
+    lax.fori_loop(0, plan[5, 0], keep, 0)
     for j in range(z0.shape[0] // (2 * tok)):
         pieces = [(ref, 2 * tok * j) for ref in (z0, z1, z2, z3)]
         load_tokens(pieces, tok, gain_ref, perm, n_s, nt_s, gt_s, (j + 1) * tok)
@@ -268,30 +287,50 @@
             gp_s[c, :, (j + 1) * tok : (j + 2) * tok] = (acc_a[c] * slope).astype(BF16)
             return carry
 
-        lax.fori_loop(0, plan[7, 0], bend, 0)
+        lax.fori_loop(0, plan[5, 0], bend, 0)
 
     left = iota((HALF, lanes), 1) < BLK
-    for out_ref, list_row, count_row in ((peer_ref, 2, 5), (own_ref, 3, 6)):
-        out_ref[...] = jnp.zeros_like(out_ref)
-        count = plan[count_row, 0]
-
-        def outer(i, carry):
-            done = []
-            for u in range(GROUP):
-                k = plan[list_row, jnp.minimum(i * GROUP + u, count - 1)]
-                r = lax.div(k, jnp.int32(per_row))
-                at_lane = pl.ds(pl.multiple_of((r >> 1) * lanes, lanes), lanes)
-                block = dot(gp_s[plan[0, k]], n_s[:, at_lane]) * scale
-                odd = (r & 1) == 1
-                top, low = block[:HALF], block[HALF:]
-                top = jnp.where(odd, pltpu.roll(top, BLK, 1), top)
-                low = jnp.where(odd, low, pltpu.roll(low, BLK, 1))
-                done.append((plan[1, k], jnp.where(left, top, low).astype(out_ref.dtype)))
-            for slot, value in done:
-                out_ref[slot] = value
-            return carry
-
-        lax.fori_loop(0, (count + GROUP - 1) // GROUP, outer, 0)
+    cap = own_ref.shape[0]
+    found[...] = jnp.zeros_like(found)
+
+    def form(pair, first):
+        end = plan[3, pair + 1]
+        at_lane = pl.ds(pl.multiple_of(pair * lanes, lanes), lanes)
+        ids = [
+            plan[2, jnp.maximum(jnp.minimum(first + u, end - 1), 0)] for u in range(BATCH)
+        ]
+        grads = jnp.concatenate([gp_s[plan[0, k] & (FIRST - 1)] for k in ids], axis=0)
+        blocks = dot(grads, n_s[:, at_lane]) * scale
+        done = []
+        for u, k in enumerate(ids):
+            odd = (lax.div(k, jnp.int32(per_row)) & 1) == 1
+            top = blocks[u * BLK : u * BLK + HALF]
+            low = blocks[u * BLK + HALF : (u + 1) * BLK]
+            top = jnp.where(odd, pltpu.roll(top, BLK, 1), top)
+            low = jnp.where(odd, low, pltpu.roll(low, BLK, 1))
+            slot = jnp.where(first < end, plan[1, k], 2 * cap)
+            done.append((slot, jnp.where(left, top, low)))
+        for slot, value in done:
+            found[slot] = value
+
+    pairs = p_out.shape[0] // 2
+
+    def begin(pair, carry):
+        form(pair, plan[3, pair])
+        return carry
+
+    lax.fori_loop(0, pairs, begin, 0, unroll=2)
+
+    def finish(pair, carry):
+        @pl.when(plan[3, pair + 1] - plan[3, pair] > BATCH)
+        def _():
+            form(pair, plan[3, pair] + BATCH)
+
+        return carry
+
+    lax.fori_loop(0, pairs, finish, 0)
+    peer_ref[...] = found[:cap].astype(peer_ref.dtype)
+    own_ref[...] = found[cap : 2 * cap]
 
 
 def fast_body(x_in, gain, w_in, w_out, grad_out, block_cols, slots):
@@ -309,34 +348,26 @@
     across_x = [(i, i ^ 1) for i in range(dp_count)]
     near = [[(i, i ^ q) for i in range(mp_count)] for q in range(mp_count)]
     z_count = dp_count // 2
-    along_z = [
-        [(((z + j) % z_count) * 2 + x, z * 2 + x) for z in range(z_count) for x in range(2)]
-        for j in range(z_count)
-    ]
-
-    own = jnp.concatenate([x_in, grad_out], axis=0)
-    gathered = [own] + [lax.ppermute(own, "mp", near[q]) for q in range(1, mp_count)]
-    column = jnp.concatenate(
-        [lax.ppermute(own, "dp", along_z[j]) for j in range(1, z_count)], axis=0
-    )
-    column_y = lax.ppermute(column, "mp", near[2])
-    columns = [
-        column,
-        lax.ppermute(column, "mp", near[1]),
-        column_y,
-        lax.ppermute(column_y, "mp", near[1]),
-    ]
-    gain_row = gain.reshape(1, feat)
+    along_z = [[(i, i ^ (2 * j)) for i in range(dp_count)] for j in (1, 3, 2)]
+
     whole = pl.BlockSpec(memory_space=pltpu.VMEM)
     mm = 2 * tok * kept * BLK * BLK
 
-    plan = pl.pallas_call(
-        functools.partial(plan_kernel, cap, col_blocks),
-        out_shape=jax.ShapeDtypeStruct((8, kept), jnp.int32),
+    plan, own = pl.pallas_call(
+        functools.partial(plan_kernel, cap, col_blocks, row_blocks),
+        out_shape=[
+            jax.ShapeDtypeStruct((8, kept), jnp.int32),
+            jax.ShapeDtypeStruct((2 * tok, width), BF16),
+        ],
         cost_estimate=pl.CostEstimate(flops=4_000_000, bytes_accessed=16384, transcendentals=0),
         name="plan",
-    )(block_cols, slots)
-
+    )(block_cols, slots, x_in, grad_out)
+
+    pieces = [lax.ppermute(own, "dp", hop) for hop in along_z]
+    gathered = [own] + [lax.ppermute(own, "mp", near[q]) for q in range(1, mp_count)]
+    gain_row = gain.reshape(1, feat)
+
+    step = min(4, row_blocks)
     shapes = [
         (per_row // GROUP * BLK, 2 * lanes),
         (BLK, per_row * BLK),
@@ -346,16 +377,27 @@
     a_in, b_in, p_out, a_out = pl.pallas_call(
         prepare_kernel,
         out_shape=[jax.ShapeDtypeStruct((row_blocks, *shape), BF16) for shape in shapes],
-        grid=(row_blocks,),
-        in_specs=[pl.BlockSpec((per_row, BLK * BLK), lambda r: (r, 0))] * 2,
-        out_specs=[pl.BlockSpec((1, *shape), lambda r: (r, 0, 0)) for shape in shapes],
-        scratch_shapes=[pltpu.VMEM((per_row * HALF, per_row * HALF), BF16)],
+        grid=(row_blocks // step,),
+        in_specs=[pl.BlockSpec((step * per_row, BLK * BLK), lambda r: (r, 0))] * 2,
+        out_specs=[pl.BlockSpec((step, *shape), lambda r: (r, 0, 0)) for shape in shapes],
+        scratch_shapes=[
+            pltpu.VMEM((per_row * HALF, per_row * HALF), BF16),
+            pltpu.VMEM((lanes, 2 * lanes), BF16),
+        ],
         compiler_params=pltpu.CompilerParams(vmem_limit_bytes=24 * MIB),
         cost_estimate=pl.CostEstimate(
             flops=8 * mm, bytes_accessed=12 * kept * BLK * BLK, transcendentals=0
         ),
         name="prepare",
-    )(w_in, w_out)
+    )(
+        pltpu.with_memory_space_constraint(w_in, pltpu.HBM),
+        pltpu.with_memory_space_constraint(w_out, pltpu.HBM),
+    )
+
+    pieces, gathered, p_out = lax.optimization_barrier((pieces, gathered, p_out))
+    column = jnp.concatenate(pieces, axis=0)
+    column_c = lax.ppermute(column, "mp", near[1])
+    column_y = lax.ppermute(column, "mp", near[2])
 
     hidden_f32 = pltpu.VMEM((col_blocks, BLK, tok), F32)
     turned = pltpu.VMEM((feat, tok), BF16)
@@ -390,6 +432,8 @@
         name="local",
     )(plan, gain_row, *gathered, a_in, b_in, p_out, a_out)
 
+    column_y, n_own = lax.optimization_barrier((column_y, n_own))
+    columns = [column, column_c, column_y, lax.ppermute(column_y, "mp", near[1])]
     rows = tok * z_count
     for_peer, for_own = pl.pallas_call(
         functools.partial(block_kernel, scale),
@@ -409,6 +453,7 @@
                 hidden_f32,
                 hidden_f32,
                 pltpu.VMEM((col_blocks, BLK, rows), BF16),
+                pltpu.VMEM((2 * cap + 1, HALF, lanes), F32),
             ],
         ),
         compiler_params=pltpu.CompilerParams(vmem_limit_bytes=40 * MIB),

time: 101 us -> 68.9 us (0.68); the launches traced: 98.7 us -> 68.7 us
  Pallas kernels: 54.9 us -> 36.4 us
  waiting for transfers between devices: 22.5 us -> 14.6 us
  local copies, waits for them, and re-layouts: 6.73 us -> 1.86 us
  starting transfers between devices: 13.6 us -> 14.8 us
    ppermute x4, waiting for transfers between devices: 10.2 us -> 2.38 us  [the longest x3 2.38 us: fast_body(): pieces = [lax.ppermute(own, 'dp', hop) for hop in along_z]]
    pallas_call x1, Pallas kernels: 26.5 us -> 19.1 us  [fast_body(): pl.pallas_call(functools.partial(block_kernel, scale), out_shape=[jax.Sha...]
    pallas_call x1, Pallas kernels: 13.1 us -> 6.08 us  [fast_body(): pl.pallas_call(prepare_kernel, out_shape=[jax.ShapeDtypeStruct((row_block...]
    pallas_call x1, Pallas kernels: 13.7 us -> 9.43 us  [fast_body(): pl.pallas_call(local_kernel, out_shape=[jax.ShapeDtypeStruct((2 * tok, wi...]
    unnamed x11 -> x8, local copies, waits for them, and re-layouts: 4.05 us -> 0.03 us
    ppermute x3, starting transfers between devices: 1.86 us -> 3.15 us  [fast_body(): lax.ppermute(own, 'mp', near[q])]
  transfers between devices with their start and end apart: 13 -> 13, of which waited for: 3 -> 3; matrix products, arithmetic and copies ran while one was open for 1% -> 1% of each run, Pallas kernels for 56% -> 50%
where the time goes in v1:
time: 68.9 us; the launch traced here: 68.7 us
  Pallas kernels  36.4 us (53%)
  starting transfers between devices  14.8 us (21%)
  waiting for transfers between devices  14.6 us (21%)
  local copies, waits for them, and re-layouts  1.86 us (3%)
  between operations  0.74 us (1%)
    pallas_call x1, Pallas kernels, fast_body(): pl.pallas_call(functools.partial(block_kernel, scale), out_shape=[jax.Sha...  19.1 us
    ppermute x1, waiting for transfers between devices, fast_body(): arrived = lax.ppermute(for_peer, 'dp', across_x)  12.2 us
    pallas_call x1, Pallas kernels, fast_body(): pl.pallas_call(local_kernel, out_shape=[jax.ShapeDtypeStruct((2 * tok, wi...  9.43 us
    pallas_call x1, Pallas kernels, fast_body(): pl.pallas_call(prepare_kernel, out_shape=[jax.ShapeDtypeStruct((row_block...  6.08 us
    ppermute x3, starting transfers between devices, fast_body(): pieces = [lax.ppermute(own, 'dp', hop) for hop in along_z]  5.86 us
    ppermute x3, starting transfers between devices, fast_body(): lax.ppermute(own, 'mp', near[q])  3.15 us
    ppermute x3, waiting for transfers between devices, fast_body(): pieces = [lax.ppermute(own, 'dp', hop) for hop in along_z]  2.38 us
    ppermute x3, starting transfers between devices, fast_body(): lax.ppermute(parts[q], 'mp', near[q])  1.87 us
  transfers between devices with their start and end apart: 13, of which 3 were waited for; matrix products, arithmetic and copies ran while one was open for 1% of the time, Pallas kernels for 50%

profile of v1, /device:TPU:0, one launch (start us, length us, event | category | flops | bytes accessed | tf_op | source)
XLA Modules:
  0.0 68.7 jit_solution(835920797772557333)
XLA Ops:
  0.6 1.8 %plan.1 = (s32[8,256]{1,0:T(8,128)}, bf16[256,256]{1,0:T(8,128)(2,1)}) custom-call(s32[1,256]{1,0:T(1,128)} %cols_ref.1, s32[1,256]{1,0:T(1,128)} %slots_ref.1, bf16[128,256]{1,0:T(8,128)(2,1)} %x_ref.1, bf16[128,256]{1,0:T(8,128)(2,1)} %grad_ref.1), custom_call_target="tpu_custom_call" | custom-call | flops 4000000 | bytes 16384 | tf_op jit(solution)/shard_map/plan/pallas_call | solution.py:356
  2.5 2.5 %collective-permute-start.5 = (bf16[256,256]{1,0:T(8,128)(2,1)}, bf16[256,256]{1,0:T(8,128)(2,1)S(1)}, u32[]{:S(2)}, u32[]{:S(2)}) collective-permute-start(bf16[256,256]{1,0:T(8,128)(2,1)} %get-tuple-element.30.s0), channel_id=1, source_target_pairs={{0,3},{1,2},{2,1},{3,0},{4,7},{5,6},{6,5},{7,4},{8,11},{9,10},{10,... | collective-permute-start | bytes 393224 | tf_op jit(solution)/shard_map/ppermute | solution.py:367
  4.9 0.6 collective-permute-start.4
  5.6 0.0 collective-permute-start.3
  5.6 2.8 %collective-permute-start.2 = (bf16[256,256]{1,0:T(8,128)(2,1)}, bf16[256,256]{1,0:T(8,128)(2,1)S(1)}, u32[]{:S(2)}, u32[]{:S(2)}) collective-permute-start(bf16[256,256]{1,0:T(8,128)(2,1)} %get-tuple-element.30.s0), channel_id=1, source_target_pairs={{0,16},{4,20},{8,24},{12,28},{16,0},{20,4},{24,8},{28,12},{1,17},{... | collective-permute-start | bytes 393224 | tf_op jit(solution)/shard_map/ppermute | solution.py:366
  8.4 1.3 %collective-permute-start.1 = (bf16[256,256]{1,0:T(8,128)(2,1)}, bf16[256,256]{1,0:T(8,128)(2,1)S(1)}, u32[]{:S(2)}, u32[]{:S(2)}) collective-permute-start(bf16[256,256]{1,0:T(8,128)(2,1)} %get-tuple-element.30.s0), channel_id=1, source_target_pairs={{0,24},{4,28},{8,16},{12,20},{16,8},{20,12},{24,0},{28,4},{1,25},{... | collective-permute-start | bytes 393224 | tf_op jit(solution)/shard_map/ppermute | solution.py:366
  9.8 0.0 collective-permute-done.5.s3
  9.8 1.7 %collective-permute-start = (bf16[256,256]{1,0:T(8,128)(2,1)}, bf16[256,256]{1,0:T(8,128)(2,1)S(1)}, u32[]{:S(2)}, u32[]{:S(2)}) collective-permute-start(bf16[256,256]{1,0:T(8,128)(2,1)} %get-tuple-element.30.s0), channel_id=1, source_target_pairs={{0,8},{4,12},{8,0},{12,4},{16,24},{20,28},{24,16},{28,20},{1,9},{5... | collective-permute-start | bytes 393224 | tf_op jit(solution)/shard_map/ppermute | solution.py:366
  11.5 6.1 %prepare.1 = (bf16[16,256,256]{2,1,0:T(8,128)(2,1)S(1)}, bf16[16,64,1024]{2,1,0:T(8,128)(2,1)S(1)}, bf16[16,512,128]{2,1,0:T(8,128)(2,1)S(1)}, bf16[16,64,1024]{2,1,0:T(8,128)(2,1)S(1)}) custom-call(bf16[256,4096]{1,0:T(8,128)(2,1)} %win_ref.1, bf16[256,4096]{1,0:T(8,128)(2,1)} %wout_ref.1), custom_call_target="tpu_custom_call" | custom-call | flops 2147483648 | bytes 12582912 | tf_op jit(solution)/shard_map/prepare/pallas_call | solution.py:377
  17.6 0.0 collective-permute-done.4.s2
  17.6 1.1 %collective-permute-done.2 = bf16[256,256]{1,0:T(8,128)(2,1)S(1)} collective-permute-done((bf16[256,256]{1,0:T(8,128)(2,1)}, bf16[256,256]{1,0:T(8,128)(2,1)S(1)}, u32[]{:S(2)}, u32[]{:S(2)}) %collective-permute-start.2) | collective-permute-done | bytes 131104 | tf_op jit(solution)/shard_map/ppermute | solution.py:366
  18.7 0.0 collective-permute-done.1
  18.7 1.3 %collective-permute-done = bf16[256,256]{1,0:T(8,128)(2,1)S(1)} collective-permute-done((bf16[256,256]{1,0:T(8,128)(2,1)}, bf16[256,256]{1,0:T(8,128)(2,1)S(1)}, u32[]{:S(2)}, u32[]{:S(2)}) %collective-permute-start) | collective-permute-done | bytes 131104 | tf_op jit(solution)/shard_map/ppermute | solution.py:366
  20.0 1.8 %collective-permute-start.10 = (bf16[768,256]{1,0:T(8,128)(2,1)S(1)}, bf16[768,256]{1,0:T(8,128)(2,1)S(1)}, u32[]{:S(2)}, u32[]{:S(2)}) collective-permute-start(bf16[768,256]{1,0:T(8,128)(2,1)S(1)} %constant_dynamic-update-slice_fusion.z0), channel_id=1, source_target_pairs={{0,2},{1,3},{2,0},{3,1},{4,6},{5,7},{6,4},{7,5},{8,10},{9,11},{10,... | collective-permute-start | bytes 1179656 | tf_op jit(solution)/shard_map/ppermute | solution.py:400
  21.8 0.0 collective-permute-start.9
  21.9 9.4 %local.1 = (bf16[256,256]{1,0:T(8,128)(2,1)S(1)}, bf16[256,256]{1,0:T(8,128)(2,1)S(1)}, bf16[256,256]{1,0:T(8,128)(2,1)S(1)}, bf16[256,256]{1,0:T(8,128)(2,1)S(1...) custom-call(s32[8,256]{1,0:T(8,128)S(1)} %copy-done.1, f32[1,1024]{1,0:T(1,128)S(1)} %bitcast.1, ...), custom_call_target="tpu_custom_call" | custom-call | flops 4294967296 | bytes 10485760 | tf_op jit(solution)/shard_map/local/pallas_call | solution.py:404
  31.3 0.0 collective-permute-done.10.z2
  31.3 0.6 collective-permute-start.11
  31.9 0.1 collective-permute-start.6
  32.0 1.1 %collective-permute-start.7 = (bf16[256,256]{1,0:T(8,128)(2,1)S(1)}, bf16[256,256]{1,0:T(8,128)(2,1)S(1)}, u32[]{:S(2)}, u32[]{:S(2)}) collective-permute-start(bf16[256,256]{1,0:T(8,128)(2,1)S(1)} %get-tuple-element.40), channel_id=1, source_target_pairs={{0,2},{1,3},{2,0},{3,1},{4,6},{5,7},{6,4},{7,5},{8,10},{9,11},{10,... | collective-permute-start | bytes 393224 | tf_op jit(solution)/shard_map/ppermute | solution.py:469
  33.1 0.7 %collective-permute-start.8 = (bf16[256,256]{1,0:T(8,128)(2,1)S(1)}, bf16[256,256]{1,0:T(8,128)(2,1)S(1)}, u32[]{:S(2)}, u32[]{:S(2)}) collective-permute-start(bf16[256,256]{1,0:T(8,128)(2,1)S(1)} %get-tuple-element.41), channel_id=1, source_target_pairs={{0,3},{1,2},{2,1},{3,0},{4,7},{5,6},{6,5},{7,4},{8,11},{9,10},{10,... | collective-permute-start | bytes 393224 | tf_op jit(solution)/shard_map/ppermute | solution.py:469
  33.8 0.0 collective-permute-done.11.z3
  33.8 19.1 %blocks.1 = (bf16[64,32,128]{2,1,0:T(8,128)(2,1)S(1)}, f32[64,32,128]{2,1,0:T(8,128)S(1)}) custom-call(s32[8,256]{1,0:T(8,128)S(1)} %copy-done.1, f32[1,1024]{1,0:T(1,128)S(1)} %bitcast.2, bf16[768,256]{1,0:T(8,128)(2,1)S(1)} %constant_dynamic-update-slice_fusion.z0, bf16[768,256]{1,0:T(8,128)(2,1)S(1)} %collective-permute-done.9.z1, ...), custom_call_target="tpu_custom_call" | custom-call | flops 6442450944 | bytes 6291456 | tf_op jit(solution)/shard_map/blocks/pallas_call | solution.py:438
  52.8 1.6 %collective-permute-start.12 = (bf16[64,32,128]{2,1,0:T(8,128)(2,1)S(1)}, bf16[64,32,128]{2,1,0:T(8,128)(2,1)S(1)}, u32[]{:S(2)}, u32[]{:S(2)}) collective-permute-start(bf16[64,32,128]{2,1,0:T(8,128)(2,1)S(1)} %get-tuple-element.50), channel_id=1, source_target_pairs={{0,4},{4,0},{8,12},{12,8},{16,20},{20,16},{24,28},{28,24},{1,5},{5... | collective-permute-start | bytes 1572872 | tf_op jit(solution)/shard_map/ppermute | solution.py:468
  54.4 0.0 collective-permute-done.6
  54.4 0.0 collective-permute-done.7
  54.4 0.0 collective-permute-done.8
  54.4 0.1 add_convert_fusion
  54.5 0.7 fusion
  55.1 12.2 %collective-permute-done.12 = bf16[64,32,128]{2,1,0:T(8,128)(2,1)S(1)} collective-permute-done((bf16[64,32,128]{2,1,0:T(8,128)(2,1)S(1)}, bf16[64,32,128]{2,1,0:T(8,128)(2,1)S(1)}, u32[]{:S(2)}, u32[]{:S(2)}) %collective-permute-start.12) | collective-permute-done | bytes 524320 | tf_op jit(solution)/shard_map/ppermute | solution.py:468
  67.4 0.2 convert_add_fusion
  67.5 1.2 %broadcast_in_dim_reshape.3 = f32[1,64,4096]{2,1,0:T(8,128)} reshape(f32[64,32,128]{2,1,0:T(8,128)S(1)} %convert_add_fusion) | data formatting | bytes 2097152 | tf_op jit(solution)/shard_map/broadcast_in_dim;reshape | solution.py:473
  (11 shorter events, 0.0 us)
Async XLA Ops:
  2.5 19.4 %copy-start = (bf16[256,256]{1,0:T(8,128)(2,1)S(1)}, bf16[256,256]{1,0:T(8,128)(2,1)}, u32[]{:S(2)}) copy-start(bf16[256,256]{1,0:T(8,128)(2,1)} %get-tuple-element.30.s0) | copy-start | bytes 393220
  2.5 19.4 %copy-start.1 = (s32[8,256]{1,0:T(8,128)S(1)}, s32[8,256]{1,0:T(8,128)}, u32[]{:S(2)}) copy-start(s32[8,256]{1,0:T(8,128)} %get-tuple-element.27.plan) | copy-start | bytes 24580
  2.5 19.4 %copy-start.2 = (f32[1024]{0:T(1024)S(1)}, f32[1024]{0:T(1024)}, u32[]{:S(2)}) copy-start(f32[1024]{0:T(1024)} %param.8) | copy-start | bytes 12292
  2.5 7.3 %collective-permute-start.5 = (bf16[256,256]{1,0:T(8,128)(2,1)}, bf16[256,256]{1,0:T(8,128)(2,1)S(1)}, u32[]{:S(2)}, u32[]{:S(2)}) collective-permute-start(bf16[256,256]{1,0:T(8,128)(2,1)} %get-tuple-element.30.s0), channel_id=1, source_target_pairs={{0,3},{1,2},{2,1},{3,0},{4,7},{5,6},{6,5},{7,4},{8,11},{9,10},{10,... | collective-permute-start | bytes 393224 | tf_op jit(solution)/shard_map/ppermute | solution.py:367
  4.9 12.6 %collective-permute-start.4 = (bf16[256,256]{1,0:T(8,128)(2,1)}, bf16[256,256]{1,0:T(8,128)(2,1)S(1)}, u32[]{:S(2)}, u32[]{:S(2)}) collective-permute-start(bf16[256,256]{1,0:T(8,128)(2,1)} %get-tuple-element.30.s0), channel_id=1, source_target_pairs={{0,2},{1,3},{2,0},{3,1},{4,6},{5,7},{6,4},{7,5},{8,10},{9,11},{10,... | collective-permute-start | bytes 393224 | tf_op jit(solution)/shard_map/ppermute | solution.py:367
  5.6 12.0 %collective-permute-start.3 = (bf16[256,256]{1,0:T(8,128)(2,1)}, bf16[256,256]{1,0:T(8,128)(2,1)S(1)}, u32[]{:S(2)}, u32[]{:S(2)}) collective-permute-start(bf16[256,256]{1,0:T(8,128)(2,1)} %get-tuple-element.30.s0), channel_id=1, source_target_pairs={{0,1},{1,0},{2,3},{3,2},{4,5},{5,4},{6,7},{7,6},{8,9},{9,8},{10,11... | collective-permute-start | bytes 393224 | tf_op jit(solution)/shard_map/ppermute | solution.py:367
  5.6 13.1 %collective-permute-start.2 = (bf16[256,256]{1,0:T(8,128)(2,1)}, bf16[256,256]{1,0:T(8,128)(2,1)S(1)}, u32[]{:S(2)}, u32[]{:S(2)}) collective-permute-start(bf16[256,256]{1,0:T(8,128)(2,1)} %get-tuple-element.30.s0), channel_id=1, source_target_pairs={{0,16},{4,20},{8,24},{12,28},{16,0},{20,4},{24,8},{28,12},{1,17},{... | collective-permute-start | bytes 393224 | tf_op jit(solution)/shard_map/ppermute | solution.py:366
  8.4 10.3 %collective-permute-start.1 = (bf16[256,256]{1,0:T(8,128)(2,1)}, bf16[256,256]{1,0:T(8,128)(2,1)S(1)}, u32[]{:S(2)}, u32[]{:S(2)}) collective-permute-start(bf16[256,256]{1,0:T(8,128)(2,1)} %get-tuple-element.30.s0), channel_id=1, source_target_pairs={{0,24},{4,28},{8,16},{12,20},{16,8},{20,12},{24,0},{28,4},{1,25},{... | collective-permute-start | bytes 393224 | tf_op jit(solution)/shard_map/ppermute | solution.py:366
  9.8 10.2 %collective-permute-start = (bf16[256,256]{1,0:T(8,128)(2,1)}, bf16[256,256]{1,0:T(8,128)(2,1)S(1)}, u32[]{:S(2)}, u32[]{:S(2)}) collective-permute-start(bf16[256,256]{1,0:T(8,128)(2,1)} %get-tuple-element.30.s0), channel_id=1, source_target_pairs={{0,8},{4,12},{8,0},{12,4},{16,24},{20,28},{24,16},{28,20},{1,9},{5... | collective-permute-start | bytes 393224 | tf_op jit(solution)/shard_map/ppermute | solution.py:366
  20.0 11.3 %collective-permute-start.10 = (bf16[768,256]{1,0:T(8,128)(2,1)S(1)}, bf16[768,256]{1,0:T(8,128)(2,1)S(1)}, u32[]{:S(2)}, u32[]{:S(2)}) collective-permute-start(bf16[768,256]{1,0:T(8,128)(2,1)S(1)} %constant_dynamic-update-slice_fusion.z0), channel_id=1, source_target_pairs={{0,2},{1,3},{2,0},{3,1},{4,6},{5,7},{6,4},{7,5},{8,10},{9,11},{10,... | collective-permute-start | bytes 1179656 | tf_op jit(solution)/shard_map/ppermute | solution.py:400
  21.8 11.9 %collective-permute-start.9 = (bf16[768,256]{1,0:T(8,128)(2,1)S(1)}, bf16[768,256]{1,0:T(8,128)(2,1)S(1)}, u32[]{:S(2)}, u32[]{:S(2)}) collective-permute-start(bf16[768,256]{1,0:T(8,128)(2,1)S(1)} %constant_dynamic-update-slice_fusion.z0), channel_id=1, source_target_pairs={{0,1},{1,0},{2,3},{3,2},{4,5},{5,4},{6,7},{7,6},{8,9},{9,8},{10,11... | collective-permute-start | bytes 1179656 | tf_op jit(solution)/shard_map/ppermute | solution.py:399
  31.3 2.4 %collective-permute-start.11 = (bf16[768,256]{1,0:T(8,128)(2,1)S(1)}, bf16[768,256]{1,0:T(8,128)(2,1)S(1)}, u32[]{:S(2)}, u32[]{:S(2)}) collective-permute-start(bf16[768,256]{1,0:T(8,128)(2,1)S(1)} %collective-permute-done.10.z2), channel_id=1, source_target_pairs={{0,1},{1,0},{2,3},{3,2},{4,5},{5,4},{6,7},{7,6},{8,9},{9,8},{10,11... | collective-permute-start | bytes 1179656 | tf_op jit(solution)/shard_map/ppermute | solution.py:436
  31.9 22.5 %collective-permute-start.6 = (bf16[256,256]{1,0:T(8,128)(2,1)S(1)}, bf16[256,256]{1,0:T(8,128)(2,1)S(1)}, u32[]{:S(2)}, u32[]{:S(2)}) collective-permute-start(bf16[256,256]{1,0:T(8,128)(2,1)S(1)} %get-tuple-element.39), channel_id=1, source_target_pairs={{0,1},{1,0},{2,3},{3,2},{4,5},{5,4},{6,7},{7,6},{8,9},{9,8},{10,11... | collective-permute-start | bytes 393224 | tf_op jit(solution)/shard_map/ppermute | solution.py:469
  32.0 22.4 %collective-permute-start.7 = (bf16[256,256]{1,0:T(8,128)(2,1)S(1)}, bf16[256,256]{1,0:T(8,128)(2,1)S(1)}, u32[]{:S(2)}, u32[]{:S(2)}) collective-permute-start(bf16[256,256]{1,0:T(8,128)(2,1)S(1)} %get-tuple-element.40), channel_id=1, source_target_pairs={{0,2},{1,3},{2,0},{3,1},{4,6},{5,7},{6,4},{7,5},{8,10},{9,11},{10,... | collective-permute-start | bytes 393224 | tf_op jit(solution)/shard_map/ppermute | solution.py:469
  33.1 21.3 %collective-permute-start.8 = (bf16[256,256]{1,0:T(8,128)(2,1)S(1)}, bf16[256,256]{1,0:T(8,128)(2,1)S(1)}, u32[]{:S(2)}, u32[]{:S(2)}) collective-permute-start(bf16[256,256]{1,0:T(8,128)(2,1)S(1)} %get-tuple-element.41), channel_id=1, source_target_pairs={{0,3},{1,2},{2,1},{3,0},{4,7},{5,6},{6,5},{7,4},{8,11},{9,10},{10,... | collective-permute-start | bytes 393224 | tf_op jit(solution)/shard_map/ppermute | solution.py:469
  52.8 14.5 %collective-permute-start.12 = (bf16[64,32,128]{2,1,0:T(8,128)(2,1)S(1)}, bf16[64,32,128]{2,1,0:T(8,128)(2,1)S(1)}, u32[]{:S(2)}, u32[]{:S(2)}) collective-permute-start(bf16[64,32,128]{2,1,0:T(8,128)(2,1)S(1)} %get-tuple-element.50), channel_id=1, source_target_pairs={{0,4},{4,0},{8,12},{12,8},{16,20},{20,16},{24,28},{28,24},{1,5},{5... | collective-permute-start | bytes 1572872 | tf_op jit(solution)/shard_map/ppermute | solution.py:468

commit v2 on v1

--- a/solution.py
+++ b/solution.py
@@ -13,7 +13,7 @@
 HALF = BLK // 2
 GROUP = 4
 FIRST = 1024
-BATCH = 16
+BATCH = 12
 
 
 norm_eps = 1e-06
@@ -60,19 +60,23 @@
     return jnp.where(col == target, 1.0, 0.0).astype(BF16)
 
 
-def plan_kernel(cap, col_blocks, row_blocks, cols_ref, slots_ref, x_ref, grad_ref, out_ref, both_ref):
+def stack_kernel(x_ref, grad_ref, both_ref):
+    tok = x_ref.shape[0]
+    both_ref[:tok, :] = x_ref[...]
+    both_ref[tok:, :] = grad_ref[...]
+
+
+def plan_kernel(cap, col_blocks, row_blocks, cols_ref, slots_ref, out_ref):
     kept = cols_ref.shape[1]
     per_row = kept // row_blocks
     me = lax.axis_index("dp")
-    tok = x_ref.shape[0]
-    both_ref[:tok, :] = x_ref[...]
-    both_ref[tok:, :] = grad_ref[...]
     cols, slots = cols_ref[...], slots_ref[...]
     owner = lax.div(slots, jnp.int32(cap))
     own = jnp.where(owner == me, 1.0, 0.0)
     peer = jnp.where(owner == (me ^ 1), 1.0, 0.0)
-    flag = own + peer
-    needed = jnp.max(jnp.where(cols == iota((col_blocks, kept), 0), flag, 0.0), axis=1, keepdims=True)
+    needed = jnp.max(
+        jnp.where(cols == iota((col_blocks, kept), 0), own + peer, 0.0), axis=1, keepdims=True
+    )
 
     def to_column(row):
         size = row.shape[1]
@@ -96,22 +100,27 @@
     cols_c = to_column(cols_r)
     earlier = iota((kept, kept), 1) < iota((kept, kept), 0)
     seen = jnp.max(jnp.where(earlier & (cols_r == cols_c), 1.0, 0.0), axis=1, keepdims=True)
-    flag_c = to_column(flag)
+    peer_c, own_c = to_column(peer), to_column(own)
     pair_end = iota((kept, kept), 0) < 2 * per_row * iota((kept, kept), 1)
+
+    def starts(flags_c):
+        return jnp.sum(jnp.where(pair_end, flags_c, 0.0), axis=0, keepdims=True)
+
     rows = [
         cols_r + FIRST * (1.0 - to_row(seen)),
-        (slots - owner * cap).astype(F32) + cap * own,
-        listed(flag, flag_c),
-        jnp.sum(jnp.where(pair_end, flag_c, 0.0), axis=0, keepdims=True),
+        (slots - owner * cap).astype(F32),
+        listed(peer, peer_c),
+        starts(peer_c),
         listed(to_row(needed), needed),
         jnp.sum(needed, axis=0, keepdims=True),
+        listed(own, own_c),
+        starts(own_c),
     ]
     for index, row in enumerate(rows):
         out_ref[index : index + 1, :] = jnp.broadcast_to(row, (1, kept)).astype(jnp.int32)
-    out_ref[len(rows) :, :] = jnp.zeros((out_ref.shape[0] - len(rows), kept), jnp.int32)
-
-
-def prepare_kernel(win_ref, wout_ref, a_in, b_in, p_out, a_out, order, both):
+
+
+def prepare_kernel(plan_ref, win_ref, wout_ref, a_in, b_in, p_out, a_out, order, both):
     count = a_in.shape[0]
     per_row, length = win_ref.shape[0] // count, win_ref.shape[1]
     lanes = 2 * BLK
@@ -220,33 +229,35 @@
                 acc_a[c] = a
         return carry
 
-    lax.fori_loop(0, row_blocks, step, 0, unroll=4)
+    lax.fori_loop(0, row_blocks, step, 0, unroll=8)
 
 
 def local_kernel(
-    plan, gain_ref, s0, s1, s2, s3, a_in, b_in, p_out, a_out, o0, o1, o2, o3, gp_ref, n_ref,
-    nt_s, gt_s, acc_v, acc_a, act_s, br_s, gn_s
+    plan, gain_ref, s0, s1, s2, s3, a_in, p_out, act_ref, gp_ref, n_ref, nt_s, gt_s, acc_v, acc_a
 ):
-    width = s0.shape[1]
-    tok = s0.shape[0] // 2
-    row_blocks, per_row = a_in.shape[0], p_out.shape[1] // HALF
-    col_blocks = acc_v.shape[0]
-    perm = even_first(width)
+    tok = n_ref.shape[0]
+    perm = even_first(s0.shape[1])
     load_tokens([(ref, 0) for ref in (s0, s1, s2, s3)], tok, gain_ref, perm, n_ref, nt_s, gt_s, 0)
     expand(plan, a_in, p_out, nt_s, gt_s, acc_v, acc_a)
 
     def bend(c, carry):
         value, slope = gelu_both(acc_v[c])
-        act_s[c] = value.astype(BF16)
+        act_ref[c] = value.astype(BF16)
         gp_ref[c] = (acc_a[c] * slope).astype(BF16)
         return carry
 
-    lax.fori_loop(0, col_blocks, bend, 0, unroll=4)
+    lax.fori_loop(0, gp_ref.shape[0], bend, 0, unroll=4)
+
+
+def contract_kernel(plan, act_ref, gp_ref, b_in, a_out, o0, o1, o2, o3, br_s, gn_s):
+    tok, width = o0.shape[0] // 2, o0.shape[1]
+    row_blocks, per_row = b_in.shape[0], b_in.shape[2] // BLK
+    perm = even_first(width)
 
     def contract(r, carry):
         at = pl.ds(pl.multiple_of(r * BLK, BLK), BLK)
         ids = [plan[0, r * per_row + k] & (FIRST - 1) for k in range(per_row)]
-        acts = [act_s[c, a * HALF : (a + 1) * HALF, :] for a in (0, 1) for c in ids]
+        acts = [act_ref[c, a * HALF : (a + 1) * HALF, :] for a in (0, 1) for c in ids]
         br_s[at, :] = dot(a_out[r], jnp.concatenate(acts, axis=0)).astype(BF16)
         grads = [gp_ref[c] for c in ids]
         gn_s[at, :] = dot(b_in[r], jnp.concatenate(grads, axis=0)).astype(BF16)
@@ -260,47 +271,51 @@
         out[tok:, :] = dot(gn_s[at, :].T, perm, ((1,), (1,))).astype(BF16)
 
 
+def chunk_kernel(
+    plan, gain_ref, s0, s1, s2, s3, a_in, p_out, gp_ref, n_ref, nt_s, gt_s, acc_v, acc_a
+):
+    chunks = gp_ref.shape[0]
+    tok = n_ref.shape[0] // chunks
+    perm = even_first(s0.shape[1])
+    count = plan[5, 0]
+    for j in range(chunks):
+        pieces = [(ref, 2 * tok * j) for ref in (s0, s1, s2, s3)]
+        load_tokens(pieces, tok, gain_ref, perm, n_ref, nt_s, gt_s, j * tok)
+        expand(plan, a_in, p_out, nt_s, gt_s, acc_v, acc_a)
+
+        def bend(i, carry):
+            for u in range(GROUP):
+                c = plan[4, jnp.minimum(i * GROUP + u, count - 1)]
+                _, slope = gelu_both(acc_v[c])
+                gp_ref[j, c] = (acc_a[c] * slope).astype(BF16)
+            return carry
+
+        lax.fori_loop(0, (count + GROUP - 1) // GROUP, bend, 0)
+
+
 def block_kernel(
-    scale, plan, gain_ref, z0, z1, z2, z3, a_in, p_out, gp_own, n_own, peer_ref, own_ref,
-    n_s, nt_s, gt_s, acc_v, acc_a, gp_s, found
+    list_row, scale, plan, gp0, gp1, gp2, n0, n1, n2, p_out, out_ref, found
 ):
-    tok = n_own.shape[0]
     per_row = p_out.shape[1] // HALF
     lanes = 2 * BLK
-    perm = even_first(z0.shape[1])
-    n_s[:tok, :] = n_own[...]
-
-    def keep(i, carry):
-        c = plan[4, i]
-        gp_s[c, :, :tok] = gp_own[c]
-        return carry
-
-    lax.fori_loop(0, plan[5, 0], keep, 0)
-    for j in range(z0.shape[0] // (2 * tok)):
-        pieces = [(ref, 2 * tok * j) for ref in (z0, z1, z2, z3)]
-        load_tokens(pieces, tok, gain_ref, perm, n_s, nt_s, gt_s, (j + 1) * tok)
-        expand(plan, a_in, p_out, nt_s, gt_s, acc_v, acc_a)
-
-        def bend(i, carry):
-            c = plan[4, i]
-            _, slope = gelu_both(acc_v[c])
-            gp_s[c, :, (j + 1) * tok : (j + 2) * tok] = (acc_a[c] * slope).astype(BF16)
-            return carry
-
-        lax.fori_loop(0, plan[5, 0], bend, 0)
-
+    pairs = p_out.shape[0] // 2
+    cap = out_ref.shape[0]
     left = iota((HALF, lanes), 1) < BLK
-    cap = own_ref.shape[0]
     found[...] = jnp.zeros_like(found)
 
     def form(pair, first):
-        end = plan[3, pair + 1]
+        end = plan[list_row + 1, pair + 1]
         at_lane = pl.ds(pl.multiple_of(pair * lanes, lanes), lanes)
         ids = [
-            plan[2, jnp.maximum(jnp.minimum(first + u, end - 1), 0)] for u in range(BATCH)
+            plan[list_row, jnp.maximum(jnp.minimum(first + u, end - 1), 0)] for u in range(BATCH)
         ]
-        grads = jnp.concatenate([gp_s[plan[0, k] & (FIRST - 1)] for k in ids], axis=0)
-        blocks = dot(grads, n_s[:, at_lane]) * scale
+        grads = []
+        for k in ids:
+            c = plan[0, k] & (FIRST - 1)
+            chunks = [gp0[c]] + [ref[j, c] for ref in (gp1, gp2) for j in range(ref.shape[0])]
+            grads.append(jnp.concatenate(chunks, axis=1))
+        normed = jnp.concatenate([ref[:, at_lane] for ref in (n0, n1, n2)], axis=0)
+        blocks = dot(jnp.concatenate(grads, axis=0), normed) * scale
         done = []
         for u, k in enumerate(ids):
             odd = (lax.div(k, jnp.int32(per_row)) & 1) == 1
@@ -308,29 +323,46 @@
             low = blocks[u * BLK + HALF : (u + 1) * BLK]
             top = jnp.where(odd, pltpu.roll(top, BLK, 1), top)
             low = jnp.where(odd, low, pltpu.roll(low, BLK, 1))
-            slot = jnp.where(first < end, plan[1, k], 2 * cap)
+            slot = jnp.where(first < end, plan[1, k], cap)
             done.append((slot, jnp.where(left, top, low)))
         for slot, value in done:
             found[slot] = value
 
-    pairs = p_out.shape[0] // 2
-
     def begin(pair, carry):
-        form(pair, plan[3, pair])
+        form(pair, plan[list_row + 1, pair])
         return carry
 
-    lax.fori_loop(0, pairs, begin, 0, unroll=2)
+    lax.fori_loop(0, pairs, begin, 0, unroll=8)
 
     def finish(pair, carry):
-        @pl.when(plan[3, pair + 1] - plan[3, pair] > BATCH)
-        def _():
-            form(pair, plan[3, pair] + BATCH)
-
-        return carry
+        begin, end = plan[list_row + 1, pair], plan[list_row + 1, pair + 1]
+
+        def more(i, carry):
+            form(pair, begin + i * BATCH)
+            return carry
+
+        return lax.fori_loop(1, (end - begin + BATCH - 1) // BATCH, more, carry)
 
     lax.fori_loop(0, pairs, finish, 0)
-    peer_ref[...] = found[:cap].astype(peer_ref.dtype)
-    own_ref[...] = found[cap : 2 * cap]
+    out_ref[...] = found[:cap].astype(out_ref.dtype)
+
+
+def finish_kernel(own_ref, arrived_ref, s0, s1, s2, s3, branch_ref, normed_ref, out_ref):
+    lanes = own_ref.shape[2]
+    rows = 8
+    for first in range(0, own_ref.shape[0], rows):
+        at = slice(first, first + rows)
+        blocks = own_ref[at] + arrived_ref[at].astype(F32)
+        turned = jnp.swapaxes(blocks, 0, 1)
+        for j in range(turned.shape[0]):
+            out_ref[at, j * lanes : (j + 1) * lanes] = turned[j]
+
+    @pl.when(pl.program_id(0) == 0)
+    def _():
+        tok = branch_ref.shape[0]
+        for out, base in ((branch_ref, 0), (normed_ref, tok)):
+            total = sum(ref[base : base + tok, :].astype(F32) for ref in (s0, s1, s2, s3))
+            out[...] = total.astype(BF16)
 
 
 def fast_body(x_in, gain, w_in, w_out, grad_out, block_cols, slots):
@@ -353,18 +385,24 @@
     whole = pl.BlockSpec(memory_space=pltpu.VMEM)
     mm = 2 * tok * kept * BLK * BLK
 
-    plan, own = pl.pallas_call(
+    own = pl.pallas_call(
+        stack_kernel,
+        out_shape=jax.ShapeDtypeStruct((2 * tok, width), BF16),
+        cost_estimate=pl.CostEstimate(flops=0, bytes_accessed=8 * tok * width, transcendentals=0),
+        name="stack",
+    )(x_in, grad_out)
+    pieces = [lax.ppermute(own, "dp", along_z[0])]
+    gathered = [own] + [lax.ppermute(own, "mp", near[q]) for q in range(1, mp_count)]
+    gathered[1], own_late = lax.optimization_barrier((gathered[1], own))
+    pieces += [lax.ppermute(own_late, "dp", hop) for hop in along_z[1:]]
+    pieces[0], cols_late, slots_late = lax.optimization_barrier((pieces[0], block_cols, slots))
+    plan = pl.pallas_call(
         functools.partial(plan_kernel, cap, col_blocks, row_blocks),
-        out_shape=[
-            jax.ShapeDtypeStruct((8, kept), jnp.int32),
-            jax.ShapeDtypeStruct((2 * tok, width), BF16),
-        ],
+        out_shape=jax.ShapeDtypeStruct((8, kept), jnp.int32),
         cost_estimate=pl.CostEstimate(flops=4_000_000, bytes_accessed=16384, transcendentals=0),
         name="plan",
-    )(block_cols, slots, x_in, grad_out)
-
-    pieces = [lax.ppermute(own, "dp", hop) for hop in along_z]
-    gathered = [own] + [lax.ppermute(own, "mp", near[q]) for q in range(1, mp_count)]
+    )(cols_late, slots_late)
+    near_piece = [pieces[0]] + [lax.ppermute(pieces[0], "mp", near[q]) for q in (1, 2)]
     gain_row = gain.reshape(1, feat)
 
     step = min(4, row_blocks)
@@ -378,7 +416,8 @@
         prepare_kernel,
         out_shape=[jax.ShapeDtypeStruct((row_blocks, *shape), BF16) for shape in shapes],
         grid=(row_blocks // step,),
-        in_specs=[pl.BlockSpec((step * per_row, BLK * BLK), lambda r: (r, 0))] * 2,
+        in_specs=[pl.BlockSpec(memory_space=pltpu.SMEM)]
+        + [pl.BlockSpec((step * per_row, BLK * BLK), lambda r: (r, 0))] * 2,
         out_specs=[pl.BlockSpec((step, *shape), lambda r: (r, 0, 0)) for shape in shapes],
         scratch_shapes=[
             pltpu.VMEM((per_row * HALF, per_row * HALF), BF16),
@@ -390,86 +429,100 @@
         ),
         name="prepare",
     )(
+        plan,
         pltpu.with_memory_space_constraint(w_in, pltpu.HBM),
         pltpu.with_memory_space_constraint(w_out, pltpu.HBM),
     )
 
-    pieces, gathered, p_out = lax.optimization_barrier((pieces, gathered, p_out))
-    column = jnp.concatenate(pieces, axis=0)
-    column_c = lax.ppermute(column, "mp", near[1])
-    column_y = lax.ppermute(column, "mp", near[2])
+    late, near_piece, gathered, p_out = lax.optimization_barrier(
+        (pieces[1:], near_piece, gathered, p_out)
+    )
+    column = jnp.concatenate(late, axis=0)
+    far_pieces = [column] + [lax.ppermute(column, "mp", near[q]) for q in (1, 2)]
+    near_piece.append(lax.ppermute(near_piece[2], "mp", near[1]))
 
     hidden_f32 = pltpu.VMEM((col_blocks, BLK, tok), F32)
     turned = pltpu.VMEM((feat, tok), BF16)
-    *parts, gp_own, n_own = pl.pallas_call(
-        local_kernel,
-        out_shape=[jax.ShapeDtypeStruct((2 * tok, width), BF16)] * mp_count
-        + [
-            jax.ShapeDtypeStruct((col_blocks, BLK, tok), BF16),
-            jax.ShapeDtypeStruct((tok, feat), BF16),
+
+    def hidden_bf16(*chunks):
+        return jax.ShapeDtypeStruct((*chunks, col_blocks, BLK, tok), BF16)
+
+    def flat(chunks):
+        return jax.ShapeDtypeStruct((chunks * tok, feat), BF16)
+
+    def call(kernel, out_shape, scratch, limit, flops, transcendentals, *args):
+        return pl.pallas_call(
+            kernel,
+            out_shape=out_shape,
+            grid_spec=pltpu.PrefetchScalarGridSpec(
+                num_scalar_prefetch=1,
+                grid=(),
+                in_specs=[whole] * (len(args) - 1),
+                out_specs=[whole] * len(out_shape),
+                scratch_shapes=scratch,
+            ),
+            compiler_params=pltpu.CompilerParams(vmem_limit_bytes=limit * MIB),
+            cost_estimate=pl.CostEstimate(
+                flops=flops, bytes_accessed=flops // (4 * tok), transcendentals=transcendentals
+            ),
+            name=(kernel.func if isinstance(kernel, functools.partial) else kernel).__name__,
+        )(*args)
+
+    scratch = [turned, turned, hidden_f32, hidden_f32]
+    act, gp_own, n_own = call(
+        local_kernel, [hidden_bf16(), hidden_bf16(), flat(1)], scratch, 32, 8 * mm, tok * hidden,
+        plan, gain_row, *gathered, a_in, p_out,
+    )
+    far_pieces[2], n_own = lax.optimization_barrier((far_pieces[2], n_own))
+    far_pieces.append(lax.ppermute(far_pieces[2], "mp", near[1]))
+    gp_near, n_near = call(
+        chunk_kernel, [hidden_bf16(1), flat(1)], scratch, 32, 8 * mm, tok * hidden // 2,
+        plan, gain_row, *near_piece, a_in, p_out,
+    )
+    gp_far, n_far = call(
+        chunk_kernel, [hidden_bf16(z_count - 2), flat(z_count - 2)], scratch, 32, 16 * mm, tok * hidden,
+        plan, gain_row, *far_pieces, a_in, p_out,
+    )
+
+    def blocks(list_row, dtype, flops, plan):
+        return call(
+            functools.partial(block_kernel, list_row, scale),
+            [jax.ShapeDtypeStruct((cap, HALF, lanes), dtype)],
+            [pltpu.VMEM((cap + 1, HALF, lanes), F32)],
+            16, flops, 0,
+            plan, gp_own, gp_near, gp_far, n_own, n_near, n_far, p_out,
+        )[0]
+
+    for_peer = blocks(2, BF16, 2 * mm, plan)
+    for_peer, plan_later, act = lax.optimization_barrier((for_peer, plan, act))
+    arrived = lax.ppermute(for_peer, "dp", across_x)
+    parts = call(
+        contract_kernel,
+        [jax.ShapeDtypeStruct((2 * tok, width), BF16)] * mp_count,
+        [turned, turned],
+        16, 0, 0,
+        plan_later, act, gp_own, b_in, a_out,
+    )
+    for_own = blocks(6, F32, 0, plan_later)
+    summed = [parts[0]] + [lax.ppermute(parts[q], "mp", near[q]) for q in range(1, mp_count)]
+    steps = 4
+    own_rows = pl.BlockSpec((cap // steps, HALF, lanes), lambda i: (i, 0, 0))
+    token_rows = pl.BlockSpec((2 * tok, width), lambda i: (0, 0))
+    result = pl.BlockSpec((tok, width), lambda i: (0, 0))
+    branch, grad_normed, owned_grad = pl.pallas_call(
+        finish_kernel,
+        out_shape=[
+            jax.ShapeDtypeStruct((tok, width), BF16),
+            jax.ShapeDtypeStruct((tok, width), BF16),
+            jax.ShapeDtypeStruct((cap, BLK * BLK), F32),
         ],
-        grid_spec=pltpu.PrefetchScalarGridSpec(
-            num_scalar_prefetch=1,
-            grid=(),
-            in_specs=[whole] * 9,
-            out_specs=[whole] * (mp_count + 2),
-            scratch_shapes=[
-                turned,
-                turned,
-                hidden_f32,
-                hidden_f32,
-                pltpu.VMEM((col_blocks, BLK, tok), BF16),
-                turned,
-                turned,
-            ],
-        ),
-        compiler_params=pltpu.CompilerParams(vmem_limit_bytes=32 * MIB),
-        cost_estimate=pl.CostEstimate(
-            flops=16 * mm,
-            bytes_accessed=10 * kept * BLK * BLK,
-            transcendentals=tok * hidden,
-        ),
-        name="local",
-    )(plan, gain_row, *gathered, a_in, b_in, p_out, a_out)
-
-    column_y, n_own = lax.optimization_barrier((column_y, n_own))
-    columns = [column, column_c, column_y, lax.ppermute(column_y, "mp", near[1])]
-    rows = tok * z_count
-    for_peer, for_own = pl.pallas_call(
-        functools.partial(block_kernel, scale),
-        out_shape=[
-            jax.ShapeDtypeStruct((cap, HALF, lanes), BF16),
-            jax.ShapeDtypeStruct((cap, HALF, lanes), F32),
-        ],
-        grid_spec=pltpu.PrefetchScalarGridSpec(
-            num_scalar_prefetch=1,
-            grid=(),
-            in_specs=[whole] * 9,
-            out_specs=[whole] * 2,
-            scratch_shapes=[
-                pltpu.VMEM((rows, feat), BF16),
-                turned,
-                turned,
-                hidden_f32,
-                hidden_f32,
-                pltpu.VMEM((col_blocks, BLK, rows), BF16),
-                pltpu.VMEM((2 * cap + 1, HALF, lanes), F32),
-            ],
-        ),
-        compiler_params=pltpu.CompilerParams(vmem_limit_bytes=40 * MIB),
-        cost_estimate=pl.CostEstimate(
-            flops=24 * mm,
-            bytes_accessed=6 * kept * BLK * BLK,
-            transcendentals=tok * hidden,
-        ),
-        name="blocks",
-    )(plan, gain_row, *columns, a_in, p_out, gp_own, n_own)
-
-    arrived = lax.ppermute(for_peer, "dp", across_x)
-    summed = [parts[0]] + [lax.ppermute(parts[q], "mp", near[q]) for q in range(1, mp_count)]
-    total = sum(part.astype(F32) for part in summed)
-    branch, grad_normed = total[:tok].astype(BF16), total[tok:].astype(BF16)
-    owned_grad = (for_own + arrived.astype(F32)).reshape(cap, BLK * BLK)
+        grid=(steps,),
+        in_specs=[own_rows] * 2 + [token_rows] * mp_count,
+        out_specs=[result, result, pl.BlockSpec((cap // steps, BLK * BLK), lambda i: (i, 0))],
+        compiler_params=pltpu.CompilerParams(vmem_limit_bytes=16 * MIB),
+        cost_estimate=pl.CostEstimate(flops=0, bytes_accessed=0, transcendentals=0),
+        name="finish",
+    )(for_own, arrived, *summed)
     return (branch, grad_normed, owned_grad[None])
 
 

time: 68.9 us -> 64.5 us (0.936)
  waiting for transfers between devices: 14.6 us -> 7.72 us
  Pallas kernels: 36.4 us -> 40.4 us
  local copies, waits for them, and re-layouts: 1.86 us -> 0.73 us
    ppermute x1, waiting for transfers between devices: 12.2 us -> 2.18 us  [fast_body(): arrived = lax.ppermute(for_peer, 'dp', across_x)]
    pallas_call x2 -> x8, Pallas kernels: 28.5 us -> 32.6 us  [the longest x6 29.3 us: call(): pl.pallas_call(kernel, out_shape=out_shape, grid_spec=pltpu.PrefetchScala...]
    ppermute x3, waiting for transfers between devices: 0.01 us -> 2.86 us  [fast_body(): lax.ppermute(parts[q], 'mp', near[q])]
    another operation x1 -> x0, local copies, waits for them, and re-layouts: 1.16 us -> none  [fast_body(): return (branch, grad_normed, owned_grad[None])]
    ppermute x3, starting transfers between devices: 3.15 us -> 2.03 us  [fast_body(): lax.ppermute(own, 'mp', near[q])]
    ppermute x6 -> x9, starting transfers between devices: 8.24 us -> 8.97 us  [the longest x2 2.62 us: fast_body(): pieces += [lax.ppermute(own_late, 'dp', hop) for hop in along_z[1:]]]
    ppermute x6 -> x9, waiting for transfers between devices: 2.38 us -> 2.33 us  [the longest x2 2.14 us: fast_body(): pieces += [lax.ppermute(own_late, 'dp', hop) for hop in along_z[1:]]]
  transfers between devices with their start and end apart: 13 -> 16, of which waited for: 3 -> 6; matrix products, arithmetic and copies ran while one was open for 1% -> 0% of each run, Pallas kernels for 50% -> 39%
where the time goes in v2:
time: 64.5 us; the launch traced here: 64.4 us
  Pallas kernels  40.4 us (63%)
  starting transfers between devices  14.7 us (23%)
  waiting for transfers between devices  7.72 us (12%)
  between operations  0.77 us (1%)
  local copies, waits for them, and re-layouts  0.73 us (1%)
    pallas_call x6, Pallas kernels, call(): pl.pallas_call(kernel, out_shape=out_shape, grid_spec=pltpu.PrefetchScala...  29.3 us
    pallas_call x1, Pallas kernels, fast_body(): pl.pallas_call(prepare_kernel, out_shape=[jax.ShapeDtypeStruct((row_block...  6.13 us
    ppermute x3, waiting for transfers between devices, fast_body(): lax.ppermute(parts[q], 'mp', near[q])  2.86 us
    ppermute x2, starting transfers between devices, fast_body(): pieces += [lax.ppermute(own_late, 'dp', hop) for hop in along_z[1:]]  2.62 us
    ppermute x1, starting transfers between devices, fast_body(): pieces = [lax.ppermute(own, 'dp', along_z[0])]  2.57 us
    ppermute x1, waiting for transfers between devices, fast_body(): arrived = lax.ppermute(for_peer, 'dp', across_x)  2.18 us
    ppermute x3, starting transfers between devices, fast_body(): lax.ppermute(parts[q], 'mp', near[q])  2.18 us
    ppermute x2, waiting for transfers between devices, fast_body(): pieces += [lax.ppermute(own_late, 'dp', hop) for hop in along_z[1:]]  2.14 us
  transfers between devices with their start and end apart: 16, of which 6 were waited for; matrix products, arithmetic and copies ran while one was open for 0% of the time, Pallas kernels for 39%

profile of v2, /device:TPU:0, one launch (start us, length us, event | category | flops | bytes accessed | tf_op | source)
XLA Modules:
  0.0 64.4 jit_solution(10471888660354396939)
XLA Ops:
  0.6 1.5 %stack.1.s0 = bf16[256,256]{1,0:T(8,128)(2,1)} custom-call(bf16[128,256]{1,0:T(8,128)(2,1)} %x_ref.1, bf16[128,256]{1,0:T(8,128)(2,1)} %grad_ref.1), custom_call_target="tpu_custom_call" | custom-call | bytes 262144 | tf_op jit(solution)/shard_map/stack/pallas_call | solution.py:388
  2.2 0.5 collective-permute-start.1
  2.6 2.6 %collective-permute-start = (bf16[256,256]{1,0:T(8,128)(2,1)}, bf16[256,256]{1,0:T(8,128)(2,1)S(1)}, u32[]{:S(2)}, u32[]{:S(2)}) collective-permute-start(bf16[256,256]{1,0:T(8,128)(2,1)} %stack.1.s0), channel_id=1, source_target_pairs={{0,8},{4,12},{8,0},{12,4},{16,24},{20,28},{24,16},{28,20},{1,9},{5... | collective-permute-start | bytes 393224 | tf_op jit(solution)/shard_map/ppermute | solution.py:394
  5.2 1.5 %collective-permute-start.6 = (bf16[256,256]{1,0:T(8,128)(2,1)}, bf16[256,256]{1,0:T(8,128)(2,1)S(1)}, u32[]{:S(2)}, u32[]{:S(2)}) collective-permute-start(bf16[256,256]{1,0:T(8,128)(2,1)} %stack.1.s0), channel_id=1, source_target_pairs={{0,2},{1,3},{2,0},{3,1},{4,6},{5,7},{6,4},{7,5},{8,10},{9,11},{10,... | collective-permute-start | bytes 393224 | tf_op jit(solution)/shard_map/ppermute | solution.py:395
  6.7 0.1 collective-permute-start.7
  6.8 2.5 %collective-permute-start.2 = (bf16[256,256]{1,0:T(8,128)(2,1)}, bf16[256,256]{1,0:T(8,128)(2,1)S(1)}, u32[]{:S(2)}, u32[]{:S(2)}) collective-permute-start(bf16[256,256]{1,0:T(8,128)(2,1)} %stack.1.s0), channel_id=1, source_target_pairs={{0,24},{4,28},{8,16},{12,20},{16,8},{20,12},{24,0},{28,4},{1,25},{... | collective-permute-start | bytes 393224 | tf_op jit(solution)/shard_map/ppermute | solution.py:397
  9.3 0.1 collective-permute-start.3
  9.4 0.2 collective-permute-done.s0
  9.6 0.1 collective-permute-start.4
  9.7 1.7 %plan.1.plan_ref = s32[8,256]{1,0:T(8,128)} custom-call(s32[1,256]{1,0:T(1,128)} %cols_ref, s32[1,256]{1,0:T(1,128)} %slots_ref), custom_call_target="tpu_custom_call" | custom-call | flops 4000000 | bytes 16384 | tf_op jit(solution)/shard_map/plan/pallas_call | solution.py:399
  11.4 0.3 collective-permute-done.6.s2
  11.7 1.5 %collective-permute-start.5 = (bf16[256,256]{1,0:T(8,128)(2,1)S(1)}, bf16[256,256]{1,0:T(8,128)(2,1)S(1)}, u32[]{:S(2)}, u32[]{:S(2)}) collective-permute-start(bf16[256,256]{1,0:T(8,128)(2,1)S(1)} %collective-permute-done.s0), channel_id=1, source_target_pairs={{0,2},{1,3},{2,0},{3,1},{4,6},{5,7},{6,4},{7,5},{8,10},{9,11},{10,... | collective-permute-start | bytes 393224 | tf_op jit(solution)/shard_map/ppermute | solution.py:405
  13.3 0.7 %copy-done.1 = s32[8,256]{1,0:T(8,128)S(1)} copy-done((s32[8,256]{1,0:T(8,128)S(1)}, s32[8,256]{1,0:T(8,128)}, u32[]{:S(2)}) %copy-start.1) | copy-done | bytes 8216
  14.0 6.1 %prepare.1 = (bf16[16,256,256]{2,1,0:T(8,128)(2,1)S(1)}, bf16[16,64,1024]{2,1,0:T(8,128)(2,1)S(1)}, bf16[16,512,128]{2,1,0:T(8,128)(2,1)S(1)}, bf16[16,64,1024]{2,1,0:T(8,128)(2,1)S(1)}) custom-call(s32[8,256]{1,0:T(8,128)S(1)} %copy-done.1, bf16[256,4096]{1,0:T(8,128)(2,1)} %win_ref.1, bf16[256,4096]{1,0:T(8,128)(2,1)} %wout_ref.1), custom_call_target="tpu_custom_call" | custom-call | flops 2147483648 | bytes 12582912 | tf_op jit(solution)/shard_map/prepare/pallas_call | solution.py:415
  20.1 2.1 %collective-permute-done.3 = bf16[256,256]{1,0:T(8,128)(2,1)S(1)} collective-permute-done((bf16[256,256]{1,0:T(8,128)(2,1)}, bf16[256,256]{1,0:T(8,128)(2,1)S(1)}, u32[]{:S(2)}, u32[]{:S(2)}) %collective-permute-start.3) | collective-permute-done | bytes 131104 | tf_op jit(solution)/shard_map/ppermute | solution.py:397
  22.3 1.6 %collective-permute-start.10 = (bf16[512,256]{1,0:T(8,128)(2,1)S(1)}, bf16[512,256]{1,0:T(8,128)(2,1)S(1)}, u32[]{:S(2)}, u32[]{:S(2)}) collective-permute-start(bf16[512,256]{1,0:T(8,128)(2,1)S(1)} %constant_dynamic-update-slice_fusion.s0), channel_id=1, source_target_pairs={{0,2},{1,3},{2,0},{3,1},{4,6},{5,7},{6,4},{7,5},{8,10},{9,11},{10,... | collective-permute-start | bytes 786440 | tf_op jit(solution)/shard_map/ppermute | solution.py:441
  23.9 0.5 collective-permute-start.8
  24.4 6.6 %local_kernel.1 = (bf16[128,64,128]{2,1,0:T(8,128)(2,1)S(1)}, bf16[128,64,128]{2,1,0:T(8,128)(2,1)S(1)}, bf16[128,1024]{1,0:T(8,128)(2,1)S(1)}) custom-call(s32[8,256]{1,0:T(8,128)S(1)} %copy-done.2, f32[1,1024]{1,0:T(1,128)S(1)} %bitcast.2, bf16[256,256]{1,0:T(8,128)(2,1)S(1)} %copy-done, bf16[256,256]{1,0:T(8,128)(2,1)S(1)} %collective-permute-done.1.s1, ...), custom_call_target="tpu_custom_call" | custom-call | flops 2147483648 | bytes 4194304 | tf_op jit(solution)/shard_map/local_kernel/pallas_call | solution.py:454
  31.1 0.1 collective-permute-start.11
  31.1 4.6 %chunk_kernel.2 = (bf16[1,128,64,128]{3,2,1,0:T(8,128)(2,1)S(1)}, bf16[128,1024]{1,0:T(8,128)(2,1)S(1)}) custom-call(s32[8,256]{1,0:T(8,128)S(1)} %copy-done.2, f32[1,1024]{1,0:T(1,128)S(1)} %bitcast.3, bf16[256,256]{1,0:T(8,128)(2,1)S(1)} %collective-permute-done.s0, bf16[256,256]{1,0:T(8,128)(2,1)S(1)} %collective-permute-done.4.s1, ...), custom_call_target="tpu_custom_call" | custom-call | flops 2147483648 | bytes 4194304 | tf_op jit(solution)/shard_map/chunk_kernel/pallas_call | solution.py:454
  35.8 8.9 %chunk_kernel.3 = (bf16[2,128,64,128]{3,2,1,0:T(8,128)(2,1)S(1)}, bf16[256,1024]{1,0:T(8,128)(2,1)S(1)}) custom-call(s32[8,256]{1,0:T(8,128)S(1)} %copy-done.2, f32[1,1024]{1,0:T(1,128)S(1)} %bitcast.4, bf16[512,256]{1,0:T(8,128)(2,1)S(1)} %constant_dynamic-update-slice_fusion.s0, bf16[512,256]{1,0:T(8,128)(2,1)S(1)} %collective-permute-done.9.s1, ...), custom_call_target="tpu_custom_call" | custom-call | flops 4294967296 | bytes 8388608 | tf_op jit(solution)/shard_map/chunk_kernel/pallas_call | solution.py:454
  44.7 3.1 %block_kernel.2 = bf16[64,32,128]{2,1,0:T(8,128)(2,1)S(1)} custom-call(s32[8,256]{1,0:T(8,128)S(1)} %copy-done.2, bf16[128,64,128]{2,1,0:T(8,128)(2,1)S(1)} %get-tuple-element.53.gp0.gp_ref, bf16[1,128,64,128]{3,2,1,0:T(8,128)(2,1)S(1)} %get-tuple-element.57.gp1, bf16[2,128,64,128]{3,2,1,0:T(8,128)(2,1)S(1)} %get-tuple-element.62.gp2, ...), custom_call_target="tpu_custom_call" | custom-call | flops 536870912 | bytes 1048576 | tf_op jit(solution)/shard_map/block_kernel/pallas_call | solution.py:454
  47.8 1.6 %collective-permute-start.12 = (bf16[64,32,128]{2,1,0:T(8,128)(2,1)S(1)}, bf16[64,32,128]{2,1,0:T(8,128)(2,1)S(1)}, u32[]{:S(2)}, u32[]{:S(2)}) collective-permute-start(bf16[64,32,128]{2,1,0:T(8,128)(2,1)S(1)} %block_kernel.2), channel_id=1, source_target_pairs={{0,4},{4,0},{8,12},{12,8},{16,20},{20,16},{24,28},{28,24},{1,5},{5... | collective-permute-start | bytes 1572872 | tf_op jit(solution)/shard_map/ppermute | solution.py:498
  49.4 3.0 %contract_kernel.1 = (bf16[256,256]{1,0:T(8,128)(2,1)S(1)}, bf16[256,256]{1,0:T(8,128)(2,1)S(1)}, bf16[256,256]{1,0:T(8,128)(2,1)S(1)}, bf16[256,256]{1,0:T(8,128)(2,1)S(1)}) custom-call(s32[8,256]{1,0:T(8,128)S(1)} %copy-done.2, bf16[128,64,128]{2,1,0:T(8,128)(2,1)S(1)} %get-tuple-element.69.act_ref, ...), custom_call_target="tpu_custom_call" | custom-call | tf_op jit(solution)/shard_map/contract_kernel/pallas_call | solution.py:454
  52.3 0.8 %collective-permute-start.13 = (bf16[256,256]{1,0:T(8,128)(2,1)S(1)}, bf16[256,256]{1,0:T(8,128)(2,1)S(1)}, u32[]{:S(2)}, u32[]{:S(2)}) collective-permute-start(bf16[256,256]{1,0:T(8,128)(2,1)S(1)} %get-tuple-element.73), channel_id=1, source_target_pairs={{0,1},{1,0},{2,3},{3,2},{4,5},{5,4},{6,7},{7,6},{8,9},{9,8},{10,11... | collective-permute-start | bytes 393224 | tf_op jit(solution)/shard_map/ppermute | solution.py:507
  53.1 1.2 %collective-permute-start.14 = (bf16[256,256]{1,0:T(8,128)(2,1)S(1)}, bf16[256,256]{1,0:T(8,128)(2,1)S(1)}, u32[]{:S(2)}, u32[]{:S(2)}) collective-permute-start(bf16[256,256]{1,0:T(8,128)(2,1)S(1)} %get-tuple-element.74), channel_id=1, source_target_pairs={{0,2},{1,3},{2,0},{3,1},{4,6},{5,7},{6,4},{7,5},{8,10},{9,11},{10,... | collective-permute-start | bytes 393224 | tf_op jit(solution)/shard_map/ppermute | solution.py:507
  54.3 0.2 collective-permute-start.15
  54.5 3.1 %block_kernel.3.own_ref = f32[64,32,128]{2,1,0:T(8,128)S(1)} custom-call(s32[8,256]{1,0:T(8,128)S(1)} %copy-done.2, bf16[128,64,128]{2,1,0:T(8,128)(2,1)S(1)} %get-tuple-element.53.gp0.gp_ref, bf16[1,128,64,128]{3,2,1,0:T(8,128)(2,1)S(1)} %get-tuple-element.57.gp1, bf16[2,128,64,128]{3,2,1,0:T(8,128)(2,1)S(1)} %get-tuple-element.62.gp2, ...), custom_call_target="tpu_custom_call" | custom-call | tf_op jit(solution)/shard_map/block_kernel/pallas_call | solution.py:454
  57.6 1.8 %collective-permute-done.14.s2 = bf16[256,256]{1,0:T(8,128)(2,1)S(1)} collective-permute-done((bf16[256,256]{1,0:T(8,128)(2,1)S(1)}, bf16[256,256]{1,0:T(8,128)(2,1)S(1)}, u32[]{:S(2)}, u32[]{:S(2)}) %collective-permute-start.14) | collective-permute-done | bytes 131104 | tf_op jit(solution)/shard_map/ppermute | solution.py:507
  59.4 1.1 %collective-permute-done.15.s3 = bf16[256,256]{1,0:T(8,128)(2,1)S(1)} collective-permute-done((bf16[256,256]{1,0:T(8,128)(2,1)S(1)}, bf16[256,256]{1,0:T(8,128)(2,1)S(1)}, u32[]{:S(2)}, u32[]{:S(2)}) %collective-permute-start.15) | collective-permute-done | bytes 131104 | tf_op jit(solution)/shard_map/ppermute | solution.py:507
  60.5 2.2 %collective-permute-done.12.arrived_ref = bf16[64,32,128]{2,1,0:T(8,128)(2,1)S(1)} collective-permute-done((bf16[64,32,128]{2,1,0:T(8,128)(2,1)S(1)}, bf16[64,32,128]{2,1,0:T(8,128)(2,1)S(1)}, u32[]{:S(2)}, u32[]{:S(2)}) %collective-permute-start.12) | collective-permute-done | bytes 524320 | tf_op jit(solution)/shard_map/ppermute | solution.py:498
  62.7 1.7 %finish.1 = (bf16[128,256]{1,0:T(8,128)(2,1)}, bf16[128,256]{1,0:T(8,128)(2,1)}, f32[64,4096]{1,0:T(8,128)}) custom-call(f32[64,32,128]{2,1,0:T(8,128)S(1)} %block_kernel.3.own_ref, bf16[64,32,128]{2,1,0:T(8,128)(2,1)S(1)} %collective-permute-done.12.arrived_ref, bf16[256,256]{1,0:T(8,128)(2,1)S(1)} %get-tuple-element.72.s0, ...), custom_call_target="tpu_custom_call" | custom-call | tf_op jit(solution)/shard_map/finish/pallas_call | solution.py:512
  (20 shorter events, 0.1 us)
Async XLA Ops:
  2.2 4.6 %collective-permute-start.1 = (bf16[256,256]{1,0:T(8,128)(2,1)}, bf16[256,256]{1,0:T(8,128)(2,1)S(1)}, u32[]{:S(2)}, u32[]{:S(2)}) collective-permute-start(bf16[256,256]{1,0:T(8,128)(2,1)} %stack.1.s0), channel_id=1, source_target_pairs={{0,1},{1,0},{2,3},{3,2},{4,5},{5,4},{6,7},{7,6},{8,9},{9,8},{10,11... | collective-permute-start | bytes 393224 | tf_op jit(solution)/shard_map/ppermute | solution.py:395
  2.6 7.0 %collective-permute-start = (bf16[256,256]{1,0:T(8,128)(2,1)}, bf16[256,256]{1,0:T(8,128)(2,1)S(1)}, u32[]{:S(2)}, u32[]{:S(2)}) collective-permute-start(bf16[256,256]{1,0:T(8,128)(2,1)} %stack.1.s0), channel_id=1, source_target_pairs={{0,8},{4,12},{8,0},{12,4},{16,24},{20,28},{24,16},{28,20},{1,9},{5... | collective-permute-start | bytes 393224 | tf_op jit(solution)/shard_map/ppermute | solution.py:394
  5.2 6.5 %collective-permute-start.6 = (bf16[256,256]{1,0:T(8,128)(2,1)}, bf16[256,256]{1,0:T(8,128)(2,1)S(1)}, u32[]{:S(2)}, u32[]{:S(2)}) collective-permute-start(bf16[256,256]{1,0:T(8,128)(2,1)} %stack.1.s0), channel_id=1, source_target_pairs={{0,2},{1,3},{2,0},{3,1},{4,6},{5,7},{6,4},{7,5},{8,10},{9,11},{10,... | collective-permute-start | bytes 393224 | tf_op jit(solution)/shard_map/ppermute | solution.py:395
  6.7 13.4 %collective-permute-start.7 = (bf16[256,256]{1,0:T(8,128)(2,1)}, bf16[256,256]{1,0:T(8,128)(2,1)S(1)}, u32[]{:S(2)}, u32[]{:S(2)}) collective-permute-start(bf16[256,256]{1,0:T(8,128)(2,1)} %stack.1.s0), channel_id=1, source_target_pairs={{0,3},{1,2},{2,1},{3,0},{4,7},{5,6},{6,5},{7,4},{8,11},{9,10},{10,... | collective-permute-start | bytes 393224 | tf_op jit(solution)/shard_map/ppermute | solution.py:395
  6.8 13.3 %collective-permute-start.2 = (bf16[256,256]{1,0:T(8,128)(2,1)}, bf16[256,256]{1,0:T(8,128)(2,1)S(1)}, u32[]{:S(2)}, u32[]{:S(2)}) collective-permute-start(bf16[256,256]{1,0:T(8,128)(2,1)} %stack.1.s0), channel_id=1, source_target_pairs={{0,24},{4,28},{8,16},{12,20},{16,8},{20,12},{24,0},{28,4},{1,25},{... | collective-permute-start | bytes 393224 | tf_op jit(solution)/shard_map/ppermute | solution.py:397
  9.3 13.0 %collective-permute-start.3 = (bf16[256,256]{1,0:T(8,128)(2,1)}, bf16[256,256]{1,0:T(8,128)(2,1)S(1)}, u32[]{:S(2)}, u32[]{:S(2)}) collective-permute-start(bf16[256,256]{1,0:T(8,128)(2,1)} %stack.1.s0), channel_id=1, source_target_pairs={{0,16},{4,20},{8,24},{12,28},{16,0},{20,4},{24,8},{28,12},{1,17},{... | collective-permute-start | bytes 393224 | tf_op jit(solution)/shard_map/ppermute | solution.py:397
  9.6 12.7 %collective-permute-start.4 = (bf16[256,256]{1,0:T(8,128)(2,1)S(1)}, bf16[256,256]{1,0:T(8,128)(2,1)S(1)}, u32[]{:S(2)}, u32[]{:S(2)}) collective-permute-start(bf16[256,256]{1,0:T(8,128)(2,1)S(1)} %collective-permute-done.s0), channel_id=1, source_target_pairs={{0,1},{1,0},{2,3},{3,2},{4,5},{5,4},{6,7},{7,6},{8,9},{9,8},{10,11... | collective-permute-start | bytes 393224 | tf_op jit(solution)/shard_map/ppermute | solution.py:405
  9.7 14.7 %copy-start.3 = (f32[1024]{0:T(1024)S(1)}, f32[1024]{0:T(1024)}, u32[]{:S(2)}) copy-start(f32[1024]{0:T(1024)} %param.8) | copy-start | bytes 12292
  11.4 13.0 %copy-start = (bf16[256,256]{1,0:T(8,128)(2,1)S(1)}, bf16[256,256]{1,0:T(8,128)(2,1)}, u32[]{:S(2)}) copy-start(bf16[256,256]{1,0:T(8,128)(2,1)} %stack.1.s0) | copy-start | bytes 393220
  11.7 10.5 %collective-permute-start.5 = (bf16[256,256]{1,0:T(8,128)(2,1)S(1)}, bf16[256,256]{1,0:T(8,128)(2,1)S(1)}, u32[]{:S(2)}, u32[]{:S(2)}) collective-permute-start(bf16[256,256]{1,0:T(8,128)(2,1)S(1)} %collective-permute-done.s0), channel_id=1, source_target_pairs={{0,2},{1,3},{2,0},{3,1},{4,6},{5,7},{6,4},{7,5},{8,10},{9,11},{10,... | collective-permute-start | bytes 393224 | tf_op jit(solution)/shard_map/ppermute | solution.py:405
  13.3 0.7 %copy-start.1 = (s32[8,256]{1,0:T(8,128)S(1)}, s32[8,256]{1,0:T(8,128)}, u32[]{:S(2)}) copy-start(s32[8,256]{1,0:T(8,128)} %plan.1.plan_ref) | copy-start | bytes 24580
  14.0 10.4 %copy-start.2 = (s32[8,256]{1,0:T(8,128)S(1)}, s32[8,256]{1,0:T(8,128)}, u32[]{:S(2)}) copy-start(s32[8,256]{1,0:T(8,128)} %plan.1.plan_ref) | copy-start | bytes 24580
  22.3 8.8 %collective-permute-start.10 = (bf16[512,256]{1,0:T(8,128)(2,1)S(1)}, bf16[512,256]{1,0:T(8,128)(2,1)S(1)}, u32[]{:S(2)}, u32[]{:S(2)}) collective-permute-start(bf16[512,256]{1,0:T(8,128)(2,1)S(1)} %constant_dynamic-update-slice_fusion.s0), channel_id=1, source_target_pairs={{0,2},{1,3},{2,0},{3,1},{4,6},{5,7},{6,4},{7,5},{8,10},{9,11},{10,... | collective-permute-start | bytes 786440 | tf_op jit(solution)/shard_map/ppermute | solution.py:441
  23.9 11.9 %collective-permute-start.9 = (bf16[512,256]{1,0:T(8,128)(2,1)S(1)}, bf16[512,256]{1,0:T(8,128)(2,1)S(1)}, u32[]{:S(2)}, u32[]{:S(2)}) collective-permute-start(bf16[512,256]{1,0:T(8,128)(2,1)S(1)} %constant_dynamic-update-slice_fusion.s0), channel_id=1, source_target_pairs={{0,1},{1,0},{2,3},{3,2},{4,5},{5,4},{6,7},{7,6},{8,9},{9,8},{10,11... | collective-permute-start | bytes 786440 | tf_op jit(solution)/shard_map/ppermute | solution.py:441
  23.9 7.3 %collective-permute-start.8 = (bf16[256,256]{1,0:T(8,128)(2,1)S(1)}, bf16[256,256]{1,0:T(8,128)(2,1)S(1)}, u32[]{:S(2)}, u32[]{:S(2)}) collective-permute-start(bf16[256,256]{1,0:T(8,128)(2,1)S(1)} %collective-permute-done.5.s2), channel_id=1, source_target_pairs={{0,1},{1,0},{2,3},{3,2},{4,5},{5,4},{6,7},{7,6},{8,9},{9,8},{10,11... | collective-permute-start | bytes 393224 | tf_op jit(solution)/shard_map/ppermute | solution.py:442
  31.1 4.7 %collective-permute-start.11 = (bf16[512,256]{1,0:T(8,128)(2,1)S(1)}, bf16[512,256]{1,0:T(8,128)(2,1)S(1)}, u32[]{:S(2)}, u32[]{:S(2)}) collective-permute-start(bf16[512,256]{1,0:T(8,128)(2,1)S(1)} %collective-permute-done.10.s2), channel_id=1, source_target_pairs={{0,1},{1,0},{2,3},{3,2},{4,5},{5,4},{6,7},{7,6},{8,9},{9,8},{10,11... | collective-permute-start | bytes 786440 | tf_op jit(solution)/shard_map/ppermute | solution.py:477
  47.8 14.9 %collective-permute-start.12 = (bf16[64,32,128]{2,1,0:T(8,128)(2,1)S(1)}, bf16[64,32,128]{2,1,0:T(8,128)(2,1)S(1)}, u32[]{:S(2)}, u32[]{:S(2)}) collective-permute-start(bf16[64,32,128]{2,1,0:T(8,128)(2,1)S(1)} %block_kernel.2), channel_id=1, source_target_pairs={{0,4},{4,0},{8,12},{12,8},{16,20},{20,16},{24,28},{28,24},{1,5},{5... | collective-permute-start | bytes 1572872 | tf_op jit(solution)/shard_map/ppermute | solution.py:498
  52.3 5.3 %collective-permute-start.13 = (bf16[256,256]{1,0:T(8,128)(2,1)S(1)}, bf16[256,256]{1,0:T(8,128)(2,1)S(1)}, u32[]{:S(2)}, u32[]{:S(2)}) collective-permute-start(bf16[256,256]{1,0:T(8,128)(2,1)S(1)} %get-tuple-element.73), channel_id=1, source_target_pairs={{0,1},{1,0},{2,3},{3,2},{4,5},{5,4},{6,7},{7,6},{8,9},{9,8},{10,11... | collective-permute-start | bytes 393224 | tf_op jit(solution)/shard_map/ppermute | solution.py:507
  53.1 6.4 %collective-permute-start.14 = (bf16[256,256]{1,0:T(8,128)(2,1)S(1)}, bf16[256,256]{1,0:T(8,128)(2,1)S(1)}, u32[]{:S(2)}, u32[]{:S(2)}) collective-permute-start(bf16[256,256]{1,0:T(8,128)(2,1)S(1)} %get-tuple-element.74), channel_id=1, source_target_pairs={{0,2},{1,3},{2,0},{3,1},{4,6},{5,7},{6,4},{7,5},{8,10},{9,11},{10,... | collective-permute-start | bytes 393224 | tf_op jit(solution)/shard_map/ppermute | solution.py:507
  54.3 6.2 %collective-permute-start.15 = (bf16[256,256]{1,0:T(8,128)(2,1)S(1)}, bf16[256,256]{1,0:T(8,128)(2,1)S(1)}, u32[]{:S(2)}, u32[]{:S(2)}) collective-permute-start(bf16[256,256]{1,0:T(8,128)(2,1)S(1)} %get-tuple-element.75), channel_id=1, source_target_pairs={{0,3},{1,2},{2,1},{3,0},{4,7},{5,6},{6,5},{7,4},{8,11},{9,10},{10,... | collective-permute-start | bytes 393224 | tf_op jit(solution)/shard_map/ppermute | solution.py:507

commit v3 on v2

--- a/solution.py
+++ b/solution.py
@@ -14,6 +14,7 @@
 GROUP = 4
 FIRST = 1024
 BATCH = 12
+BEND = 8
 
 
 norm_eps = 1e-06
@@ -152,6 +153,7 @@
 
     ordered_in, ordered_out = by_block(win_ref), by_block(wout_ref)
     left = iota((HALF, lanes), 1) < BLK
+    left2 = iota((BLK, lanes), 1) < BLK
     for n in range(count):
         of_n = slice(n * lanes, (n + 1) * lanes)
         kept_in = dot(ordered_in[:, of_n], both[...])
@@ -165,9 +167,15 @@
             b_in[n, HALF:, at] = jnp.where(left, first[:, lanes:], second[:, :lanes]).astype(BF16)
         for quad in range(per_row // GROUP):
             rows_of = slice(quad * lanes, (quad + 1) * lanes)
-            turned = kept_in[rows_of, :lanes].astype(BF16).T
-            a_in[n, quad * BLK : (quad + 1) * BLK, :lanes] = turned[:BLK]
-            a_in[n, quad * BLK : (quad + 1) * BLK, lanes:] = turned[BLK:]
+            straight, swapped = kept_in[rows_of, :lanes], kept_in[rows_of, lanes:]
+            pairs = jnp.concatenate(
+                [
+                    jnp.where(left2, straight[:BLK], swapped[BLK:]),
+                    jnp.where(left2, swapped[:BLK], straight[BLK:]),
+                ],
+                axis=0,
+            )
+            a_in[n, rows_of, :] = pairs.astype(BF16).T
             turned = kept_out[rows_of].T
             a_out[n, :, rows_of] = turned[:BLK]
             a_out[n, :, rows + quad * lanes : rows + (quad + 1) * lanes] = turned[BLK:]
@@ -203,10 +211,8 @@
         spread = []
         for a in (0, 1):
             part = normed[a * HALF : (a + 1) * HALF]
-            for u in range(GROUP):
-                spread.append(
-                    jnp.concatenate([part if v == u else gap for v in range(GROUP)], axis=1)
-                )
+            spread.append(jnp.concatenate([part, gap], axis=1))
+            spread.append(jnp.concatenate([gap, part], axis=1))
         terms_v = dot(a_in[r], jnp.concatenate(spread, axis=0))
         cots = jnp.concatenate(
             [jnp.concatenate([cot, gap2], axis=1), jnp.concatenate([gap2, cot], axis=1)], axis=0
@@ -218,7 +224,8 @@
                 k = quad * GROUP + u
                 code = plan[0, r * per_row + k]
                 c, first = code & (FIRST - 1), code >= FIRST
-                v = terms_v[quad * BLK : (quad + 1) * BLK, u * tok : (u + 1) * tok]
+                rows = terms_v[(k // 2) * BLK : (k // 2 + 1) * BLK]
+                v = rows[:, (k % 2) * tok : (k % 2 + 1) * tok]
                 rows = terms_a[k * HALF : (k + 1) * HALF]
                 a = jnp.concatenate([rows[:, :tok], rows[:, tok:]], axis=0)
                 v = jnp.where(first, v, acc_v[c] + v)
@@ -229,7 +236,7 @@
                 acc_a[c] = a
         return carry
 
-    lax.fori_loop(0, row_blocks, step, 0, unroll=8)
+    lax.fori_loop(0, row_blocks, step, 0, unroll=16)
 
 
 def local_kernel(
@@ -263,7 +270,7 @@
         gn_s[at, :] = dot(b_in[r], jnp.concatenate(grads, axis=0)).astype(BF16)
         return carry
 
-    lax.fori_loop(0, row_blocks, contract, 0, unroll=4)
+    lax.fori_loop(0, row_blocks, contract, 0, unroll=8)
     mine = lax.axis_index("mp")
     for q, out in enumerate((o0, o1, o2, o3)):
         at = pl.ds(pl.multiple_of((mine ^ q) * width, width), width)
@@ -284,13 +291,13 @@
         expand(plan, a_in, p_out, nt_s, gt_s, acc_v, acc_a)
 
         def bend(i, carry):
-            for u in range(GROUP):
-                c = plan[4, jnp.minimum(i * GROUP + u, count - 1)]
+            for u in range(BEND):
+                c = plan[4, jnp.minimum(i * BEND + u, count - 1)]
                 _, slope = gelu_both(acc_v[c])
                 gp_ref[j, c] = (acc_a[c] * slope).astype(BF16)
             return carry
 
-        lax.fori_loop(0, (count + GROUP - 1) // GROUP, bend, 0)
+        lax.fori_loop(0, (count + BEND - 1) // BEND, bend, 0)
 
 
 def block_kernel(
@@ -407,7 +414,7 @@
 
     step = min(4, row_blocks)
     shapes = [
-        (per_row // GROUP * BLK, 2 * lanes),
+        (per_row // 2 * BLK, lanes),
         (BLK, per_row * BLK),
         (per_row * HALF, lanes),
         (BLK, per_row * BLK),

time: 64.5 us -> 62.4 us (0.967)
  Pallas kernels: 40.4 us -> 38.5 us
    pallas_call x6, Pallas kernels: 29.3 us -> 27.4 us  [call(): pl.pallas_call(kernel, out_shape=out_shape, grid_spec=pltpu.PrefetchScala...]
  transfers between devices with their start and end apart: 16 -> 16, of which waited for: 6 -> 7; matrix products, arithmetic and copies ran while one was open for 0% -> 0% of each run, Pallas kernels for 39% -> 38%
where the time goes in v3:
time: 62.4 us
  Pallas kernels  38.5 us (62%)
  starting transfers between devices  15.1 us (24%)
  waiting for transfers between devices  7.27 us (12%)
  between operations  0.76 us (1%)
  local copies, waits for them, and re-layouts  0.73 us (1%)
    pallas_call x6, Pallas kernels, call(): pl.pallas_call(kernel, out_shape=out_shape, grid_spec=pltpu.PrefetchScala...  27.4 us
    pallas_call x1, Pallas kernels, fast_body(): pl.pallas_call(prepare_kernel, out_shape=[jax.ShapeDtypeStruct((row_block...  6.14 us
    ppermute x3, waiting for transfers between devices, fast_body(): lax.ppermute(parts[q], 'mp', near[q])  2.86 us
    ppermute x3, starting transfers between devices, fast_body(): lax.ppermute(parts[q], 'mp', near[q])  2.62 us
    ppermute x2, starting transfers between devices, fast_body(): pieces += [lax.ppermute(own_late, 'dp', hop) for hop in along_z[1:]]  2.62 us
    ppermute x1, starting transfers between devices, fast_body(): pieces = [lax.ppermute(own, 'dp', along_z[0])]  2.57 us
    ppermute x2, waiting for transfers between devices, fast_body(): pieces += [lax.ppermute(own_late, 'dp', hop) for hop in along_z[1:]]  2.13 us
    ppermute x3, starting transfers between devices, fast_body(): lax.ppermute(own, 'mp', near[q])  2.03 us
  transfers between devices with their start and end apart: 16, of which 7 were waited for; matrix products, arithmetic and copies ran while one was open for 0% of the time, Pallas kernels for 38%

profile of v3, /device:TPU:0, one launch (start us, length us, event | category | flops | bytes accessed | tf_op | source)
XLA Modules:
  0.0 62.4 jit_solution(16676120284584092806)
XLA Ops:
  0.6 1.5 %stack.1.s0 = bf16[256,256]{1,0:T(8,128)(2,1)} custom-call(bf16[128,256]{1,0:T(8,128)(2,1)} %x_ref.1, bf16[128,256]{1,0:T(8,128)(2,1)} %grad_ref.1), custom_call_target="tpu_custom_call" | custom-call | bytes 262144 | tf_op jit(solution)/shard_map/stack/pallas_call | solution.py:395
  2.2 0.5 collective-permute-start.1
  2.6 2.6 %collective-permute-start = (bf16[256,256]{1,0:T(8,128)(2,1)}, bf16[256,256]{1,0:T(8,128)(2,1)S(1)}, u32[]{:S(2)}, u32[]{:S(2)}) collective-permute-start(bf16[256,256]{1,0:T(8,128)(2,1)} %stack.1.s0), channel_id=1, source_target_pairs={{0,8},{4,12},{8,0},{12,4},{16,24},{20,28},{24,16},{28,20},{1,9},{5... | collective-permute-start | bytes 393224 | tf_op jit(solution)/shard_map/ppermute | solution.py:401
  5.2 1.5 %collective-permute-start.6 = (bf16[256,256]{1,0:T(8,128)(2,1)}, bf16[256,256]{1,0:T(8,128)(2,1)S(1)}, u32[]{:S(2)}, u32[]{:S(2)}) collective-permute-start(bf16[256,256]{1,0:T(8,128)(2,1)} %stack.1.s0), channel_id=1, source_target_pairs={{0,2},{1,3},{2,0},{3,1},{4,6},{5,7},{6,4},{7,5},{8,10},{9,11},{10,... | collective-permute-start | bytes 393224 | tf_op jit(solution)/shard_map/ppermute | solution.py:402
  6.7 0.1 collective-permute-start.7
  6.8 2.5 %collective-permute-start.2 = (bf16[256,256]{1,0:T(8,128)(2,1)}, bf16[256,256]{1,0:T(8,128)(2,1)S(1)}, u32[]{:S(2)}, u32[]{:S(2)}) collective-permute-start(bf16[256,256]{1,0:T(8,128)(2,1)} %stack.1.s0), channel_id=1, source_target_pairs={{0,24},{4,28},{8,16},{12,20},{16,8},{20,12},{24,0},{28,4},{1,25},{... | collective-permute-start | bytes 393224 | tf_op jit(solution)/shard_map/ppermute | solution.py:404
  9.3 0.1 collective-permute-start.3
  9.4 0.2 collective-permute-done.s0
  9.6 0.1 collective-permute-start.4
  9.7 1.7 %plan.1.plan_ref = s32[8,256]{1,0:T(8,128)} custom-call(s32[1,256]{1,0:T(1,128)} %cols_ref, s32[1,256]{1,0:T(1,128)} %slots_ref), custom_call_target="tpu_custom_call" | custom-call | flops 4000000 | bytes 16384 | tf_op jit(solution)/shard_map/plan/pallas_call | solution.py:406
  11.4 0.3 collective-permute-done.6.s2
  11.7 1.5 %collective-permute-start.5 = (bf16[256,256]{1,0:T(8,128)(2,1)S(1)}, bf16[256,256]{1,0:T(8,128)(2,1)S(1)}, u32[]{:S(2)}, u32[]{:S(2)}) collective-permute-start(bf16[256,256]{1,0:T(8,128)(2,1)S(1)} %collective-permute-done.s0), channel_id=1, source_target_pairs={{0,2},{1,3},{2,0},{3,1},{4,6},{5,7},{6,4},{7,5},{8,10},{9,11},{10,... | collective-permute-start | bytes 393224 | tf_op jit(solution)/shard_map/ppermute | solution.py:412
  13.3 0.7 %copy-done.1 = s32[8,256]{1,0:T(8,128)S(1)} copy-done((s32[8,256]{1,0:T(8,128)S(1)}, s32[8,256]{1,0:T(8,128)}, u32[]{:S(2)}) %copy-start.1) | copy-done | bytes 8216
  14.0 6.1 %prepare.1 = (bf16[16,512,128]{2,1,0:T(8,128)(2,1)S(1)}, bf16[16,64,1024]{2,1,0:T(8,128)(2,1)S(1)}, bf16[16,512,128]{2,1,0:T(8,128)(2,1)S(1)}, bf16[16,64,1024]{2,1,0:T(8,128)(2,1)S(1)}) custom-call(s32[8,256]{1,0:T(8,128)S(1)} %copy-done.1, bf16[256,4096]{1,0:T(8,128)(2,1)} %win_ref.1, bf16[256,4096]{1,0:T(8,128)(2,1)} %wout_ref.1), custom_call_target="tpu_custom_call" | custom-call | flops 2147483648 | bytes 12582912 | tf_op jit(solution)/shard_map/prepare/pallas_call | solution.py:422
  20.1 2.1 %collective-permute-done.3 = bf16[256,256]{1,0:T(8,128)(2,1)S(1)} collective-permute-done((bf16[256,256]{1,0:T(8,128)(2,1)}, bf16[256,256]{1,0:T(8,128)(2,1)S(1)}, u32[]{:S(2)}, u32[]{:S(2)}) %collective-permute-start.3) | collective-permute-done | bytes 131104 | tf_op jit(solution)/shard_map/ppermute | solution.py:404
  22.3 1.6 %collective-permute-start.10 = (bf16[512,256]{1,0:T(8,128)(2,1)S(1)}, bf16[512,256]{1,0:T(8,128)(2,1)S(1)}, u32[]{:S(2)}, u32[]{:S(2)}) collective-permute-start(bf16[512,256]{1,0:T(8,128)(2,1)S(1)} %constant_dynamic-update-slice_fusion.s0), channel_id=1, source_target_pairs={{0,2},{1,3},{2,0},{3,1},{4,6},{5,7},{6,4},{7,5},{8,10},{9,11},{10,... | collective-permute-start | bytes 786440 | tf_op jit(solution)/shard_map/ppermute | solution.py:448
  23.9 0.5 collective-permute-start.8
  24.4 6.1 %local_kernel.1 = (bf16[128,64,128]{2,1,0:T(8,128)(2,1)S(1)}, bf16[128,64,128]{2,1,0:T(8,128)(2,1)S(1)}, bf16[128,1024]{1,0:T(8,128)(2,1)S(1)}) custom-call(s32[8,256]{1,0:T(8,128)S(1)} %copy-done.2, f32[1,1024]{1,0:T(1,128)S(1)} %bitcast.2, bf16[256,256]{1,0:T(8,128)(2,1)S(1)} %copy-done, bf16[256,256]{1,0:T(8,128)(2,1)S(1)} %collective-permute-done.1.s1, ...), custom_call_target="tpu_custom_call" | custom-call | flops 2147483648 | bytes 4194304 | tf_op jit(solution)/shard_map/local_kernel/pallas_call | solution.py:461
  30.5 0.1 collective-permute-done.10.s2
  30.6 4.3 %chunk_kernel.2 = (bf16[1,128,64,128]{3,2,1,0:T(8,128)(2,1)S(1)}, bf16[128,1024]{1,0:T(8,128)(2,1)S(1)}) custom-call(s32[8,256]{1,0:T(8,128)S(1)} %copy-done.2, f32[1,1024]{1,0:T(1,128)S(1)} %bitcast.3, bf16[256,256]{1,0:T(8,128)(2,1)S(1)} %collective-permute-done.s0, bf16[256,256]{1,0:T(8,128)(2,1)S(1)} %collective-permute-done.4.s1, ...), custom_call_target="tpu_custom_call" | custom-call | flops 2147483648 | bytes 4194304 | tf_op jit(solution)/shard_map/chunk_kernel/pallas_call | solution.py:461
  34.9 8.1 %chunk_kernel.3 = (bf16[2,128,64,128]{3,2,1,0:T(8,128)(2,1)S(1)}, bf16[256,1024]{1,0:T(8,128)(2,1)S(1)}) custom-call(s32[8,256]{1,0:T(8,128)S(1)} %copy-done.2, f32[1,1024]{1,0:T(1,128)S(1)} %bitcast.4, bf16[512,256]{1,0:T(8,128)(2,1)S(1)} %constant_dynamic-update-slice_fusion.s0, bf16[512,256]{1,0:T(8,128)(2,1)S(1)} %collective-permute-done.9.s1, ...), custom_call_target="tpu_custom_call" | custom-call | flops 4294967296 | bytes 8388608 | tf_op jit(solution)/shard_map/chunk_kernel/pallas_call | solution.py:461
  43.0 3.1 %block_kernel.2 = bf16[64,32,128]{2,1,0:T(8,128)(2,1)S(1)} custom-call(s32[8,256]{1,0:T(8,128)S(1)} %copy-done.2, bf16[128,64,128]{2,1,0:T(8,128)(2,1)S(1)} %get-tuple-element.53.gp0.gp_ref, bf16[1,128,64,128]{3,2,1,0:T(8,128)(2,1)S(1)} %get-tuple-element.57.gp1, bf16[2,128,64,128]{3,2,1,0:T(8,128)(2,1)S(1)} %get-tuple-element.62.gp2, ...), custom_call_target="tpu_custom_call" | custom-call | flops 536870912 | bytes 1048576 | tf_op jit(solution)/shard_map/block_kernel/pallas_call | solution.py:461
  46.1 1.6 %collective-permute-start.12 = (bf16[64,32,128]{2,1,0:T(8,128)(2,1)S(1)}, bf16[64,32,128]{2,1,0:T(8,128)(2,1)S(1)}, u32[]{:S(2)}, u32[]{:S(2)}) collective-permute-start(bf16[64,32,128]{2,1,0:T(8,128)(2,1)S(1)} %block_kernel.2), channel_id=1, source_target_pairs={{0,4},{4,0},{8,12},{12,8},{16,20},{20,16},{24,28},{28,24},{1,5},{5... | collective-permute-start | bytes 1572872 | tf_op jit(solution)/shard_map/ppermute | solution.py:505
  47.7 2.7 %contract_kernel.1 = (bf16[256,256]{1,0:T(8,128)(2,1)S(1)}, bf16[256,256]{1,0:T(8,128)(2,1)S(1)}, bf16[256,256]{1,0:T(8,128)(2,1)S(1)}, bf16[256,256]{1,0:T(8,128)(2,1)S(1)}) custom-call(s32[8,256]{1,0:T(8,128)S(1)} %copy-done.2, bf16[128,64,128]{2,1,0:T(8,128)(2,1)S(1)} %get-tuple-element.69.act_ref, ...), custom_call_target="tpu_custom_call" | custom-call | tf_op jit(solution)/shard_map/contract_kernel/pallas_call | solution.py:461
  50.4 1.2 %collective-permute-start.13 = (bf16[256,256]{1,0:T(8,128)(2,1)S(1)}, bf16[256,256]{1,0:T(8,128)(2,1)S(1)}, u32[]{:S(2)}, u32[]{:S(2)}) collective-permute-start(bf16[256,256]{1,0:T(8,128)(2,1)S(1)} %get-tuple-element.73), channel_id=1, source_target_pairs={{0,1},{1,0},{2,3},{3,2},{4,5},{5,4},{6,7},{7,6},{8,9},{9,8},{10,11... | collective-permute-start | bytes 393224 | tf_op jit(solution)/shard_map/ppermute | solution.py:514
  51.6 0.6 collective-permute-start.14
  52.2 0.8 %collective-permute-start.15 = (bf16[256,256]{1,0:T(8,128)(2,1)S(1)}, bf16[256,256]{1,0:T(8,128)(2,1)S(1)}, u32[]{:S(2)}, u32[]{:S(2)}) collective-permute-start(bf16[256,256]{1,0:T(8,128)(2,1)S(1)} %get-tuple-element.75), channel_id=1, source_target_pairs={{0,3},{1,2},{2,1},{3,0},{4,7},{5,6},{6,5},{7,4},{8,11},{9,10},{10,... | collective-permute-start | bytes 393224 | tf_op jit(solution)/shard_map/ppermute | solution.py:514
  53.0 3.1 %block_kernel.3.own_ref = f32[64,32,128]{2,1,0:T(8,128)S(1)} custom-call(s32[8,256]{1,0:T(8,128)S(1)} %copy-done.2, bf16[128,64,128]{2,1,0:T(8,128)(2,1)S(1)} %get-tuple-element.53.gp0.gp_ref, bf16[1,128,64,128]{3,2,1,0:T(8,128)(2,1)S(1)} %get-tuple-element.57.gp1, bf16[2,128,64,128]{3,2,1,0:T(8,128)(2,1)S(1)} %get-tuple-element.62.gp2, ...), custom_call_target="tpu_custom_call" | custom-call | tf_op jit(solution)/shard_map/block_kernel/pallas_call | solution.py:461
  56.1 1.8 %collective-permute-done.14.s2 = bf16[256,256]{1,0:T(8,128)(2,1)S(1)} collective-permute-done((bf16[256,256]{1,0:T(8,128)(2,1)S(1)}, bf16[256,256]{1,0:T(8,128)(2,1)S(1)}, u32[]{:S(2)}, u32[]{:S(2)}) %collective-permute-start.14) | collective-permute-done | bytes 131104 | tf_op jit(solution)/shard_map/ppermute | solution.py:514
  57.9 1.1 %collective-permute-done.15.s3 = bf16[256,256]{1,0:T(8,128)(2,1)S(1)} collective-permute-done((bf16[256,256]{1,0:T(8,128)(2,1)S(1)}, bf16[256,256]{1,0:T(8,128)(2,1)S(1)}, u32[]{:S(2)}, u32[]{:S(2)}) %collective-permute-start.15) | collective-permute-done | bytes 131104 | tf_op jit(solution)/shard_map/ppermute | solution.py:514
  59.0 1.7 %collective-permute-done.12.arrived_ref = bf16[64,32,128]{2,1,0:T(8,128)(2,1)S(1)} collective-permute-done((bf16[64,32,128]{2,1,0:T(8,128)(2,1)S(1)}, bf16[64,32,128]{2,1,0:T(8,128)(2,1)S(1)}, u32[]{:S(2)}, u32[]{:S(2)}) %collective-permute-start.12) | collective-permute-done | bytes 524320 | tf_op jit(solution)/shard_map/ppermute | solution.py:505
  60.6 1.7 %finish.1 = (bf16[128,256]{1,0:T(8,128)(2,1)}, bf16[128,256]{1,0:T(8,128)(2,1)}, f32[64,4096]{1,0:T(8,128)}) custom-call(f32[64,32,128]{2,1,0:T(8,128)S(1)} %block_kernel.3.own_ref, bf16[64,32,128]{2,1,0:T(8,128)(2,1)S(1)} %collective-permute-done.12.arrived_ref, bf16[256,256]{1,0:T(8,128)(2,1)S(1)} %get-tuple-element.72.s0, ...), custom_call_target="tpu_custom_call" | custom-call | tf_op jit(solution)/shard_map/finish/pallas_call | solution.py:519
  (20 shorter events, 0.1 us)
Async XLA Ops:
  2.2 4.6 %collective-permute-start.1 = (bf16[256,256]{1,0:T(8,128)(2,1)}, bf16[256,256]{1,0:T(8,128)(2,1)S(1)}, u32[]{:S(2)}, u32[]{:S(2)}) collective-permute-start(bf16[256,256]{1,0:T(8,128)(2,1)} %stack.1.s0), channel_id=1, source_target_pairs={{0,1},{1,0},{2,3},{3,2},{4,5},{5,4},{6,7},{7,6},{8,9},{9,8},{10,11... | collective-permute-start | bytes 393224 | tf_op jit(solution)/shard_map/ppermute | solution.py:402
  2.6 7.0 %collective-permute-start = (bf16[256,256]{1,0:T(8,128)(2,1)}, bf16[256,256]{1,0:T(8,128)(2,1)S(1)}, u32[]{:S(2)}, u32[]{:S(2)}) collective-permute-start(bf16[256,256]{1,0:T(8,128)(2,1)} %stack.1.s0), channel_id=1, source_target_pairs={{0,8},{4,12},{8,0},{12,4},{16,24},{20,28},{24,16},{28,20},{1,9},{5... | collective-permute-start | bytes 393224 | tf_op jit(solution)/shard_map/ppermute | solution.py:401
  5.2 6.5 %collective-permute-start.6 = (bf16[256,256]{1,0:T(8,128)(2,1)}, bf16[256,256]{1,0:T(8,128)(2,1)S(1)}, u32[]{:S(2)}, u32[]{:S(2)}) collective-permute-start(bf16[256,256]{1,0:T(8,128)(2,1)} %stack.1.s0), channel_id=1, source_target_pairs={{0,2},{1,3},{2,0},{3,1},{4,6},{5,7},{6,4},{7,5},{8,10},{9,11},{10,... | collective-permute-start | bytes 393224 | tf_op jit(solution)/shard_map/ppermute | solution.py:402
  6.7 13.4 %collective-permute-start.7 = (bf16[256,256]{1,0:T(8,128)(2,1)}, bf16[256,256]{1,0:T(8,128)(2,1)S(1)}, u32[]{:S(2)}, u32[]{:S(2)}) collective-permute-start(bf16[256,256]{1,0:T(8,128)(2,1)} %stack.1.s0), channel_id=1, source_target_pairs={{0,3},{1,2},{2,1},{3,0},{4,7},{5,6},{6,5},{7,4},{8,11},{9,10},{10,... | collective-permute-start | bytes 393224 | tf_op jit(solution)/shard_map/ppermute | solution.py:402
  6.8 13.3 %collective-permute-start.2 = (bf16[256,256]{1,0:T(8,128)(2,1)}, bf16[256,256]{1,0:T(8,128)(2,1)S(1)}, u32[]{:S(2)}, u32[]{:S(2)}) collective-permute-start(bf16[256,256]{1,0:T(8,128)(2,1)} %stack.1.s0), channel_id=1, source_target_pairs={{0,24},{4,28},{8,16},{12,20},{16,8},{20,12},{24,0},{28,4},{1,25},{... | collective-permute-start | bytes 393224 | tf_op jit(solution)/shard_map/ppermute | solution.py:404
  9.3 13.0 %collective-permute-start.3 = (bf16[256,256]{1,0:T(8,128)(2,1)}, bf16[256,256]{1,0:T(8,128)(2,1)S(1)}, u32[]{:S(2)}, u32[]{:S(2)}) collective-permute-start(bf16[256,256]{1,0:T(8,128)(2,1)} %stack.1.s0), channel_id=1, source_target_pairs={{0,16},{4,20},{8,24},{12,28},{16,0},{20,4},{24,8},{28,12},{1,17},{... | collective-permute-start | bytes 393224 | tf_op jit(solution)/shard_map/ppermute | solution.py:404
  9.6 12.7 %collective-permute-start.4 = (bf16[256,256]{1,0:T(8,128)(2,1)S(1)}, bf16[256,256]{1,0:T(8,128)(2,1)S(1)}, u32[]{:S(2)}, u32[]{:S(2)}) collective-permute-start(bf16[256,256]{1,0:T(8,128)(2,1)S(1)} %collective-permute-done.s0), channel_id=1, source_target_pairs={{0,1},{1,0},{2,3},{3,2},{4,5},{5,4},{6,7},{7,6},{8,9},{9,8},{10,11... | collective-permute-start | bytes 393224 | tf_op jit(solution)/shard_map/ppermute | solution.py:412
  9.7 14.7 %copy-start.3 = (f32[1024]{0:T(1024)S(1)}, f32[1024]{0:T(1024)}, u32[]{:S(2)}) copy-start(f32[1024]{0:T(1024)} %param.8) | copy-start | bytes 12292
  11.4 13.0 %copy-start = (bf16[256,256]{1,0:T(8,128)(2,1)S(1)}, bf16[256,256]{1,0:T(8,128)(2,1)}, u32[]{:S(2)}) copy-start(bf16[256,256]{1,0:T(8,128)(2,1)} %stack.1.s0) | copy-start | bytes 393220
  11.7 10.5 %collective-permute-start.5 = (bf16[256,256]{1,0:T(8,128)(2,1)S(1)}, bf16[256,256]{1,0:T(8,128)(2,1)S(1)}, u32[]{:S(2)}, u32[]{:S(2)}) collective-permute-start(bf16[256,256]{1,0:T(8,128)(2,1)S(1)} %collective-permute-done.s0), channel_id=1, source_target_pairs={{0,2},{1,3},{2,0},{3,1},{4,6},{5,7},{6,4},{7,5},{8,10},{9,11},{10,... | collective-permute-start | bytes 393224 | tf_op jit(solution)/shard_map/ppermute | solution.py:412
  13.3 0.7 %copy-start.1 = (s32[8,256]{1,0:T(8,128)S(1)}, s32[8,256]{1,0:T(8,128)}, u32[]{:S(2)}) copy-start(s32[8,256]{1,0:T(8,128)} %plan.1.plan_ref) | copy-start | bytes 24580
  14.0 10.4 %copy-start.2 = (s32[8,256]{1,0:T(8,128)S(1)}, s32[8,256]{1,0:T(8,128)}, u32[]{:S(2)}) copy-start(s32[8,256]{1,0:T(8,128)} %plan.1.plan_ref) | copy-start | bytes 24580
  22.3 8.2 %collective-permute-start.10 = (bf16[512,256]{1,0:T(8,128)(2,1)S(1)}, bf16[512,256]{1,0:T(8,128)(2,1)S(1)}, u32[]{:S(2)}, u32[]{:S(2)}) collective-permute-start(bf16[512,256]{1,0:T(8,128)(2,1)S(1)} %constant_dynamic-update-slice_fusion.s0), channel_id=1, source_target_pairs={{0,2},{1,3},{2,0},{3,1},{4,6},{5,7},{6,4},{7,5},{8,10},{9,11},{10,... | collective-permute-start | bytes 786440 | tf_op jit(solution)/shard_map/ppermute | solution.py:448
  23.9 11.0 %collective-permute-start.9 = (bf16[512,256]{1,0:T(8,128)(2,1)S(1)}, bf16[512,256]{1,0:T(8,128)(2,1)S(1)}, u32[]{:S(2)}, u32[]{:S(2)}) collective-permute-start(bf16[512,256]{1,0:T(8,128)(2,1)S(1)} %constant_dynamic-update-slice_fusion.s0), channel_id=1, source_target_pairs={{0,1},{1,0},{2,3},{3,2},{4,5},{5,4},{6,7},{7,6},{8,9},{9,8},{10,11... | collective-permute-start | bytes 786440 | tf_op jit(solution)/shard_map/ppermute | solution.py:448
  23.9 6.7 %collective-permute-start.8 = (bf16[256,256]{1,0:T(8,128)(2,1)S(1)}, bf16[256,256]{1,0:T(8,128)(2,1)S(1)}, u32[]{:S(2)}, u32[]{:S(2)}) collective-permute-start(bf16[256,256]{1,0:T(8,128)(2,1)S(1)} %collective-permute-done.5.s2), channel_id=1, source_target_pairs={{0,1},{1,0},{2,3},{3,2},{4,5},{5,4},{6,7},{7,6},{8,9},{9,8},{10,11... | collective-permute-start | bytes 393224 | tf_op jit(solution)/shard_map/ppermute | solution.py:449
  30.5 4.4 %collective-permute-start.11 = (bf16[512,256]{1,0:T(8,128)(2,1)S(1)}, bf16[512,256]{1,0:T(8,128)(2,1)S(1)}, u32[]{:S(2)}, u32[]{:S(2)}) collective-permute-start(bf16[512,256]{1,0:T(8,128)(2,1)S(1)} %collective-permute-done.10.s2), channel_id=1, source_target_pairs={{0,1},{1,0},{2,3},{3,2},{4,5},{5,4},{6,7},{7,6},{8,9},{9,8},{10,11... | collective-permute-start | bytes 786440 | tf_op jit(solution)/shard_map/ppermute | solution.py:484
  46.1 14.5 %collective-permute-start.12 = (bf16[64,32,128]{2,1,0:T(8,128)(2,1)S(1)}, bf16[64,32,128]{2,1,0:T(8,128)(2,1)S(1)}, u32[]{:S(2)}, u32[]{:S(2)}) collective-permute-start(bf16[64,32,128]{2,1,0:T(8,128)(2,1)S(1)} %block_kernel.2), channel_id=1, source_target_pairs={{0,4},{4,0},{8,12},{12,8},{16,20},{20,16},{24,28},{28,24},{1,5},{5... | collective-permute-start | bytes 1572872 | tf_op jit(solution)/shard_map/ppermute | solution.py:505
  50.4 5.7 %collective-permute-start.13 = (bf16[256,256]{1,0:T(8,128)(2,1)S(1)}, bf16[256,256]{1,0:T(8,128)(2,1)S(1)}, u32[]{:S(2)}, u32[]{:S(2)}) collective-permute-start(bf16[256,256]{1,0:T(8,128)(2,1)S(1)} %get-tuple-element.73), channel_id=1, source_target_pairs={{0,1},{1,0},{2,3},{3,2},{4,5},{5,4},{6,7},{7,6},{8,9},{9,8},{10,11... | collective-permute-start | bytes 393224 | tf_op jit(solution)/shard_map/ppermute | solution.py:514
  51.6 6.4 %collective-permute-start.14 = (bf16[256,256]{1,0:T(8,128)(2,1)S(1)}, bf16[256,256]{1,0:T(8,128)(2,1)S(1)}, u32[]{:S(2)}, u32[]{:S(2)}) collective-permute-start(bf16[256,256]{1,0:T(8,128)(2,1)S(1)} %get-tuple-element.74), channel_id=1, source_target_pairs={{0,2},{1,3},{2,0},{3,1},{4,6},{5,7},{6,4},{7,5},{8,10},{9,11},{10,... | collective-permute-start | bytes 393224 | tf_op jit(solution)/shard_map/ppermute | solution.py:514
  52.2 6.8 %collective-permute-start.15 = (bf16[256,256]{1,0:T(8,128)(2,1)S(1)}, bf16[256,256]{1,0:T(8,128)(2,1)S(1)}, u32[]{:S(2)}, u32[]{:S(2)}) collective-permute-start(bf16[256,256]{1,0:T(8,128)(2,1)S(1)} %get-tuple-element.75), channel_id=1, source_target_pairs={{0,3},{1,2},{2,1},{3,0},{4,7},{5,6},{6,5},{7,4},{8,11},{9,10},{10,... | collective-permute-start | bytes 393224 | tf_op jit(solution)/shard_map/ppermute | solution.py:514

commit v4 on v3

--- a/solution.py
+++ b/solution.py
@@ -301,12 +301,12 @@
 
 
 def block_kernel(
-    list_row, scale, plan, gp0, gp1, gp2, n0, n1, n2, p_out, out_ref, found
+    list_row, scale, plan, gp0, gp1, gp2, n0, n1, n2, p_out, found
 ):
     per_row = p_out.shape[1] // HALF
     lanes = 2 * BLK
     pairs = p_out.shape[0] // 2
-    cap = out_ref.shape[0]
+    cap = found.shape[0] - 1
     left = iota((HALF, lanes), 1) < BLK
     found[...] = jnp.zeros_like(found)
 
@@ -331,7 +331,7 @@
             top = jnp.where(odd, pltpu.roll(top, BLK, 1), top)
             low = jnp.where(odd, low, pltpu.roll(low, BLK, 1))
             slot = jnp.where(first < end, plan[1, k], cap)
-            done.append((slot, jnp.where(left, top, low)))
+            done.append((slot, jnp.where(left, top, low).astype(found.dtype)))
         for slot, value in done:
             found[slot] = value
 
@@ -351,7 +351,6 @@
         return lax.fori_loop(1, (end - begin + BATCH - 1) // BATCH, more, carry)
 
     lax.fori_loop(0, pairs, finish, 0)
-    out_ref[...] = found[:cap].astype(out_ref.dtype)
 
 
 def finish_kernel(own_ref, arrived_ref, s0, s1, s2, s3, branch_ref, normed_ref, out_ref):
@@ -399,8 +398,9 @@
         name="stack",
     )(x_in, grad_out)
     pieces = [lax.ppermute(own, "dp", along_z[0])]
-    gathered = [own] + [lax.ppermute(own, "mp", near[q]) for q in range(1, mp_count)]
-    gathered[1], own_late = lax.optimization_barrier((gathered[1], own))
+    over_core, own_late = lax.optimization_barrier((lax.ppermute(own, "mp", near[1]), own))
+    over_y = lax.ppermute(own_late, "mp", near[2])
+    gathered = [own, over_core, over_y, lax.ppermute(over_y, "mp", near[1])]
     pieces += [lax.ppermute(own_late, "dp", hop) for hop in along_z[1:]]
     pieces[0], cols_late, slots_late = lax.optimization_barrier((pieces[0], block_cols, slots))
     plan = pl.pallas_call(
@@ -494,8 +494,8 @@
     def blocks(list_row, dtype, flops, plan):
         return call(
             functools.partial(block_kernel, list_row, scale),
-            [jax.ShapeDtypeStruct((cap, HALF, lanes), dtype)],
-            [pltpu.VMEM((cap + 1, HALF, lanes), F32)],
+            [jax.ShapeDtypeStruct((cap + 1, HALF, lanes), dtype)],
+            [],
             16, flops, 0,
             plan, gp_own, gp_near, gp_far, n_own, n_near, n_far, p_out,
         )[0]
@@ -512,7 +512,7 @@
     )
     for_own = blocks(6, F32, 0, plan_later)
     summed = [parts[0]] + [lax.ppermute(parts[q], "mp", near[q]) for q in range(1, mp_count)]
-    steps = 4
+    steps = 2
     own_rows = pl.BlockSpec((cap // steps, HALF, lanes), lambda i: (i, 0, 0))
     token_rows = pl.BlockSpec((2 * tok, width), lambda i: (0, 0))
     result = pl.BlockSpec((tok, width), lambda i: (0, 0))

time: 62.4 us -> 60.5 us (0.970)
  waiting for transfers between devices: 7.27 us -> 4.4 us
  Pallas kernels: 38.5 us -> 39.6 us
    pallas_call x6, Pallas kernels: 27.4 us -> 29 us  [call(): pl.pallas_call(kernel, out_shape=out_shape, grid_spec=pltpu.PrefetchScala...]
    ppermute x1, waiting for transfers between devices: 1.68 us -> 0.21 us  [fast_body(): arrived = lax.ppermute(for_peer, 'dp', across_x)]
    ppermute x2, starting transfers between devices: 1.59 us -> 0.57 us  [fast_body(): lax.ppermute(column, 'mp', near[q])]
    ppermute x2, starting transfers between devices: 2.62 us -> 3.58 us  [fast_body(): pieces += [lax.ppermute(own_late, 'dp', hop) for hop in along_z[1:]]]
    ppermute x1, starting transfers between devices: 1.55 us -> 2.43 us  [fast_body(): arrived = lax.ppermute(for_peer, 'dp', across_x)]
    ppermute x3, starting transfers between devices: 2.62 us -> 1.93 us  [fast_body(): lax.ppermute(parts[q], 'mp', near[q])]
    ppermute x2, starting transfers between devices: 1.61 us -> 0.95 us  [fast_body(): lax.ppermute(pieces[0], 'mp', near[q])]
  transfers between devices with their start and end apart: 16 -> 16, of which waited for: 7 -> 5; matrix products, arithmetic and copies ran while one was open for 0% -> 0% of each run, Pallas kernels for 38% -> 42%
where the time goes in v4:
time: 60.5 us; the launch traced here: 60.2 us
  Pallas kernels  39.6 us (65%)
  starting transfers between devices  14.7 us (24%)
  waiting for transfers between devices  4.4 us (7%)
  between operations  0.78 us (1%)
  local copies, waits for them, and re-layouts  0.73 us (1%)
    pallas_call x6, Pallas kernels, call(): pl.pallas_call(kernel, out_shape=out_shape, grid_spec=pltpu.PrefetchScala...  29 us
    pallas_call x1, Pallas kernels, fast_body(): pl.pallas_call(prepare_kernel, out_shape=[jax.ShapeDtypeStruct((row_block...  6.13 us
    ppermute x2, starting transfers between devices, fast_body(): pieces += [lax.ppermute(own_late, 'dp', hop) for hop in along_z[1:]]  3.58 us
    ppermute x1, starting transfers between devices, fast_body(): pieces = [lax.ppermute(own, 'dp', along_z[0])]  2.57 us
    ppermute x3, waiting for transfers between devices, fast_body(): lax.ppermute(parts[q], 'mp', near[q])  2.47 us
    ppermute x1, starting transfers between devices, fast_body(): arrived = lax.ppermute(for_peer, 'dp', across_x)  2.43 us
    ppermute x3, starting transfers between devices, fast_body(): lax.ppermute(parts[q], 'mp', near[q])  1.93 us
    pallas_call x1, Pallas kernels, fast_body(): pl.pallas_call(functools.partial(plan_kernel, cap, col_blocks, row_blocks...  1.73 us
  transfers between devices with their start and end apart: 16, of which 5 were waited for; matrix products, arithmetic and copies ran while one was open for 0% of the time, Pallas kernels for 42%

profile of v4, /device:TPU:0, one launch (start us, length us, event | category | flops | bytes accessed | tf_op | source)
XLA Modules:
  0.0 60.2 jit_solution(10740352122559875780)
XLA Ops:
  0.6 1.5 %stack.1.s0 = bf16[256,256]{1,0:T(8,128)(2,1)} custom-call(bf16[128,256]{1,0:T(8,128)(2,1)} %x_ref.1, bf16[128,256]{1,0:T(8,128)(2,1)} %grad_ref.1), custom_call_target="tpu_custom_call" | custom-call | bytes 262144 | tf_op jit(solution)/shard_map/stack/pallas_call | solution.py:394
  2.2 0.5 collective-permute-start.1
  2.6 2.6 %collective-permute-start = (bf16[256,256]{1,0:T(8,128)(2,1)}, bf16[256,256]{1,0:T(8,128)(2,1)S(1)}, u32[]{:S(2)}, u32[]{:S(2)}) collective-permute-start(bf16[256,256]{1,0:T(8,128)(2,1)} %stack.1.s0), channel_id=1, source_target_pairs={{0,8},{4,12},{8,0},{12,4},{16,24},{20,28},{24,16},{28,20},{1,9},{5... | collective-permute-start | bytes 393224 | tf_op jit(solution)/shard_map/ppermute | solution.py:400
  5.2 0.0 collective-permute-done.1.s1
  5.2 1.5 %collective-permute-start.6 = (bf16[256,256]{1,0:T(8,128)(2,1)}, bf16[256,256]{1,0:T(8,128)(2,1)S(1)}, u32[]{:S(2)}, u32[]{:S(2)}) collective-permute-start(bf16[256,256]{1,0:T(8,128)(2,1)} %stack.1.s0), channel_id=1, source_target_pairs={{0,2},{1,3},{2,0},{3,1},{4,6},{5,7},{6,4},{7,5},{8,10},{9,11},{10,... | collective-permute-start | bytes 393224 | tf_op jit(solution)/shard_map/ppermute | solution.py:402
  6.7 3.6 %collective-permute-start.2 = (bf16[256,256]{1,0:T(8,128)(2,1)}, bf16[256,256]{1,0:T(8,128)(2,1)S(1)}, u32[]{:S(2)}, u32[]{:S(2)}) collective-permute-start(bf16[256,256]{1,0:T(8,128)(2,1)} %stack.1.s0), channel_id=1, source_target_pairs={{0,24},{4,28},{8,16},{12,20},{16,8},{20,12},{24,0},{28,4},{1,25},{... | collective-permute-start | bytes 393224 | tf_op jit(solution)/shard_map/ppermute | solution.py:404
  10.3 0.0 collective-permute-start.3
  10.3 0.0 collective-permute-done.s0
  10.3 0.9 %collective-permute-start.5 = (bf16[256,256]{1,0:T(8,128)(2,1)S(1)}, bf16[256,256]{1,0:T(8,128)(2,1)S(1)}, u32[]{:S(2)}, u32[]{:S(2)}) collective-permute-start(bf16[256,256]{1,0:T(8,128)(2,1)S(1)} %collective-permute-done.s0), channel_id=1, source_target_pairs={{0,2},{1,3},{2,0},{3,1},{4,6},{5,7},{6,4},{7,5},{8,10},{9,11},{10,... | collective-permute-start | bytes 393224 | tf_op jit(solution)/shard_map/ppermute | solution.py:412
  11.3 1.7 %plan.1.plan_ref = s32[8,256]{1,0:T(8,128)} custom-call(s32[1,256]{1,0:T(1,128)} %cols_ref, s32[1,256]{1,0:T(1,128)} %slots_ref), custom_call_target="tpu_custom_call" | custom-call | flops 4000000 | bytes 16384 | tf_op jit(solution)/shard_map/plan/pallas_call | solution.py:406
  13.0 0.0 collective-permute-done.6.s2
  13.0 0.2 collective-permute-start.7
  13.2 0.7 %copy-done.1 = s32[8,256]{1,0:T(8,128)S(1)} copy-done((s32[8,256]{1,0:T(8,128)S(1)}, s32[8,256]{1,0:T(8,128)}, u32[]{:S(2)}) %copy-start.1) | copy-done | bytes 8216
  13.9 6.1 %prepare.1 = (bf16[16,512,128]{2,1,0:T(8,128)(2,1)S(1)}, bf16[16,64,1024]{2,1,0:T(8,128)(2,1)S(1)}, bf16[16,512,128]{2,1,0:T(8,128)(2,1)S(1)}, bf16[16,64,1024]{2,1,0:T(8,128)(2,1)S(1)}) custom-call(s32[8,256]{1,0:T(8,128)S(1)} %copy-done.1, bf16[256,4096]{1,0:T(8,128)(2,1)} %win_ref.1, bf16[256,4096]{1,0:T(8,128)(2,1)} %wout_ref.1), custom_call_target="tpu_custom_call" | custom-call | flops 2147483648 | bytes 12582912 | tf_op jit(solution)/shard_map/prepare/pallas_call | solution.py:422
  20.1 1.5 %collective-permute-done.3 = bf16[256,256]{1,0:T(8,128)(2,1)S(1)} collective-permute-done((bf16[256,256]{1,0:T(8,128)(2,1)}, bf16[256,256]{1,0:T(8,128)(2,1)S(1)}, u32[]{:S(2)}, u32[]{:S(2)}) %collective-permute-start.3) | collective-permute-done | bytes 131104 | tf_op jit(solution)/shard_map/ppermute | solution.py:404
  21.7 0.6 collective-permute-start.10
  22.2 0.5 collective-permute-start.8
  22.8 6.1 %local_kernel.1 = (bf16[128,64,128]{2,1,0:T(8,128)(2,1)S(1)}, bf16[128,64,128]{2,1,0:T(8,128)(2,1)S(1)}, bf16[128,1024]{1,0:T(8,128)(2,1)S(1)}) custom-call(s32[8,256]{1,0:T(8,128)S(1)} %copy-done.2, f32[1,1024]{1,0:T(1,128)S(1)} %bitcast.2, bf16[256,256]{1,0:T(8,128)(2,1)S(1)} %copy-done, bf16[256,256]{1,0:T(8,128)(2,1)S(1)} %collective-permute-done.1.s1, ...), custom_call_target="tpu_custom_call" | custom-call | flops 2147483648 | bytes 4194304 | tf_op jit(solution)/shard_map/local_kernel/pallas_call | solution.py:461
  28.9 0.2 collective-permute-done.10.s2
  29.0 4.6 %chunk_kernel.2 = (bf16[1,128,64,128]{3,2,1,0:T(8,128)(2,1)S(1)}, bf16[128,1024]{1,0:T(8,128)(2,1)S(1)}) custom-call(s32[8,256]{1,0:T(8,128)S(1)} %copy-done.2, f32[1,1024]{1,0:T(1,128)S(1)} %bitcast.3, bf16[256,256]{1,0:T(8,128)(2,1)S(1)} %collective-permute-done.s0, bf16[256,256]{1,0:T(8,128)(2,1)S(1)} %collective-permute-done.4.s1, ...), custom_call_target="tpu_custom_call" | custom-call | flops 2147483648 | bytes 4194304 | tf_op jit(solution)/shard_map/chunk_kernel/pallas_call | solution.py:461
  33.6 8.7 %chunk_kernel.3 = (bf16[2,128,64,128]{3,2,1,0:T(8,128)(2,1)S(1)}, bf16[256,1024]{1,0:T(8,128)(2,1)S(1)}) custom-call(s32[8,256]{1,0:T(8,128)S(1)} %copy-done.2, f32[1,1024]{1,0:T(1,128)S(1)} %bitcast.4, bf16[512,256]{1,0:T(8,128)(2,1)S(1)} %constant_dynamic-update-slice_fusion.s0, bf16[512,256]{1,0:T(8,128)(2,1)S(1)} %collective-permute-done.9.s1, ...), custom_call_target="tpu_custom_call" | custom-call | flops 4294967296 | bytes 8388608 | tf_op jit(solution)/shard_map/chunk_kernel/pallas_call | solution.py:461
  42.4 3.0 %block_kernel.2 = bf16[65,32,128]{2,1,0:T(8,128)(2,1)S(1)} custom-call(s32[8,256]{1,0:T(8,128)S(1)} %copy-done.2, bf16[128,64,128]{2,1,0:T(8,128)(2,1)S(1)} %get-tuple-element.53.gp0.gp_ref, bf16[1,128,64,128]{3,2,1,0:T(8,128)(2,1)S(1)} %get-tuple-element.57.gp1, bf16[2,128,64,128]{3,2,1,0:T(8,128)(2,1)S(1)} %get-tuple-element.62.gp2, ...), custom_call_target="tpu_custom_call" | custom-call | flops 536870912 | bytes 1048576 | tf_op jit(solution)/shard_map/block_kernel/pallas_call | solution.py:461
  45.4 2.4 %collective-permute-start.12 = (bf16[65,32,128]{2,1,0:T(8,128)(2,1)S(1)}, bf16[65,32,128]{2,1,0:T(8,128)(2,1)S(1)}, u32[]{:S(2)}, u32[]{:S(2)}) collective-permute-start(bf16[65,32,128]{2,1,0:T(8,128)(2,1)S(1)} %block_kernel.2), channel_id=1, source_target_pairs={{0,4},{4,0},{8,12},{12,8},{16,20},{20,16},{24,28},{28,24},{1,5},{5... | collective-permute-start | bytes 1597448 | tf_op jit(solution)/shard_map/ppermute | solution.py:505
  47.8 2.7 %contract_kernel.1 = (bf16[256,256]{1,0:T(8,128)(2,1)S(1)}, bf16[256,256]{1,0:T(8,128)(2,1)S(1)}, bf16[256,256]{1,0:T(8,128)(2,1)S(1)}, bf16[256,256]{1,0:T(8,128)(2,1)S(1)}) custom-call(s32[8,256]{1,0:T(8,128)S(1)} %copy-done.2, bf16[128,64,128]{2,1,0:T(8,128)(2,1)S(1)} %get-tuple-element.69.act_ref, ...), custom_call_target="tpu_custom_call" | custom-call | tf_op jit(solution)/shard_map/contract_kernel/pallas_call | solution.py:461
  50.5 0.1 collective-permute-start.13
  50.6 0.1 collective-permute-start.14
  50.6 1.8 %collective-permute-start.15 = (bf16[256,256]{1,0:T(8,128)(2,1)S(1)}, bf16[256,256]{1,0:T(8,128)(2,1)S(1)}, u32[]{:S(2)}, u32[]{:S(2)}) collective-permute-start(bf16[256,256]{1,0:T(8,128)(2,1)S(1)} %get-tuple-element.75), channel_id=1, source_target_pairs={{0,3},{1,2},{2,1},{3,0},{4,7},{5,6},{6,5},{7,4},{8,11},{9,10},{10,... | collective-permute-start | bytes 393224 | tf_op jit(solution)/shard_map/ppermute | solution.py:514
  52.4 3.9 %block_kernel.3.own_ref = f32[65,32,128]{2,1,0:T(8,128)S(1)} custom-call(s32[8,256]{1,0:T(8,128)S(1)} %copy-done.2, bf16[128,64,128]{2,1,0:T(8,128)(2,1)S(1)} %get-tuple-element.53.gp0.gp_ref, bf16[1,128,64,128]{3,2,1,0:T(8,128)(2,1)S(1)} %get-tuple-element.57.gp1, bf16[2,128,64,128]{3,2,1,0:T(8,128)(2,1)S(1)} %get-tuple-element.62.gp2, ...), custom_call_target="tpu_custom_call" | custom-call | tf_op jit(solution)/shard_map/block_kernel/pallas_call | solution.py:461
  56.4 0.6 collective-permute-done.14.s2
  56.9 1.9 %collective-permute-done.15.s3 = bf16[256,256]{1,0:T(8,128)(2,1)S(1)} collective-permute-done((bf16[256,256]{1,0:T(8,128)(2,1)S(1)}, bf16[256,256]{1,0:T(8,128)(2,1)S(1)}, u32[]{:S(2)}, u32[]{:S(2)}) %collective-permute-start.15) | collective-permute-done | bytes 131104 | tf_op jit(solution)/shard_map/ppermute | solution.py:514
  58.8 0.2 collective-permute-done.12.arrived_ref
  59.0 1.2 %finish.1 = (bf16[128,256]{1,0:T(8,128)(2,1)}, bf16[128,256]{1,0:T(8,128)(2,1)}, f32[64,4096]{1,0:T(8,128)}) custom-call(f32[65,32,128]{2,1,0:T(8,128)S(1)} %block_kernel.3.own_ref, bf16[65,32,128]{2,1,0:T(8,128)(2,1)S(1)} %collective-permute-done.12.arrived_ref, bf16[256,256]{1,0:T(8,128)(2,1)S(1)} %get-tuple-element.72.s0, ...), custom_call_target="tpu_custom_call" | custom-call | tf_op jit(solution)/shard_map/finish/pallas_call | solution.py:519
  (20 shorter events, 0.1 us)
Async XLA Ops:
  2.2 3.0 %collective-permute-start.1 = (bf16[256,256]{1,0:T(8,128)(2,1)}, bf16[256,256]{1,0:T(8,128)(2,1)S(1)}, u32[]{:S(2)}, u32[]{:S(2)}) collective-permute-start(bf16[256,256]{1,0:T(8,128)(2,1)} %stack.1.s0), channel_id=1, source_target_pairs={{0,1},{1,0},{2,3},{3,2},{4,5},{5,4},{6,7},{7,6},{8,9},{9,8},{10,11... | collective-permute-start | bytes 393224 | tf_op jit(solution)/shard_map/ppermute | solution.py:401
  2.6 7.7 %collective-permute-start = (bf16[256,256]{1,0:T(8,128)(2,1)}, bf16[256,256]{1,0:T(8,128)(2,1)S(1)}, u32[]{:S(2)}, u32[]{:S(2)}) collective-permute-start(bf16[256,256]{1,0:T(8,128)(2,1)} %stack.1.s0), channel_id=1, source_target_pairs={{0,8},{4,12},{8,0},{12,4},{16,24},{20,28},{24,16},{28,20},{1,9},{5... | collective-permute-start | bytes 393224 | tf_op jit(solution)/shard_map/ppermute | solution.py:400
  5.2 7.8 %collective-permute-start.6 = (bf16[256,256]{1,0:T(8,128)(2,1)}, bf16[256,256]{1,0:T(8,128)(2,1)S(1)}, u32[]{:S(2)}, u32[]{:S(2)}) collective-permute-start(bf16[256,256]{1,0:T(8,128)(2,1)} %stack.1.s0), channel_id=1, source_target_pairs={{0,2},{1,3},{2,0},{3,1},{4,6},{5,7},{6,4},{7,5},{8,10},{9,11},{10,... | collective-permute-start | bytes 393224 | tf_op jit(solution)/shard_map/ppermute | solution.py:402
  6.7 13.4 %collective-permute-start.2 = (bf16[256,256]{1,0:T(8,128)(2,1)}, bf16[256,256]{1,0:T(8,128)(2,1)S(1)}, u32[]{:S(2)}, u32[]{:S(2)}) collective-permute-start(bf16[256,256]{1,0:T(8,128)(2,1)} %stack.1.s0), channel_id=1, source_target_pairs={{0,24},{4,28},{8,16},{12,20},{16,8},{20,12},{24,0},{28,4},{1,25},{... | collective-permute-start | bytes 393224 | tf_op jit(solution)/shard_map/ppermute | solution.py:404
  10.3 11.3 %collective-permute-start.3 = (bf16[256,256]{1,0:T(8,128)(2,1)}, bf16[256,256]{1,0:T(8,128)(2,1)S(1)}, u32[]{:S(2)}, u32[]{:S(2)}) collective-permute-start(bf16[256,256]{1,0:T(8,128)(2,1)} %stack.1.s0), channel_id=1, source_target_pairs={{0,16},{4,20},{8,24},{12,28},{16,0},{20,4},{24,8},{28,12},{1,17},{... | collective-permute-start | bytes 393224 | tf_op jit(solution)/shard_map/ppermute | solution.py:404
  10.3 11.3 %collective-permute-start.4 = (bf16[256,256]{1,0:T(8,128)(2,1)S(1)}, bf16[256,256]{1,0:T(8,128)(2,1)S(1)}, u32[]{:S(2)}, u32[]{:S(2)}) collective-permute-start(bf16[256,256]{1,0:T(8,128)(2,1)S(1)} %collective-permute-done.s0), channel_id=1, source_target_pairs={{0,1},{1,0},{2,3},{3,2},{4,5},{5,4},{6,7},{7,6},{8,9},{9,8},{10,11... | collective-permute-start | bytes 393224 | tf_op jit(solution)/shard_map/ppermute | solution.py:412
  10.3 11.3 %collective-permute-start.5 = (bf16[256,256]{1,0:T(8,128)(2,1)S(1)}, bf16[256,256]{1,0:T(8,128)(2,1)S(1)}, u32[]{:S(2)}, u32[]{:S(2)}) collective-permute-start(bf16[256,256]{1,0:T(8,128)(2,1)S(1)} %collective-permute-done.s0), channel_id=1, source_target_pairs={{0,2},{1,3},{2,0},{3,1},{4,6},{5,7},{6,4},{7,5},{8,10},{9,11},{10,... | collective-permute-start | bytes 393224 | tf_op jit(solution)/shard_map/ppermute | solution.py:412
  11.3 11.5 %copy-start.3 = (f32[1024]{0:T(1024)S(1)}, f32[1024]{0:T(1024)}, u32[]{:S(2)}) copy-start(f32[1024]{0:T(1024)} %param.8) | copy-start | bytes 12292
  13.0 9.8 %copy-start = (bf16[256,256]{1,0:T(8,128)(2,1)S(1)}, bf16[256,256]{1,0:T(8,128)(2,1)}, u32[]{:S(2)}) copy-start(bf16[256,256]{1,0:T(8,128)(2,1)} %stack.1.s0) | copy-start | bytes 393220
  13.0 8.6 %collective-permute-start.7 = (bf16[256,256]{1,0:T(8,128)(2,1)S(1)}, bf16[256,256]{1,0:T(8,128)(2,1)S(1)}, u32[]{:S(2)}, u32[]{:S(2)}) collective-permute-start(bf16[256,256]{1,0:T(8,128)(2,1)S(1)} %collective-permute-done.6.s2), channel_id=1, source_target_pairs={{0,1},{1,0},{2,3},{3,2},{4,5},{5,4},{6,7},{7,6},{8,9},{9,8},{10,11... | collective-permute-start | bytes 393224 | tf_op jit(solution)/shard_map/ppermute | solution.py:403
  13.2 0.7 %copy-start.1 = (s32[8,256]{1,0:T(8,128)S(1)}, s32[8,256]{1,0:T(8,128)}, u32[]{:S(2)}) copy-start(s32[8,256]{1,0:T(8,128)} %plan.1.plan_ref) | copy-start | bytes 24580
  13.9 8.8 %copy-start.2 = (s32[8,256]{1,0:T(8,128)S(1)}, s32[8,256]{1,0:T(8,128)}, u32[]{:S(2)}) copy-start(s32[8,256]{1,0:T(8,128)} %plan.1.plan_ref) | copy-start | bytes 24580
  21.7 7.3 %collective-permute-start.10 = (bf16[512,256]{1,0:T(8,128)(2,1)S(1)}, bf16[512,256]{1,0:T(8,128)(2,1)S(1)}, u32[]{:S(2)}, u32[]{:S(2)}) collective-permute-start(bf16[512,256]{1,0:T(8,128)(2,1)S(1)} %constant_dynamic-update-slice_fusion.s0), channel_id=1, source_target_pairs={{0,2},{1,3},{2,0},{3,1},{4,6},{5,7},{6,4},{7,5},{8,10},{9,11},{10,... | collective-permute-start | bytes 786440 | tf_op jit(solution)/shard_map/ppermute | solution.py:448
  22.2 11.4 %collective-permute-start.9 = (bf16[512,256]{1,0:T(8,128)(2,1)S(1)}, bf16[512,256]{1,0:T(8,128)(2,1)S(1)}, u32[]{:S(2)}, u32[]{:S(2)}) collective-permute-start(bf16[512,256]{1,0:T(8,128)(2,1)S(1)} %constant_dynamic-update-slice_fusion.s0), channel_id=1, source_target_pairs={{0,1},{1,0},{2,3},{3,2},{4,5},{5,4},{6,7},{7,6},{8,9},{9,8},{10,11... | collective-permute-start | bytes 786440 | tf_op jit(solution)/shard_map/ppermute | solution.py:448
  22.2 6.8 %collective-permute-start.8 = (bf16[256,256]{1,0:T(8,128)(2,1)S(1)}, bf16[256,256]{1,0:T(8,128)(2,1)S(1)}, u32[]{:S(2)}, u32[]{:S(2)}) collective-permute-start(bf16[256,256]{1,0:T(8,128)(2,1)S(1)} %collective-permute-done.5.s2), channel_id=1, source_target_pairs={{0,1},{1,0},{2,3},{3,2},{4,5},{5,4},{6,7},{7,6},{8,9},{9,8},{10,11... | collective-permute-start | bytes 393224 | tf_op jit(solution)/shard_map/ppermute | solution.py:449
  29.0 4.6 %collective-permute-start.11 = (bf16[512,256]{1,0:T(8,128)(2,1)S(1)}, bf16[512,256]{1,0:T(8,128)(2,1)S(1)}, u32[]{:S(2)}, u32[]{:S(2)}) collective-permute-start(bf16[512,256]{1,0:T(8,128)(2,1)S(1)} %collective-permute-done.10.s2), channel_id=1, source_target_pairs={{0,1},{1,0},{2,3},{3,2},{4,5},{5,4},{6,7},{7,6},{8,9},{9,8},{10,11... | collective-permute-start | bytes 786440 | tf_op jit(solution)/shard_map/ppermute | solution.py:484
  45.4 13.7 %collective-permute-start.12 = (bf16[65,32,128]{2,1,0:T(8,128)(2,1)S(1)}, bf16[65,32,128]{2,1,0:T(8,128)(2,1)S(1)}, u32[]{:S(2)}, u32[]{:S(2)}) collective-permute-start(bf16[65,32,128]{2,1,0:T(8,128)(2,1)S(1)} %block_kernel.2), channel_id=1, source_target_pairs={{0,4},{4,0},{8,12},{12,8},{16,20},{20,16},{24,28},{28,24},{1,5},{5... | collective-permute-start | bytes 1597448 | tf_op jit(solution)/shard_map/ppermute | solution.py:505
  50.5 5.9 %collective-permute-start.13 = (bf16[256,256]{1,0:T(8,128)(2,1)S(1)}, bf16[256,256]{1,0:T(8,128)(2,1)S(1)}, u32[]{:S(2)}, u32[]{:S(2)}) collective-permute-start(bf16[256,256]{1,0:T(8,128)(2,1)S(1)} %get-tuple-element.73), channel_id=1, source_target_pairs={{0,1},{1,0},{2,3},{3,2},{4,5},{5,4},{6,7},{7,6},{8,9},{9,8},{10,11... | collective-permute-start | bytes 393224 | tf_op jit(solution)/shard_map/ppermute | solution.py:514
  50.6 6.4 %collective-permute-start.14 = (bf16[256,256]{1,0:T(8,128)(2,1)S(1)}, bf16[256,256]{1,0:T(8,128)(2,1)S(1)}, u32[]{:S(2)}, u32[]{:S(2)}) collective-permute-start(bf16[256,256]{1,0:T(8,128)(2,1)S(1)} %get-tuple-element.74), channel_id=1, source_target_pairs={{0,2},{1,3},{2,0},{3,1},{4,6},{5,7},{6,4},{7,5},{8,10},{9,11},{10,... | collective-permute-start | bytes 393224 | tf_op jit(solution)/shard_map/ppermute | solution.py:514
  50.6 8.2 %collective-permute-start.15 = (bf16[256,256]{1,0:T(8,128)(2,1)S(1)}, bf16[256,256]{1,0:T(8,128)(2,1)S(1)}, u32[]{:S(2)}, u32[]{:S(2)}) collective-permute-start(bf16[256,256]{1,0:T(8,128)(2,1)S(1)} %get-tuple-element.75), channel_id=1, source_target_pairs={{0,3},{1,2},{2,1},{3,0},{4,7},{5,6},{6,5},{7,4},{8,11},{9,10},{10,... | collective-permute-start | bytes 393224 | tf_op jit(solution)/shard_map/ppermute | solution.py:514

commit v5 on v4

--- a/solution.py
+++ b/solution.py
@@ -13,7 +13,7 @@
 HALF = BLK // 2
 GROUP = 4
 FIRST = 1024
-BATCH = 12
+BATCH = 10
 BEND = 8
 
 
@@ -253,7 +253,7 @@
         gp_ref[c] = (acc_a[c] * slope).astype(BF16)
         return carry
 
-    lax.fori_loop(0, gp_ref.shape[0], bend, 0, unroll=4)
+    lax.fori_loop(0, gp_ref.shape[0], bend, 0, unroll=8)
 
 
 def contract_kernel(plan, act_ref, gp_ref, b_in, a_out, o0, o1, o2, o3, br_s, gn_s):
@@ -270,7 +270,7 @@
         gn_s[at, :] = dot(b_in[r], jnp.concatenate(grads, axis=0)).astype(BF16)
         return carry
 
-    lax.fori_loop(0, row_blocks, contract, 0, unroll=8)
+    lax.fori_loop(0, row_blocks, contract, 0, unroll=16)
     mine = lax.axis_index("mp")
     for q, out in enumerate((o0, o1, o2, o3)):
         at = pl.ds(pl.multiple_of((mine ^ q) * width, width), width)
@@ -287,8 +287,9 @@
     count = plan[5, 0]
     for j in range(chunks):
         pieces = [(ref, 2 * tok * j) for ref in (s0, s1, s2, s3)]
-        load_tokens(pieces, tok, gain_ref, perm, n_ref, nt_s, gt_s, j * tok)
-        expand(plan, a_in, p_out, nt_s, gt_s, acc_v, acc_a)
+        load_tokens(pieces, tok, gain_ref, perm, n_ref, nt_s.at[j], gt_s.at[j], j * tok)
+    for j in range(chunks):
+        expand(plan, a_in, p_out, nt_s.at[j], gt_s.at[j], acc_v, acc_a)
 
         def bend(i, carry):
             for u in range(BEND):
@@ -400,7 +401,7 @@
     pieces = [lax.ppermute(own, "dp", along_z[0])]
     over_core, own_late = lax.optimization_barrier((lax.ppermute(own, "mp", near[1]), own))
     over_y = lax.ppermute(own_late, "mp", near[2])
-    gathered = [own, over_core, over_y, lax.ppermute(over_y, "mp", near[1])]
+    gathered = [own, over_core, over_y, lax.ppermute(own_late, "mp", near[3])]
     pieces += [lax.ppermute(own_late, "dp", hop) for hop in along_z[1:]]
     pieces[0], cols_late, slots_late = lax.optimization_barrier((pieces[0], block_cols, slots))
     plan = pl.pallas_call(
@@ -409,7 +410,7 @@
         cost_estimate=pl.CostEstimate(flops=4_000_000, bytes_accessed=16384, transcendentals=0),
         name="plan",
     )(cols_late, slots_late)
-    near_piece = [pieces[0]] + [lax.ppermute(pieces[0], "mp", near[q]) for q in (1, 2)]
+    near_piece = [pieces[0], lax.ppermute(pieces[0], "mp", near[2])]
     gain_row = gain.reshape(1, feat)
 
     step = min(4, row_blocks)
@@ -446,7 +447,12 @@
     )
     column = jnp.concatenate(late, axis=0)
     far_pieces = [column] + [lax.ppermute(column, "mp", near[q]) for q in (1, 2)]
-    near_piece.append(lax.ppermute(near_piece[2], "mp", near[1]))
+    near_piece = [
+        near_piece[0],
+        lax.ppermute(near_piece[0], "mp", near[1]),
+        near_piece[1],
+        lax.ppermute(near_piece[1], "mp", near[1]),
+    ]
 
     hidden_f32 = pltpu.VMEM((col_blocks, BLK, tok), F32)
     turned = pltpu.VMEM((feat, tok), BF16)
@@ -476,6 +482,10 @@
         )(*args)
 
     scratch = [turned, turned, hidden_f32, hidden_f32]
+
+    def chunk_scratch(chunks):
+        return [pltpu.VMEM((chunks, feat, tok), BF16)] * 2 + [hidden_f32] * 2
+
     act, gp_own, n_own = call(
         local_kernel, [hidden_bf16(), hidden_bf16(), flat(1)], scratch, 32, 8 * mm, tok * hidden,
         plan, gain_row, *gathered, a_in, p_out,
@@ -483,11 +493,11 @@
     far_pieces[2], n_own = lax.optimization_barrier((far_pieces[2], n_own))
     far_pieces.append(lax.ppermute(far_pieces[2], "mp", near[1]))
     gp_near, n_near = call(
-        chunk_kernel, [hidden_bf16(1), flat(1)], scratch, 32, 8 * mm, tok * hidden // 2,
+        chunk_kernel, [hidden_bf16(1), flat(1)], chunk_scratch(1), 32, 8 * mm, tok * hidden // 2,
         plan, gain_row, *near_piece, a_in, p_out,
     )
     gp_far, n_far = call(
-        chunk_kernel, [hidden_bf16(z_count - 2), flat(z_count - 2)], scratch, 32, 16 * mm, tok * hidden,
+        chunk_kernel, [hidden_bf16(z_count - 2), flat(z_count - 2)], chunk_scratch(z_count - 2), 32, 16 * mm, tok * hidden,
         plan, gain_row, *far_pieces, a_in, p_out,
     )
 

time: 60.5 us -> 60.6 us (level)
  Pallas kernels: 39.6 us -> 37.9 us
  starting transfers between devices: 14.7 us -> 15.7 us
  waiting for transfers between devices: 4.4 us -> 5.22 us
    pallas_call x6, Pallas kernels: 29 us -> 27.3 us  [call(): pl.pallas_call(kernel, out_shape=out_shape, grid_spec=pltpu.PrefetchScala...]
    ppermute x2, waiting for transfers between devices: 1.55 us -> 0.23 us  [fast_body(): pieces += [lax.ppermute(own_late, 'dp', hop) for hop in along_z[1:]]]
    ppermute x1, waiting for transfers between devices: 0.21 us -> 1.47 us  [fast_body(): arrived = lax.ppermute(for_peer, 'dp', across_x)]
    ppermute x2, starting transfers between devices: 0.57 us -> 1.59 us  [fast_body(): lax.ppermute(column, 'mp', near[q])]
  transfers between devices with their start and end apart: 16 -> 16, of which waited for: 5 -> 5; matrix products, arithmetic and copies ran while one was open for 0% -> 0% of each run, Pallas kernels for 42% -> 40%
where the time goes in v5:
time: 60.6 us; the launch traced here: 60.4 us
  Pallas kernels  37.9 us (63%)
  starting transfers between devices  15.7 us (26%)
  waiting for transfers between devices  5.22 us (9%)
  between operations  0.78 us (1%)
  local copies, waits for them, and re-layouts  0.73 us (1%)
    pallas_call x6, Pallas kernels, call(): pl.pallas_call(kernel, out_shape=out_shape, grid_spec=pltpu.PrefetchScala...  27.3 us
    pallas_call x1, Pallas kernels, fast_body(): pl.pallas_call(prepare_kernel, out_shape=[jax.ShapeDtypeStruct((row_block...  6.19 us
    ppermute x2, starting transfers between devices, fast_body(): pieces += [lax.ppermute(own_late, 'dp', hop) for hop in along_z[1:]]  3.58 us
    ppermute x3, waiting for transfers between devices, fast_body(): lax.ppermute(parts[q], 'mp', near[q])  2.87 us
    ppermute x1, starting transfers between devices, fast_body(): pieces = [lax.ppermute(own, 'dp', along_z[0])]  2.57 us
    ppermute x1, starting transfers between devices, fast_body(): arrived = lax.ppermute(for_peer, 'dp', across_x)  2.36 us
    ppermute x3, starting transfers between devices, fast_body(): lax.ppermute(parts[q], 'mp', near[q])  1.93 us
    pallas_call x1, Pallas kernels, fast_body(): pl.pallas_call(functools.partial(plan_kernel, cap, col_blocks, row_blocks...  1.72 us
  transfers between devices with their start and end apart: 16, of which 5 were waited for; matrix products, arithmetic and copies ran while one was open for 0% of the time, Pallas kernels for 40%

profile of v5, /device:TPU:0, one launch (start us, length us, event | category | flops | bytes accessed | tf_op | source)
XLA Modules:
  0.0 60.4 jit_solution(8095617419563343739)
XLA Ops:
  0.6 1.5 %stack.1.s0 = bf16[256,256]{1,0:T(8,128)(2,1)} custom-call(bf16[128,256]{1,0:T(8,128)(2,1)} %x_ref.1, bf16[128,256]{1,0:T(8,128)(2,1)} %grad_ref.1), custom_call_target="tpu_custom_call" | custom-call | bytes 262144 | tf_op jit(solution)/shard_map/stack/pallas_call | solution.py:395
  2.2 0.5 collective-permute-start.1
  2.6 2.6 %collective-permute-start = (bf16[256,256]{1,0:T(8,128)(2,1)}, bf16[256,256]{1,0:T(8,128)(2,1)S(1)}, u32[]{:S(2)}, u32[]{:S(2)}) collective-permute-start(bf16[256,256]{1,0:T(8,128)(2,1)} %stack.1.s0), channel_id=1, source_target_pairs={{0,8},{4,12},{8,0},{12,4},{16,24},{20,28},{24,16},{28,20},{1,9},{5... | collective-permute-start | bytes 393224 | tf_op jit(solution)/shard_map/ppermute | solution.py:401
  5.2 0.0 collective-permute-done.1.s1
  5.2 3.6 %collective-permute-start.2 = (bf16[256,256]{1,0:T(8,128)(2,1)}, bf16[256,256]{1,0:T(8,128)(2,1)S(1)}, u32[]{:S(2)}, u32[]{:S(2)}) collective-permute-start(bf16[256,256]{1,0:T(8,128)(2,1)} %stack.1.s0), channel_id=1, source_target_pairs={{0,24},{4,28},{8,16},{12,20},{16,8},{20,12},{24,0},{28,4},{1,25},{... | collective-permute-start | bytes 393224 | tf_op jit(solution)/shard_map/ppermute | solution.py:405
  8.8 0.0 collective-permute-start.3
  8.8 1.5 %collective-permute-start.5 = (bf16[256,256]{1,0:T(8,128)(2,1)}, bf16[256,256]{1,0:T(8,128)(2,1)S(1)}, u32[]{:S(2)}, u32[]{:S(2)}) collective-permute-start(bf16[256,256]{1,0:T(8,128)(2,1)} %stack.1.s0), channel_id=1, source_target_pairs={{0,2},{1,3},{2,0},{3,1},{4,6},{5,7},{6,4},{7,5},{8,10},{9,11},{10,... | collective-permute-start | bytes 393224 | tf_op jit(solution)/shard_map/ppermute | solution.py:403
  10.3 1.2 %collective-permute-start.4 = (bf16[256,256]{1,0:T(8,128)(2,1)S(1)}, bf16[256,256]{1,0:T(8,128)(2,1)S(1)}, u32[]{:S(2)}, u32[]{:S(2)}) collective-permute-start(bf16[256,256]{1,0:T(8,128)(2,1)S(1)} %collective-permute-done.s0), channel_id=1, source_target_pairs={{0,2},{1,3},{2,0},{3,1},{4,6},{5,7},{6,4},{7,5},{8,10},{9,11},{10,... | collective-permute-start | bytes 393224 | tf_op jit(solution)/shard_map/ppermute | solution.py:413
  11.5 1.7 %plan.1.plan_ref = s32[8,256]{1,0:T(8,128)} custom-call(s32[1,256]{1,0:T(1,128)} %cols_ref, s32[1,256]{1,0:T(1,128)} %slots_ref), custom_call_target="tpu_custom_call" | custom-call | flops 4000000 | bytes 16384 | tf_op jit(solution)/shard_map/plan/pallas_call | solution.py:407
  13.2 0.7 %copy-done.1 = s32[8,256]{1,0:T(8,128)S(1)} copy-done((s32[8,256]{1,0:T(8,128)S(1)}, s32[8,256]{1,0:T(8,128)}, u32[]{:S(2)}) %copy-start.1) | copy-done | bytes 8216
  13.9 6.2 %prepare.1 = (bf16[16,512,128]{2,1,0:T(8,128)(2,1)S(1)}, bf16[16,64,1024]{2,1,0:T(8,128)(2,1)S(1)}, bf16[16,512,128]{2,1,0:T(8,128)(2,1)S(1)}, bf16[16,64,1024]{2,1,0:T(8,128)(2,1)S(1)}) custom-call(s32[8,256]{1,0:T(8,128)S(1)} %copy-done.1, bf16[256,4096]{1,0:T(8,128)(2,1)} %win_ref.1, bf16[256,4096]{1,0:T(8,128)(2,1)} %wout_ref.1), custom_call_target="tpu_custom_call" | custom-call | flops 2147483648 | bytes 12582912 | tf_op jit(solution)/shard_map/prepare/pallas_call | solution.py:423
  20.1 0.0 collective-permute-done.2
  20.2 0.2 collective-permute-done.3
  20.4 0.0 collective-permute-done.6.s3
  20.4 0.0 collective-permute-done.4.s2
  20.4 1.6 %collective-permute-start.10 = (bf16[512,256]{1,0:T(8,128)(2,1)S(1)}, bf16[512,256]{1,0:T(8,128)(2,1)S(1)}, u32[]{:S(2)}, u32[]{:S(2)}) collective-permute-start(bf16[512,256]{1,0:T(8,128)(2,1)S(1)} %constant_dynamic-update-slice_fusion.s0), channel_id=1, source_target_pairs={{0,2},{1,3},{2,0},{3,1},{4,6},{5,7},{6,4},{7,5},{8,10},{9,11},{10,... | collective-permute-start | bytes 786440 | tf_op jit(solution)/shard_map/ppermute | solution.py:449
  22.0 0.5 collective-permute-start.7
  22.5 6.0 %local_kernel.1 = (bf16[128,64,128]{2,1,0:T(8,128)(2,1)S(1)}, bf16[128,64,128]{2,1,0:T(8,128)(2,1)S(1)}, bf16[128,1024]{1,0:T(8,128)(2,1)S(1)}) custom-call(s32[8,256]{1,0:T(8,128)S(1)} %copy-done.2, f32[1,1024]{1,0:T(1,128)S(1)} %bitcast.2, bf16[256,256]{1,0:T(8,128)(2,1)S(1)} %copy-done, bf16[256,256]{1,0:T(8,128)(2,1)S(1)} %collective-permute-done.1.s1, ...), custom_call_target="tpu_custom_call" | custom-call | flops 2147483648 | bytes 4194304 | tf_op jit(solution)/shard_map/local_kernel/pallas_call | solution.py:467
  28.5 0.6 %collective-permute-done.10.s2 = bf16[512,256]{1,0:T(8,128)(2,1)S(1)} collective-permute-done((bf16[512,256]{1,0:T(8,128)(2,1)S(1)}, bf16[512,256]{1,0:T(8,128)(2,1)S(1)}, u32[]{:S(2)}, u32[]{:S(2)}) %collective-permute-start.10) | collective-permute-done | bytes 262176 | tf_op jit(solution)/shard_map/ppermute | solution.py:449
  29.2 4.5 %chunk_kernel.2 = (bf16[1,128,64,128]{3,2,1,0:T(8,128)(2,1)S(1)}, bf16[128,1024]{1,0:T(8,128)(2,1)S(1)}) custom-call(s32[8,256]{1,0:T(8,128)S(1)} %copy-done.2, f32[1,1024]{1,0:T(1,128)S(1)} %bitcast.3, bf16[256,256]{1,0:T(8,128)(2,1)S(1)} %collective-permute-done.s0, bf16[256,256]{1,0:T(8,128)(2,1)S(1)} %collective-permute-done.7.s1, ...), custom_call_target="tpu_custom_call" | custom-call | flops 2147483648 | bytes 4194304 | tf_op jit(solution)/shard_map/chunk_kernel/pallas_call | solution.py:467
  33.6 8.3 %chunk_kernel.3 = (bf16[2,128,64,128]{3,2,1,0:T(8,128)(2,1)S(1)}, bf16[256,1024]{1,0:T(8,128)(2,1)S(1)}) custom-call(s32[8,256]{1,0:T(8,128)S(1)} %copy-done.2, f32[1,1024]{1,0:T(1,128)S(1)} %bitcast.4, bf16[512,256]{1,0:T(8,128)(2,1)S(1)} %constant_dynamic-update-slice_fusion.s0, bf16[512,256]{1,0:T(8,128)(2,1)S(1)} %collective-permute-done.9.s1, ...), custom_call_target="tpu_custom_call" | custom-call | flops 4294967296 | bytes 8388608 | tf_op jit(solution)/shard_map/chunk_kernel/pallas_call | solution.py:467
  41.9 2.7 %block_kernel.2 = bf16[65,32,128]{2,1,0:T(8,128)(2,1)S(1)} custom-call(s32[8,256]{1,0:T(8,128)S(1)} %copy-done.2, bf16[128,64,128]{2,1,0:T(8,128)(2,1)S(1)} %get-tuple-element.52.gp0.gp_ref, bf16[1,128,64,128]{3,2,1,0:T(8,128)(2,1)S(1)} %get-tuple-element.55.gp1, bf16[2,128,64,128]{3,2,1,0:T(8,128)(2,1)S(1)} %get-tuple-element.60.gp2, ...), custom_call_target="tpu_custom_call" | custom-call | flops 536870912 | bytes 1048576 | tf_op jit(solution)/shard_map/block_kernel/pallas_call | solution.py:467
  44.6 2.4 %collective-permute-start.12 = (bf16[65,32,128]{2,1,0:T(8,128)(2,1)S(1)}, bf16[65,32,128]{2,1,0:T(8,128)(2,1)S(1)}, u32[]{:S(2)}, u32[]{:S(2)}) collective-permute-start(bf16[65,32,128]{2,1,0:T(8,128)(2,1)S(1)} %block_kernel.2), channel_id=1, source_target_pairs={{0,4},{4,0},{8,12},{12,8},{16,20},{20,16},{24,28},{28,24},{1,5},{5... | collective-permute-start | bytes 1597448 | tf_op jit(solution)/shard_map/ppermute | solution.py:515
  46.9 2.4 %contract_kernel.1 = (bf16[256,256]{1,0:T(8,128)(2,1)S(1)}, bf16[256,256]{1,0:T(8,128)(2,1)S(1)}, bf16[256,256]{1,0:T(8,128)(2,1)S(1)}, bf16[256,256]{1,0:T(8,128)(2,1)S(1)}) custom-call(s32[8,256]{1,0:T(8,128)S(1)} %copy-done.2, bf16[128,64,128]{2,1,0:T(8,128)(2,1)S(1)} %get-tuple-element.67.act_ref, ...), custom_call_target="tpu_custom_call" | custom-call | tf_op jit(solution)/shard_map/contract_kernel/pallas_call | solution.py:467
  49.3 0.1 collective-permute-start.13
  49.4 0.1 collective-permute-start.14
  49.5 1.8 %collective-permute-start.15 = (bf16[256,256]{1,0:T(8,128)(2,1)S(1)}, bf16[256,256]{1,0:T(8,128)(2,1)S(1)}, u32[]{:S(2)}, u32[]{:S(2)}) collective-permute-start(bf16[256,256]{1,0:T(8,128)(2,1)S(1)} %get-tuple-element.73), channel_id=1, source_target_pairs={{0,3},{1,2},{2,1},{3,0},{4,7},{5,6},{6,5},{7,4},{8,11},{9,10},{10,... | collective-permute-start | bytes 393224 | tf_op jit(solution)/shard_map/ppermute | solution.py:524
  51.3 3.5 %block_kernel.3.own_ref = f32[65,32,128]{2,1,0:T(8,128)S(1)} custom-call(s32[8,256]{1,0:T(8,128)S(1)} %copy-done.2, bf16[128,64,128]{2,1,0:T(8,128)(2,1)S(1)} %get-tuple-element.52.gp0.gp_ref, bf16[1,128,64,128]{3,2,1,0:T(8,128)(2,1)S(1)} %get-tuple-element.55.gp1, bf16[2,128,64,128]{3,2,1,0:T(8,128)(2,1)S(1)} %get-tuple-element.60.gp2, ...), custom_call_target="tpu_custom_call" | custom-call | tf_op jit(solution)/shard_map/block_kernel/pallas_call | solution.py:467
  54.8 1.0 %collective-permute-done.14.s2 = bf16[256,256]{1,0:T(8,128)(2,1)S(1)} collective-permute-done((bf16[256,256]{1,0:T(8,128)(2,1)S(1)}, bf16[256,256]{1,0:T(8,128)(2,1)S(1)}, u32[]{:S(2)}, u32[]{:S(2)}) %collective-permute-start.14) | collective-permute-done | bytes 131104 | tf_op jit(solution)/shard_map/ppermute | solution.py:524
  55.8 1.9 %collective-permute-done.15.s3 = bf16[256,256]{1,0:T(8,128)(2,1)S(1)} collective-permute-done((bf16[256,256]{1,0:T(8,128)(2,1)S(1)}, bf16[256,256]{1,0:T(8,128)(2,1)S(1)}, u32[]{:S(2)}, u32[]{:S(2)}) %collective-permute-start.15) | collective-permute-done | bytes 131104 | tf_op jit(solution)/shard_map/ppermute | solution.py:524
  57.7 1.5 %collective-permute-done.12.arrived_ref = bf16[65,32,128]{2,1,0:T(8,128)(2,1)S(1)} collective-permute-done((bf16[65,32,128]{2,1,0:T(8,128)(2,1)S(1)}, bf16[65,32,128]{2,1,0:T(8,128)(2,1)S(1)}, u32[]{:S(2)}, u32[]{:S(2)}) %collective-permute-start.12) | collective-permute-done | bytes 532512 | tf_op jit(solution)/shard_map/ppermute | solution.py:515
  59.2 1.2 %finish.1 = (bf16[128,256]{1,0:T(8,128)(2,1)}, bf16[128,256]{1,0:T(8,128)(2,1)}, f32[64,4096]{1,0:T(8,128)}) custom-call(f32[65,32,128]{2,1,0:T(8,128)S(1)} %block_kernel.3.own_ref, bf16[65,32,128]{2,1,0:T(8,128)(2,1)S(1)} %collective-permute-done.12.arrived_ref, bf16[256,256]{1,0:T(8,128)(2,1)S(1)} %get-tuple-element.70.s0, ...), custom_call_target="tpu_custom_call" | custom-call | tf_op jit(solution)/shard_map/finish/pallas_call | solution.py:529
  (20 shorter events, 0.1 us)
Async XLA Ops:
  2.2 3.0 %collective-permute-start.1 = (bf16[256,256]{1,0:T(8,128)(2,1)}, bf16[256,256]{1,0:T(8,128)(2,1)S(1)}, u32[]{:S(2)}, u32[]{:S(2)}) collective-permute-start(bf16[256,256]{1,0:T(8,128)(2,1)} %stack.1.s0), channel_id=1, source_target_pairs={{0,1},{1,0},{2,3},{3,2},{4,5},{5,4},{6,7},{7,6},{8,9},{9,8},{10,11... | collective-permute-start | bytes 393224 | tf_op jit(solution)/shard_map/ppermute | solution.py:402
  2.6 7.7 %collective-permute-start = (bf16[256,256]{1,0:T(8,128)(2,1)}, bf16[256,256]{1,0:T(8,128)(2,1)S(1)}, u32[]{:S(2)}, u32[]{:S(2)}) collective-permute-start(bf16[256,256]{1,0:T(8,128)(2,1)} %stack.1.s0), channel_id=1, source_target_pairs={{0,8},{4,12},{8,0},{12,4},{16,24},{20,28},{24,16},{28,20},{1,9},{5... | collective-permute-start | bytes 393224 | tf_op jit(solution)/shard_map/ppermute | solution.py:401
  5.2 14.9 %collective-permute-start.2 = (bf16[256,256]{1,0:T(8,128)(2,1)}, bf16[256,256]{1,0:T(8,128)(2,1)S(1)}, u32[]{:S(2)}, u32[]{:S(2)}) collective-permute-start(bf16[256,256]{1,0:T(8,128)(2,1)} %stack.1.s0), channel_id=1, source_target_pairs={{0,24},{4,28},{8,16},{12,20},{16,8},{20,12},{24,0},{28,4},{1,25},{... | collective-permute-start | bytes 393224 | tf_op jit(solution)/shard_map/ppermute | solution.py:405
  8.8 11.6 %collective-permute-start.3 = (bf16[256,256]{1,0:T(8,128)(2,1)}, bf16[256,256]{1,0:T(8,128)(2,1)S(1)}, u32[]{:S(2)}, u32[]{:S(2)}) collective-permute-start(bf16[256,256]{1,0:T(8,128)(2,1)} %stack.1.s0), channel_id=1, source_target_pairs={{0,16},{4,20},{8,24},{12,28},{16,0},{20,4},{24,8},{28,12},{1,17},{... | collective-permute-start | bytes 393224 | tf_op jit(solution)/shard_map/ppermute | solution.py:405
  8.8 11.6 %collective-permute-start.5 = (bf16[256,256]{1,0:T(8,128)(2,1)}, bf16[256,256]{1,0:T(8,128)(2,1)S(1)}, u32[]{:S(2)}, u32[]{:S(2)}) collective-permute-start(bf16[256,256]{1,0:T(8,128)(2,1)} %stack.1.s0), channel_id=1, source_target_pairs={{0,2},{1,3},{2,0},{3,1},{4,6},{5,7},{6,4},{7,5},{8,10},{9,11},{10,... | collective-permute-start | bytes 393224 | tf_op jit(solution)/shard_map/ppermute | solution.py:403
  10.3 10.1 %collective-permute-start.6 = (bf16[256,256]{1,0:T(8,128)(2,1)}, bf16[256,256]{1,0:T(8,128)(2,1)S(1)}, u32[]{:S(2)}, u32[]{:S(2)}) collective-permute-start(bf16[256,256]{1,0:T(8,128)(2,1)} %stack.1.s0), channel_id=1, source_target_pairs={{0,3},{1,2},{2,1},{3,0},{4,7},{5,6},{6,5},{7,4},{8,11},{9,10},{10,... | collective-permute-start | bytes 393224 | tf_op jit(solution)/shard_map/ppermute | solution.py:404
  10.3 10.1 %collective-permute-start.4 = (bf16[256,256]{1,0:T(8,128)(2,1)S(1)}, bf16[256,256]{1,0:T(8,128)(2,1)S(1)}, u32[]{:S(2)}, u32[]{:S(2)}) collective-permute-start(bf16[256,256]{1,0:T(8,128)(2,1)S(1)} %collective-permute-done.s0), channel_id=1, source_target_pairs={{0,2},{1,3},{2,0},{3,1},{4,6},{5,7},{6,4},{7,5},{8,10},{9,11},{10,... | collective-permute-start | bytes 393224 | tf_op jit(solution)/shard_map/ppermute | solution.py:413
  13.2 0.7 %copy-start.1 = (s32[8,256]{1,0:T(8,128)S(1)}, s32[8,256]{1,0:T(8,128)}, u32[]{:S(2)}) copy-start(s32[8,256]{1,0:T(8,128)} %plan.1.plan_ref) | copy-start | bytes 24580
  13.9 8.6 %copy-start = (bf16[256,256]{1,0:T(8,128)(2,1)S(1)}, bf16[256,256]{1,0:T(8,128)(2,1)}, u32[]{:S(2)}) copy-start(bf16[256,256]{1,0:T(8,128)(2,1)} %stack.1.s0) | copy-start | bytes 393220
  13.9 8.6 %copy-start.2 = (s32[8,256]{1,0:T(8,128)S(1)}, s32[8,256]{1,0:T(8,128)}, u32[]{:S(2)}) copy-start(s32[8,256]{1,0:T(8,128)} %plan.1.plan_ref) | copy-start | bytes 24580
  13.9 8.6 %copy-start.3 = (f32[1024]{0:T(1024)S(1)}, f32[1024]{0:T(1024)}, u32[]{:S(2)}) copy-start(f32[1024]{0:T(1024)} %param.8) | copy-start | bytes 12292
  20.4 8.7 %collective-permute-start.10 = (bf16[512,256]{1,0:T(8,128)(2,1)S(1)}, bf16[512,256]{1,0:T(8,128)(2,1)S(1)}, u32[]{:S(2)}, u32[]{:S(2)}) collective-permute-start(bf16[512,256]{1,0:T(8,128)(2,1)S(1)} %constant_dynamic-update-slice_fusion.s0), channel_id=1, source_target_pairs={{0,2},{1,3},{2,0},{3,1},{4,6},{5,7},{6,4},{7,5},{8,10},{9,11},{10,... | collective-permute-start | bytes 786440 | tf_op jit(solution)/shard_map/ppermute | solution.py:449
  22.0 11.6 %collective-permute-start.9 = (bf16[512,256]{1,0:T(8,128)(2,1)S(1)}, bf16[512,256]{1,0:T(8,128)(2,1)S(1)}, u32[]{:S(2)}, u32[]{:S(2)}) collective-permute-start(bf16[512,256]{1,0:T(8,128)(2,1)S(1)} %constant_dynamic-update-slice_fusion.s0), channel_id=1, source_target_pairs={{0,1},{1,0},{2,3},{3,2},{4,5},{5,4},{6,7},{7,6},{8,9},{9,8},{10,11... | collective-permute-start | bytes 786440 | tf_op jit(solution)/shard_map/ppermute | solution.py:449
  22.0 7.1 %collective-permute-start.7 = (bf16[256,256]{1,0:T(8,128)(2,1)S(1)}, bf16[256,256]{1,0:T(8,128)(2,1)S(1)}, u32[]{:S(2)}, u32[]{:S(2)}) collective-permute-start(bf16[256,256]{1,0:T(8,128)(2,1)S(1)} %collective-permute-done.s0), channel_id=1, source_target_pairs={{0,1},{1,0},{2,3},{3,2},{4,5},{5,4},{6,7},{7,6},{8,9},{9,8},{10,11... | collective-permute-start | bytes 393224 | tf_op jit(solution)/shard_map/ppermute | solution.py:452
  22.5 6.6 %collective-permute-start.8 = (bf16[256,256]{1,0:T(8,128)(2,1)S(1)}, bf16[256,256]{1,0:T(8,128)(2,1)S(1)}, u32[]{:S(2)}, u32[]{:S(2)}) collective-permute-start(bf16[256,256]{1,0:T(8,128)(2,1)S(1)} %collective-permute-done.4.s2), channel_id=1, source_target_pairs={{0,1},{1,0},{2,3},{3,2},{4,5},{5,4},{6,7},{7,6},{8,9},{9,8},{10,11... | collective-permute-start | bytes 393224 | tf_op jit(solution)/shard_map/ppermute | solution.py:454
  29.2 4.5 %collective-permute-start.11 = (bf16[512,256]{1,0:T(8,128)(2,1)S(1)}, bf16[512,256]{1,0:T(8,128)(2,1)S(1)}, u32[]{:S(2)}, u32[]{:S(2)}) collective-permute-start(bf16[512,256]{1,0:T(8,128)(2,1)S(1)} %collective-permute-done.10.s2), channel_id=1, source_target_pairs={{0,1},{1,0},{2,3},{3,2},{4,5},{5,4},{6,7},{7,6},{8,9},{9,8},{10,11... | collective-permute-start | bytes 786440 | tf_op jit(solution)/shard_map/ppermute | solution.py:494
  44.6 14.6 %collective-permute-start.12 = (bf16[65,32,128]{2,1,0:T(8,128)(2,1)S(1)}, bf16[65,32,128]{2,1,0:T(8,128)(2,1)S(1)}, u32[]{:S(2)}, u32[]{:S(2)}) collective-permute-start(bf16[65,32,128]{2,1,0:T(8,128)(2,1)S(1)} %block_kernel.2), channel_id=1, source_target_pairs={{0,4},{4,0},{8,12},{12,8},{16,20},{20,16},{24,28},{28,24},{1,5},{5... | collective-permute-start | bytes 1597448 | tf_op jit(solution)/shard_map/ppermute | solution.py:515
  49.3 5.5 %collective-permute-start.13 = (bf16[256,256]{1,0:T(8,128)(2,1)S(1)}, bf16[256,256]{1,0:T(8,128)(2,1)S(1)}, u32[]{:S(2)}, u32[]{:S(2)}) collective-permute-start(bf16[256,256]{1,0:T(8,128)(2,1)S(1)} %get-tuple-element.71), channel_id=1, source_target_pairs={{0,1},{1,0},{2,3},{3,2},{4,5},{5,4},{6,7},{7,6},{8,9},{9,8},{10,11... | collective-permute-start | bytes 393224 | tf_op jit(solution)/shard_map/ppermute | solution.py:524
  49.4 6.4 %collective-permute-start.14 = (bf16[256,256]{1,0:T(8,128)(2,1)S(1)}, bf16[256,256]{1,0:T(8,128)(2,1)S(1)}, u32[]{:S(2)}, u32[]{:S(2)}) collective-permute-start(bf16[256,256]{1,0:T(8,128)(2,1)S(1)} %get-tuple-element.72), channel_id=1, source_target_pairs={{0,2},{1,3},{2,0},{3,1},{4,6},{5,7},{6,4},{7,5},{8,10},{9,11},{10,... | collective-permute-start | bytes 393224 | tf_op jit(solution)/shard_map/ppermute | solution.py:524
  49.5 8.2 %collective-permute-start.15 = (bf16[256,256]{1,0:T(8,128)(2,1)S(1)}, bf16[256,256]{1,0:T(8,128)(2,1)S(1)}, u32[]{:S(2)}, u32[]{:S(2)}) collective-permute-start(bf16[256,256]{1,0:T(8,128)(2,1)S(1)} %get-tuple-element.73), channel_id=1, source_target_pairs={{0,3},{1,2},{2,1},{3,0},{4,7},{5,6},{6,5},{7,4},{8,11},{9,10},{10,... | collective-permute-start | bytes 393224 | tf_op jit(solution)/shard_map/ppermute | solution.py:524

commit v6 on v5

--- a/solution.py
+++ b/solution.py
@@ -14,7 +14,7 @@
 GROUP = 4
 FIRST = 1024
 BATCH = 10
-BEND = 8
+BEND = 16
 
 
 norm_eps = 1e-06

time: 60.6 us -> 60.8 us (level)
  waiting for transfers between devices: 5.22 us -> 6.46 us
  Pallas kernels: 37.9 us -> 37.2 us
    ppermute x1, waiting for transfers between devices: 1.47 us -> 2.31 us  [fast_body(): arrived = lax.ppermute(for_peer, 'dp', across_x)]
    ppermute x1, starting transfers between devices: 2.36 us -> 1.56 us  [fast_body(): arrived = lax.ppermute(for_peer, 'dp', across_x)]
    pallas_call x6, Pallas kernels: 27.3 us -> 26.5 us  [call(): pl.pallas_call(kernel, out_shape=out_shape, grid_spec=pltpu.PrefetchScala...]
  transfers between devices with their start and end apart: 16 -> 16, of which waited for: 5 -> 5; matrix products, arithmetic and copies ran while one was open for 0% -> 0% of each run, Pallas kernels for 40% -> 39%
where the time goes in v6:
time: 60.8 us; the launch traced here: 60.5 us
  Pallas kernels  37.2 us (61%)
  starting transfers between devices  15.3 us (25%)
  waiting for transfers between devices  6.46 us (11%)
  between operations  0.77 us (1%)
  local copies, waits for them, and re-layouts  0.73 us (1%)
    pallas_call x6, Pallas kernels, call(): pl.pallas_call(kernel, out_shape=out_shape, grid_spec=pltpu.PrefetchScala...  26.5 us
    pallas_call x1, Pallas kernels, fast_body(): pl.pallas_call(prepare_kernel, out_shape=[jax.ShapeDtypeStruct((row_block...  6.19 us
    ppermute x2, starting transfers between devices, fast_body(): pieces += [lax.ppermute(own_late, 'dp', hop) for hop in along_z[1:]]  3.58 us
    ppermute x3, waiting for transfers between devices, fast_body(): lax.ppermute(parts[q], 'mp', near[q])  3.27 us
    ppermute x1, starting transfers between devices, fast_body(): pieces = [lax.ppermute(own, 'dp', along_z[0])]  2.57 us
    ppermute x3, starting transfers between devices, fast_body(): lax.ppermute(parts[q], 'mp', near[q])  2.32 us
    ppermute x1, waiting for transfers between devices, fast_body(): arrived = lax.ppermute(for_peer, 'dp', across_x)  2.31 us
    pallas_call x1, Pallas kernels, fast_body(): pl.pallas_call(functools.partial(plan_kernel, cap, col_blocks, row_blocks...  1.72 us
  transfers between devices with their start and end apart: 16, of which 5 were waited for; matrix products, arithmetic and copies ran while one was open for 0% of the time, Pallas kernels for 39%

profile of v6, /device:TPU:0, one launch (start us, length us, event | category | flops | bytes accessed | tf_op | source)
XLA Modules:
  0.0 60.5 jit_solution(3944799715319043556)
XLA Ops:
  0.6 1.5 %stack.1.s0 = bf16[256,256]{1,0:T(8,128)(2,1)} custom-call(bf16[128,256]{1,0:T(8,128)(2,1)} %x_ref.1, bf16[128,256]{1,0:T(8,128)(2,1)} %grad_ref.1), custom_call_target="tpu_custom_call" | custom-call | bytes 262144 | tf_op jit(solution)/shard_map/stack/pallas_call | solution.py:395
  2.2 0.5 collective-permute-start.1
  2.6 2.6 %collective-permute-start = (bf16[256,256]{1,0:T(8,128)(2,1)}, bf16[256,256]{1,0:T(8,128)(2,1)S(1)}, u32[]{:S(2)}, u32[]{:S(2)}) collective-permute-start(bf16[256,256]{1,0:T(8,128)(2,1)} %stack.1.s0), channel_id=1, source_target_pairs={{0,8},{4,12},{8,0},{12,4},{16,24},{20,28},{24,16},{28,20},{1,9},{5... | collective-permute-start | bytes 393224 | tf_op jit(solution)/shard_map/ppermute | solution.py:401
  5.2 3.6 %collective-permute-start.2 = (bf16[256,256]{1,0:T(8,128)(2,1)}, bf16[256,256]{1,0:T(8,128)(2,1)S(1)}, u32[]{:S(2)}, u32[]{:S(2)}) collective-permute-start(bf16[256,256]{1,0:T(8,128)(2,1)} %stack.1.s0), channel_id=1, source_target_pairs={{0,24},{4,28},{8,16},{12,20},{16,8},{20,12},{24,0},{28,4},{1,25},{... | collective-permute-start | bytes 393224 | tf_op jit(solution)/shard_map/ppermute | solution.py:405
  8.8 1.5 %collective-permute-start.5 = (bf16[256,256]{1,0:T(8,128)(2,1)}, bf16[256,256]{1,0:T(8,128)(2,1)S(1)}, u32[]{:S(2)}, u32[]{:S(2)}) collective-permute-start(bf16[256,256]{1,0:T(8,128)(2,1)} %stack.1.s0), channel_id=1, source_target_pairs={{0,2},{1,3},{2,0},{3,1},{4,6},{5,7},{6,4},{7,5},{8,10},{9,11},{10,... | collective-permute-start | bytes 393224 | tf_op jit(solution)/shard_map/ppermute | solution.py:403
  10.3 0.0 collective-permute-start.6
  10.3 0.0 collective-permute-done.s0
  10.3 1.2 %collective-permute-start.4 = (bf16[256,256]{1,0:T(8,128)(2,1)S(1)}, bf16[256,256]{1,0:T(8,128)(2,1)S(1)}, u32[]{:S(2)}, u32[]{:S(2)}) collective-permute-start(bf16[256,256]{1,0:T(8,128)(2,1)S(1)} %collective-permute-done.s0), channel_id=1, source_target_pairs={{0,2},{1,3},{2,0},{3,1},{4,6},{5,7},{6,4},{7,5},{8,10},{9,11},{10,... | collective-permute-start | bytes 393224 | tf_op jit(solution)/shard_map/ppermute | solution.py:413
  11.5 1.7 %plan.1.plan_ref = s32[8,256]{1,0:T(8,128)} custom-call(s32[1,256]{1,0:T(1,128)} %cols_ref, s32[1,256]{1,0:T(1,128)} %slots_ref), custom_call_target="tpu_custom_call" | custom-call | flops 4000000 | bytes 16384 | tf_op jit(solution)/shard_map/plan/pallas_call | solution.py:407
  13.2 0.7 %copy-done.1 = s32[8,256]{1,0:T(8,128)S(1)} copy-done((s32[8,256]{1,0:T(8,128)S(1)}, s32[8,256]{1,0:T(8,128)}, u32[]{:S(2)}) %copy-start.1) | copy-done | bytes 8216
  13.9 6.2 %prepare.1 = (bf16[16,512,128]{2,1,0:T(8,128)(2,1)S(1)}, bf16[16,64,1024]{2,1,0:T(8,128)(2,1)S(1)}, bf16[16,512,128]{2,1,0:T(8,128)(2,1)S(1)}, bf16[16,64,1024]{2,1,0:T(8,128)(2,1)S(1)}) custom-call(s32[8,256]{1,0:T(8,128)S(1)} %copy-done.1, bf16[256,4096]{1,0:T(8,128)(2,1)} %win_ref.1, bf16[256,4096]{1,0:T(8,128)(2,1)} %wout_ref.1), custom_call_target="tpu_custom_call" | custom-call | flops 2147483648 | bytes 12582912 | tf_op jit(solution)/shard_map/prepare/pallas_call | solution.py:423
  20.2 0.2 collective-permute-done.3
  20.4 0.0 collective-permute-done.5.s2
  20.4 0.0 collective-permute-done.6.s3
  20.4 1.6 %collective-permute-start.10 = (bf16[512,256]{1,0:T(8,128)(2,1)S(1)}, bf16[512,256]{1,0:T(8,128)(2,1)S(1)}, u32[]{:S(2)}, u32[]{:S(2)}) collective-permute-start(bf16[512,256]{1,0:T(8,128)(2,1)S(1)} %constant_dynamic-update-slice_fusion.s0), channel_id=1, source_target_pairs={{0,2},{1,3},{2,0},{3,1},{4,6},{5,7},{6,4},{7,5},{8,10},{9,11},{10,... | collective-permute-start | bytes 786440 | tf_op jit(solution)/shard_map/ppermute | solution.py:449
  22.0 0.0 collective-permute-start.9
  22.0 0.5 collective-permute-start.7
  22.5 6.0 %local_kernel.1 = (bf16[128,64,128]{2,1,0:T(8,128)(2,1)S(1)}, bf16[128,64,128]{2,1,0:T(8,128)(2,1)S(1)}, bf16[128,1024]{1,0:T(8,128)(2,1)S(1)}) custom-call(s32[8,256]{1,0:T(8,128)S(1)} %copy-done.2, f32[1,1024]{1,0:T(1,128)S(1)} %bitcast.2, bf16[256,256]{1,0:T(8,128)(2,1)S(1)} %copy-done, bf16[256,256]{1,0:T(8,128)(2,1)S(1)} %collective-permute-done.1.s1, ...), custom_call_target="tpu_custom_call" | custom-call | flops 2147483648 | bytes 4194304 | tf_op jit(solution)/shard_map/local_kernel/pallas_call | solution.py:467
  28.5 0.6 %collective-permute-done.10.s2 = bf16[512,256]{1,0:T(8,128)(2,1)S(1)} collective-permute-done((bf16[512,256]{1,0:T(8,128)(2,1)S(1)}, bf16[512,256]{1,0:T(8,128)(2,1)S(1)}, u32[]{:S(2)}, u32[]{:S(2)}) %collective-permute-start.10) | collective-permute-done | bytes 262176 | tf_op jit(solution)/shard_map/ppermute | solution.py:449
  29.2 0.0 collective-permute-start.11
  29.2 4.6 %chunk_kernel.2 = (bf16[1,128,64,128]{3,2,1,0:T(8,128)(2,1)S(1)}, bf16[128,1024]{1,0:T(8,128)(2,1)S(1)}) custom-call(s32[8,256]{1,0:T(8,128)S(1)} %copy-done.2, f32[1,1024]{1,0:T(1,128)S(1)} %bitcast.3, bf16[256,256]{1,0:T(8,128)(2,1)S(1)} %collective-permute-done.s0, bf16[256,256]{1,0:T(8,128)(2,1)S(1)} %collective-permute-done.7.s1, ...), custom_call_target="tpu_custom_call" | custom-call | flops 2147483648 | bytes 4194304 | tf_op jit(solution)/shard_map/chunk_kernel/pallas_call | solution.py:467
  33.8 8.2 %chunk_kernel.3 = (bf16[2,128,64,128]{3,2,1,0:T(8,128)(2,1)S(1)}, bf16[256,1024]{1,0:T(8,128)(2,1)S(1)}) custom-call(s32[8,256]{1,0:T(8,128)S(1)} %copy-done.2, f32[1,1024]{1,0:T(1,128)S(1)} %bitcast.4, bf16[512,256]{1,0:T(8,128)(2,1)S(1)} %constant_dynamic-update-slice_fusion.s0, bf16[512,256]{1,0:T(8,128)(2,1)S(1)} %collective-permute-done.9.s1, ...), custom_call_target="tpu_custom_call" | custom-call | flops 4294967296 | bytes 8388608 | tf_op jit(solution)/shard_map/chunk_kernel/pallas_call | solution.py:467
  42.0 2.7 %block_kernel.2 = bf16[65,32,128]{2,1,0:T(8,128)(2,1)S(1)} custom-call(s32[8,256]{1,0:T(8,128)S(1)} %copy-done.2, bf16[128,64,128]{2,1,0:T(8,128)(2,1)S(1)} %get-tuple-element.52.gp0.gp_ref, bf16[1,128,64,128]{3,2,1,0:T(8,128)(2,1)S(1)} %get-tuple-element.55.gp1, bf16[2,128,64,128]{3,2,1,0:T(8,128)(2,1)S(1)} %get-tuple-element.60.gp2, ...), custom_call_target="tpu_custom_call" | custom-call | flops 536870912 | bytes 1048576 | tf_op jit(solution)/shard_map/block_kernel/pallas_call | solution.py:467
  44.7 1.6 %collective-permute-start.12 = (bf16[65,32,128]{2,1,0:T(8,128)(2,1)S(1)}, bf16[65,32,128]{2,1,0:T(8,128)(2,1)S(1)}, u32[]{:S(2)}, u32[]{:S(2)}) collective-permute-start(bf16[65,32,128]{2,1,0:T(8,128)(2,1)S(1)} %block_kernel.2), channel_id=1, source_target_pairs={{0,4},{4,0},{8,12},{12,8},{16,20},{20,16},{24,28},{28,24},{1,5},{5... | collective-permute-start | bytes 1597448 | tf_op jit(solution)/shard_map/ppermute | solution.py:515
  46.2 2.4 %contract_kernel.1 = (bf16[256,256]{1,0:T(8,128)(2,1)S(1)}, bf16[256,256]{1,0:T(8,128)(2,1)S(1)}, bf16[256,256]{1,0:T(8,128)(2,1)S(1)}, bf16[256,256]{1,0:T(8,128)(2,1)S(1)}) custom-call(s32[8,256]{1,0:T(8,128)S(1)} %copy-done.2, bf16[128,64,128]{2,1,0:T(8,128)(2,1)S(1)} %get-tuple-element.67.act_ref, ...), custom_call_target="tpu_custom_call" | custom-call | tf_op jit(solution)/shard_map/contract_kernel/pallas_call | solution.py:467
  48.6 0.3 collective-permute-start.13
  48.9 2.0 %collective-permute-start.14 = (bf16[256,256]{1,0:T(8,128)(2,1)S(1)}, bf16[256,256]{1,0:T(8,128)(2,1)S(1)}, u32[]{:S(2)}, u32[]{:S(2)}) collective-permute-start(bf16[256,256]{1,0:T(8,128)(2,1)S(1)} %get-tuple-element.72), channel_id=1, source_target_pairs={{0,2},{1,3},{2,0},{3,1},{4,6},{5,7},{6,4},{7,5},{8,10},{9,11},{10,... | collective-permute-start | bytes 393224 | tf_op jit(solution)/shard_map/ppermute | solution.py:524
  51.0 2.7 %block_kernel.3.own_ref = f32[65,32,128]{2,1,0:T(8,128)S(1)} custom-call(s32[8,256]{1,0:T(8,128)S(1)} %copy-done.2, bf16[128,64,128]{2,1,0:T(8,128)(2,1)S(1)} %get-tuple-element.52.gp0.gp_ref, bf16[1,128,64,128]{3,2,1,0:T(8,128)(2,1)S(1)} %get-tuple-element.55.gp1, bf16[2,128,64,128]{3,2,1,0:T(8,128)(2,1)S(1)} %get-tuple-element.60.gp2, ...), custom_call_target="tpu_custom_call" | custom-call | tf_op jit(solution)/shard_map/block_kernel/pallas_call | solution.py:467
  53.7 1.6 %collective-permute-done.14.s2 = bf16[256,256]{1,0:T(8,128)(2,1)S(1)} collective-permute-done((bf16[256,256]{1,0:T(8,128)(2,1)S(1)}, bf16[256,256]{1,0:T(8,128)(2,1)S(1)}, u32[]{:S(2)}, u32[]{:S(2)}) %collective-permute-start.14) | collective-permute-done | bytes 131104 | tf_op jit(solution)/shard_map/ppermute | solution.py:524
  55.3 1.7 %collective-permute-done.15.s3 = bf16[256,256]{1,0:T(8,128)(2,1)S(1)} collective-permute-done((bf16[256,256]{1,0:T(8,128)(2,1)S(1)}, bf16[256,256]{1,0:T(8,128)(2,1)S(1)}, u32[]{:S(2)}, u32[]{:S(2)}) %collective-permute-start.15) | collective-permute-done | bytes 131104 | tf_op jit(solution)/shard_map/ppermute | solution.py:524
  57.0 2.3 %collective-permute-done.12.arrived_ref = bf16[65,32,128]{2,1,0:T(8,128)(2,1)S(1)} collective-permute-done((bf16[65,32,128]{2,1,0:T(8,128)(2,1)S(1)}, bf16[65,32,128]{2,1,0:T(8,128)(2,1)S(1)}, u32[]{:S(2)}, u32[]{:S(2)}) %collective-permute-start.12) | collective-permute-done | bytes 532512 | tf_op jit(solution)/shard_map/ppermute | solution.py:515
  59.3 1.2 %finish.1 = (bf16[128,256]{1,0:T(8,128)(2,1)}, bf16[128,256]{1,0:T(8,128)(2,1)}, f32[64,4096]{1,0:T(8,128)}) custom-call(f32[65,32,128]{2,1,0:T(8,128)S(1)} %block_kernel.3.own_ref, bf16[65,32,128]{2,1,0:T(8,128)(2,1)S(1)} %collective-permute-done.12.arrived_ref, bf16[256,256]{1,0:T(8,128)(2,1)S(1)} %get-tuple-element.70.s0, ...), custom_call_target="tpu_custom_call" | custom-call | tf_op jit(solution)/shard_map/finish/pallas_call | solution.py:529
  (20 shorter events, 0.1 us)
Async XLA Ops:
  2.2 3.0 %collective-permute-start.1 = (bf16[256,256]{1,0:T(8,128)(2,1)}, bf16[256,256]{1,0:T(8,128)(2,1)S(1)}, u32[]{:S(2)}, u32[]{:S(2)}) collective-permute-start(bf16[256,256]{1,0:T(8,128)(2,1)} %stack.1.s0), channel_id=1, source_target_pairs={{0,1},{1,0},{2,3},{3,2},{4,5},{5,4},{6,7},{7,6},{8,9},{9,8},{10,11... | collective-permute-start | bytes 393224 | tf_op jit(solution)/shard_map/ppermute | solution.py:402
  2.6 7.7 %collective-permute-start = (bf16[256,256]{1,0:T(8,128)(2,1)}, bf16[256,256]{1,0:T(8,128)(2,1)S(1)}, u32[]{:S(2)}, u32[]{:S(2)}) collective-permute-start(bf16[256,256]{1,0:T(8,128)(2,1)} %stack.1.s0), channel_id=1, source_target_pairs={{0,8},{4,12},{8,0},{12,4},{16,24},{20,28},{24,16},{28,20},{1,9},{5... | collective-permute-start | bytes 393224 | tf_op jit(solution)/shard_map/ppermute | solution.py:401
  5.2 14.9 %collective-permute-start.2 = (bf16[256,256]{1,0:T(8,128)(2,1)}, bf16[256,256]{1,0:T(8,128)(2,1)S(1)}, u32[]{:S(2)}, u32[]{:S(2)}) collective-permute-start(bf16[256,256]{1,0:T(8,128)(2,1)} %stack.1.s0), channel_id=1, source_target_pairs={{0,24},{4,28},{8,16},{12,20},{16,8},{20,12},{24,0},{28,4},{1,25},{... | collective-permute-start | bytes 393224 | tf_op jit(solution)/shard_map/ppermute | solution.py:405
  8.8 11.6 %collective-permute-start.3 = (bf16[256,256]{1,0:T(8,128)(2,1)}, bf16[256,256]{1,0:T(8,128)(2,1)S(1)}, u32[]{:S(2)}, u32[]{:S(2)}) collective-permute-start(bf16[256,256]{1,0:T(8,128)(2,1)} %stack.1.s0), channel_id=1, source_target_pairs={{0,16},{4,20},{8,24},{12,28},{16,0},{20,4},{24,8},{28,12},{1,17},{... | collective-permute-start | bytes 393224 | tf_op jit(solution)/shard_map/ppermute | solution.py:405
  8.8 11.6 %collective-permute-start.5 = (bf16[256,256]{1,0:T(8,128)(2,1)}, bf16[256,256]{1,0:T(8,128)(2,1)S(1)}, u32[]{:S(2)}, u32[]{:S(2)}) collective-permute-start(bf16[256,256]{1,0:T(8,128)(2,1)} %stack.1.s0), channel_id=1, source_target_pairs={{0,2},{1,3},{2,0},{3,1},{4,6},{5,7},{6,4},{7,5},{8,10},{9,11},{10,... | collective-permute-start | bytes 393224 | tf_op jit(solution)/shard_map/ppermute | solution.py:403
  10.3 10.1 %collective-permute-start.6 = (bf16[256,256]{1,0:T(8,128)(2,1)}, bf16[256,256]{1,0:T(8,128)(2,1)S(1)}, u32[]{:S(2)}, u32[]{:S(2)}) collective-permute-start(bf16[256,256]{1,0:T(8,128)(2,1)} %stack.1.s0), channel_id=1, source_target_pairs={{0,3},{1,2},{2,1},{3,0},{4,7},{5,6},{6,5},{7,4},{8,11},{9,10},{10,... | collective-permute-start | bytes 393224 | tf_op jit(solution)/shard_map/ppermute | solution.py:404
  10.3 10.1 %collective-permute-start.4 = (bf16[256,256]{1,0:T(8,128)(2,1)S(1)}, bf16[256,256]{1,0:T(8,128)(2,1)S(1)}, u32[]{:S(2)}, u32[]{:S(2)}) collective-permute-start(bf16[256,256]{1,0:T(8,128)(2,1)S(1)} %collective-permute-done.s0), channel_id=1, source_target_pairs={{0,2},{1,3},{2,0},{3,1},{4,6},{5,7},{6,4},{7,5},{8,10},{9,11},{10,... | collective-permute-start | bytes 393224 | tf_op jit(solution)/shard_map/ppermute | solution.py:413
  13.2 0.7 %copy-start.1 = (s32[8,256]{1,0:T(8,128)S(1)}, s32[8,256]{1,0:T(8,128)}, u32[]{:S(2)}) copy-start(s32[8,256]{1,0:T(8,128)} %plan.1.plan_ref) | copy-start | bytes 24580
  13.9 8.6 %copy-start = (bf16[256,256]{1,0:T(8,128)(2,1)S(1)}, bf16[256,256]{1,0:T(8,128)(2,1)}, u32[]{:S(2)}) copy-start(bf16[256,256]{1,0:T(8,128)(2,1)} %stack.1.s0) | copy-start | bytes 393220
  13.9 8.6 %copy-start.2 = (s32[8,256]{1,0:T(8,128)S(1)}, s32[8,256]{1,0:T(8,128)}, u32[]{:S(2)}) copy-start(s32[8,256]{1,0:T(8,128)} %plan.1.plan_ref) | copy-start | bytes 24580
  13.9 8.6 %copy-start.3 = (f32[1024]{0:T(1024)S(1)}, f32[1024]{0:T(1024)}, u32[]{:S(2)}) copy-start(f32[1024]{0:T(1024)} %param.8) | copy-start | bytes 12292
  20.4 8.7 %collective-permute-start.10 = (bf16[512,256]{1,0:T(8,128)(2,1)S(1)}, bf16[512,256]{1,0:T(8,128)(2,1)S(1)}, u32[]{:S(2)}, u32[]{:S(2)}) collective-permute-start(bf16[512,256]{1,0:T(8,128)(2,1)S(1)} %constant_dynamic-update-slice_fusion.s0), channel_id=1, source_target_pairs={{0,2},{1,3},{2,0},{3,1},{4,6},{5,7},{6,4},{7,5},{8,10},{9,11},{10,... | collective-permute-start | bytes 786440 | tf_op jit(solution)/shard_map/ppermute | solution.py:449
  22.0 11.8 %collective-permute-start.9 = (bf16[512,256]{1,0:T(8,128)(2,1)S(1)}, bf16[512,256]{1,0:T(8,128)(2,1)S(1)}, u32[]{:S(2)}, u32[]{:S(2)}) collective-permute-start(bf16[512,256]{1,0:T(8,128)(2,1)S(1)} %constant_dynamic-update-slice_fusion.s0), channel_id=1, source_target_pairs={{0,1},{1,0},{2,3},{3,2},{4,5},{5,4},{6,7},{7,6},{8,9},{9,8},{10,11... | collective-permute-start | bytes 786440 | tf_op jit(solution)/shard_map/ppermute | solution.py:449
  22.0 7.1 %collective-permute-start.7 = (bf16[256,256]{1,0:T(8,128)(2,1)S(1)}, bf16[256,256]{1,0:T(8,128)(2,1)S(1)}, u32[]{:S(2)}, u32[]{:S(2)}) collective-permute-start(bf16[256,256]{1,0:T(8,128)(2,1)S(1)} %collective-permute-done.s0), channel_id=1, source_target_pairs={{0,1},{1,0},{2,3},{3,2},{4,5},{5,4},{6,7},{7,6},{8,9},{9,8},{10,11... | collective-permute-start | bytes 393224 | tf_op jit(solution)/shard_map/ppermute | solution.py:452
  22.5 6.6 %collective-permute-start.8 = (bf16[256,256]{1,0:T(8,128)(2,1)S(1)}, bf16[256,256]{1,0:T(8,128)(2,1)S(1)}, u32[]{:S(2)}, u32[]{:S(2)}) collective-permute-start(bf16[256,256]{1,0:T(8,128)(2,1)S(1)} %collective-permute-done.4.s2), channel_id=1, source_target_pairs={{0,1},{1,0},{2,3},{3,2},{4,5},{5,4},{6,7},{7,6},{8,9},{9,8},{10,11... | collective-permute-start | bytes 393224 | tf_op jit(solution)/shard_map/ppermute | solution.py:454
  29.2 4.6 %collective-permute-start.11 = (bf16[512,256]{1,0:T(8,128)(2,1)S(1)}, bf16[512,256]{1,0:T(8,128)(2,1)S(1)}, u32[]{:S(2)}, u32[]{:S(2)}) collective-permute-start(bf16[512,256]{1,0:T(8,128)(2,1)S(1)} %collective-permute-done.10.s2), channel_id=1, source_target_pairs={{0,1},{1,0},{2,3},{3,2},{4,5},{5,4},{6,7},{7,6},{8,9},{9,8},{10,11... | collective-permute-start | bytes 786440 | tf_op jit(solution)/shard_map/ppermute | solution.py:494
  44.7 14.6 %collective-permute-start.12 = (bf16[65,32,128]{2,1,0:T(8,128)(2,1)S(1)}, bf16[65,32,128]{2,1,0:T(8,128)(2,1)S(1)}, u32[]{:S(2)}, u32[]{:S(2)}) collective-permute-start(bf16[65,32,128]{2,1,0:T(8,128)(2,1)S(1)} %block_kernel.2), channel_id=1, source_target_pairs={{0,4},{4,0},{8,12},{12,8},{16,20},{20,16},{24,28},{28,24},{1,5},{5... | collective-permute-start | bytes 1597448 | tf_op jit(solution)/shard_map/ppermute | solution.py:515
  48.6 5.0 %collective-permute-start.13 = (bf16[256,256]{1,0:T(8,128)(2,1)S(1)}, bf16[256,256]{1,0:T(8,128)(2,1)S(1)}, u32[]{:S(2)}, u32[]{:S(2)}) collective-permute-start(bf16[256,256]{1,0:T(8,128)(2,1)S(1)} %get-tuple-element.71), channel_id=1, source_target_pairs={{0,1},{1,0},{2,3},{3,2},{4,5},{5,4},{6,7},{7,6},{8,9},{9,8},{10,11... | collective-permute-start | bytes 393224 | tf_op jit(solution)/shard_map/ppermute | solution.py:524
  48.9 6.3 %collective-permute-start.14 = (bf16[256,256]{1,0:T(8,128)(2,1)S(1)}, bf16[256,256]{1,0:T(8,128)(2,1)S(1)}, u32[]{:S(2)}, u32[]{:S(2)}) collective-permute-start(bf16[256,256]{1,0:T(8,128)(2,1)S(1)} %get-tuple-element.72), channel_id=1, source_target_pairs={{0,2},{1,3},{2,0},{3,1},{4,6},{5,7},{6,4},{7,5},{8,10},{9,11},{10,... | collective-permute-start | bytes 393224 | tf_op jit(solution)/shard_map/ppermute | solution.py:524
  51.0 6.0 %collective-permute-start.15 = (bf16[256,256]{1,0:T(8,128)(2,1)S(1)}, bf16[256,256]{1,0:T(8,128)(2,1)S(1)}, u32[]{:S(2)}, u32[]{:S(2)}) collective-permute-start(bf16[256,256]{1,0:T(8,128)(2,1)S(1)} %get-tuple-element.73), channel_id=1, source_target_pairs={{0,3},{1,2},{2,1},{3,0},{4,7},{5,6},{6,5},{7,4},{8,11},{9,10},{10,... | collective-permute-start | bytes 393224 | tf_op jit(solution)/shard_map/ppermute | solution.py:524
